TPU v7x, 32 devices: a whole 2x2x4 slice. The times are simulated.
32 devices in a mesh: groups: 2 (over y), seq: 16 (over z, x, core).
Axes of the slice: x: 2, y: 2, z: 4, core: 2. Of those that a mesh axis runs over, the one named last changes fastest.
Arguments:
- queries: bfloat16 [8192, 768], P(('groups', 'seq')), parts along dimension 0, may hold values from -6 to 6
- keys: bfloat16 [8192, 768], P(('groups', 'seq')), parts along dimension 0, may hold values from -6 to 6
- values: bfloat16 [8192, 768], P(('groups', 'seq')), parts along dimension 0, may hold values from -6 to 6
- out_grad: bfloat16 [8192, 768], P(('groups', 'seq')), parts along dimension 0, may hold values from -6 to 6
- slide_lengths: int32 [16], P('groups'), parts along dimension 0, may hold values from 1 to 2560, 4096 in all
- head_offsets: int32 [3, 16], replicated, may hold values from 0 to 3
Outputs:
- attended: bfloat16 [8192, 768], P(('groups', 'seq')), parts along dimension 0
- query_grad: bfloat16 [8192, 768], P(('groups', 'seq')), parts along dimension 0
- key_grad: bfloat16 [8192, 768], P(('groups', 'seq')), parts along dimension 0
- value_grad: bfloat16 [8192, 768], P(('groups', 'seq')), parts along dimension 0
There are 2 independent parts, one for each index of `groups`. A program takes and returns all parts, laid end to end along the dimension named above; an argument that names none is the same for every part. Nothing has to cross between parts.
Inputs may be any that keep to these rules, and one draw needn't show every extreme that they name: `slide_lengths`: the slides lie end to end over the 4096 tokens of a part, in order.
All inputs are finite; a program needn't handle non-finite values.
Results may differ from a plain program's by a relative error of at most 0.03.
Values may be sent and summed in bfloat16 or wider, within the bound.
No kernel may reach another device: no remote copies, remote signals or barrier semaphores. Data moves between devices by JAX's collectives and lax.ppermute only.
A program may use at most 128 MiB of HBM per device.

v0:
```python
from functools import partial
import math

import jax
import jax.numpy as jnp
from jax import lax
from jax.experimental import pallas as pl
from jax.experimental.pallas import tpu as pltpu
from jax.sharding import PartitionSpec as P

SEG0 = 1024
BIG = 2.0**100
LOG2E = math.log2(math.e)
BF16 = jnp.bfloat16
F32 = jnp.float32
VMEM_LIMIT = 44 << 20


class Plan:
    def __init__(self, tok_rows, model_width, level_count, head_count, slide_count, device_count):
        self.tok = tok_rows
        self.levels = level_count
        self.heads = head_count
        self.hd = model_width // head_count
        self.slides = slide_count
        self.devices = device_count
        self.stride = device_count * tok_rows // SEG0
        self.bits = self.stride.bit_length() - 1
        self.near = min((SEG0 << (level_count - 2)) // tok_rows, device_count)
        self.far = device_count // self.near
        self.chunks = head_count // self.near
        self.segs = self.near * tok_rows // SEG0
        self.seg_dev = SEG0 // tok_rows
        self.cdev = tok_rows // self.stride
        self.cseg = SEG0 // self.stride
        self.rows = self.near * tok_rows
        self.last_rows = self.segs * self.cseg
        self.tiles = []
        for level in range(level_count - 1):
            for first in range(0, self.segs, 1 << level):
                self.tiles.append((level, first))
        self.all_rows = len(self.tiles) * SEG0
        self.half = tok_rows // 2
        self.slide_pad = -(-slide_count // 8) * 8
        assert 2 * self.hd + 8 + self.slide_pad <= 128 and 4 * self.hd <= 256


def reversed_bits(value, bits):
    out = value * 0
    for b in range(bits):
        out = out + ((value >> b) & 1) * (1 << (bits - 1 - b))
    return out


def dot(a, b):
    return lax.dot_general(a, b, (((1,), (0,)), ((), ())), preferred_element_type=F32)


def iota(shape, axis):
    return lax.broadcasted_iota(jnp.int32, shape, axis)


def kernel_call(body, out_shape, in_specs, scratch=(), flops=0, name=None):
    return pl.pallas_call(
        body,
        out_shape=out_shape,
        in_specs=in_specs,
        scratch_shapes=list(scratch),
        name=name,
        compiler_params=pltpu.CompilerParams(vmem_limit_bytes=VMEM_LIMIT),
        cost_estimate=pl.CostEstimate(flops=flops, bytes_accessed=1 << 20, transcendentals=0),
    )


VMEM = pl.BlockSpec(memory_space=pltpu.VMEM)
SMEM = pl.BlockSpec(memory_space=pltpu.SMEM)


def class_of_token(plan, shape, axis_row, axis_tok):
    row, tok = iota(shape, axis_row), iota(shape, axis_tok)
    want = (row % plan.cdev) * plan.stride + reversed_bits(row // plan.cdev, plan.bits)
    return jnp.where(want == tok, 1.0, 0.0).astype(BF16)


def pack_body(plan, q_ref, k_ref, v_ref, g_ref, off_ref, *outs):
    main_refs, last_ref = outs[:-1], outs[-1]
    order = class_of_token(plan, (plan.tok, plan.tok), 0, 1)
    sorted_rows = [dot(order, ref[...]) for ref in (q_ref, k_ref, v_ref, g_ref)]
    hd, half = plan.hd, plan.half
    for chunk in range(plan.chunks):
        for dest in range(plan.near):
            col = (chunk * plan.near + dest) * hd
            parts = [
                x[h * half : (h + 1) * half, col : col + hd] for h in range(2) for x in sorted_rows
            ]
            main_refs[chunk][dest] = jnp.concatenate(parts, axis=1).astype(BF16)
    last_rows(plan, sorted_rows[1], sorted_rows[2], off_ref, last_ref)


def last_rows(plan, k, v, off_ref, last_ref):
    hd, cdev = plan.hd, plan.cdev
    classes = range(plan.stride)
    pad = jnp.zeros((cdev, 128 - 2 * hd), F32)
    for dest in range(plan.near):
        blocks = []
        for chunk in range(plan.chunks):
            head = chunk * plan.near + dest
            col = head * hd
            place = reversed_bits(off_ref[plan.levels - 1, head] % plan.stride, plan.bits)
            both = jnp.concatenate([k[:, col : col + hd], v[:, col : col + hd]], axis=1)
            got = jnp.zeros((cdev, 2 * hd), F32)
            for c in classes:
                got = jnp.where(place == c, both[c * cdev : (c + 1) * cdev], got)
            blocks.append(jnp.concatenate([got, pad], axis=1))
        rows = jnp.concatenate(blocks, axis=0).astype(BF16)
        for group in range(plan.far):
            last_ref[group * plan.near + dest] = rows


def slide_rows(plan, pos, len_ref):
    slide = jnp.zeros(pos.shape, jnp.int32)
    end = 0
    for i in range(plan.slides):
        end = end + len_ref[i]
        slide = slide + jnp.where(pos >= end, 1, 0)
    shape = (plan.slide_pad, pos.shape[1])
    return jnp.where(iota(shape, 0) == slide, 1.0, 0.0)


def key_features(plan, k, one_hot):
    n = k.shape[1]
    rest = 128 - 2 * plan.hd - 8 - plan.slide_pad
    return jnp.concatenate([k, k, jnp.ones((8, n), F32), one_hot, jnp.zeros((rest, n), F32)], axis=0)


def query_features(plan, q, one_hot):
    n = q.shape[1]
    rest = 128 - 2 * plan.hd - 8 - plan.slide_pad
    q = q * (plan.hd**-0.5 * LOG2E)
    high = q.astype(BF16).astype(F32)
    return jnp.concatenate(
        [high, q - high, jnp.zeros((8, n), F32), (one_hot - 1.0) * BIG, jnp.zeros((rest, n), F32)],
        axis=0,
    )


def value_features(plan, v):
    n = v.shape[1]
    return jnp.concatenate([v, jnp.ones((8, n), F32), jnp.zeros((64 - plan.hd - 8, n), F32)], axis=0)


def forward_tile(plan, keys, queries_t, values_t):
    s = dot(keys, queries_t)
    peak = jnp.max(s, axis=0, keepdims=True)
    p = jnp.exp2(s - peak).astype(BF16)
    o = dot(values_t, p)
    n = o.shape[1]
    hd = plan.hd
    full = jnp.concatenate(
        [o[: hd + 8], jnp.broadcast_to(peak, (8, n)), jnp.zeros((128 - hd - 16, n), F32)], axis=0
    )
    return full.T


def merged(plan, a, b):
    at = plan.hd + 8
    peak_a, peak_b = a[:, at : at + 1], b[:, at : at + 1]
    peak = jnp.maximum(peak_a, peak_b)
    both = a * jnp.exp2(peak_a - peak) + b * jnp.exp2(peak_b - peak)
    return jnp.where(iota(a.shape, 1) >= at, peak, both)


def level_start(plan, off_ref, level, chunk):
    head = chunk * plan.near + lax.rem(lax.axis_index("seq"), plan.near)
    bits = level if level < plan.levels - 1 else plan.bits
    rows = SEG0 >> bits
    return reversed_bits(off_ref[level, head] % (1 << bits), bits) * rows, rows


def tile_pieces(plan, off_ref, chunk, tile):
    level, first = plan.tiles[tile]
    start, rows = level_start(plan, off_ref, level, chunk)
    return [
        (pl.multiple_of((first + i) * SEG0 + start, 128), i * rows, rows) for i in range(1 << level)
    ]


def forward_body(plan, chunk, x_ref, len_ref, off_ref, ka, kat, qa0, ga0, vat, gt, qt, acc_ref, xs, qat, res):
    hd, half = plan.hd, plan.half
    base = lax.axis_index("seq") // plan.near * plan.rows
    for src in range(plan.near):
        seg, at = src // plan.seg_dev, src % plan.seg_dev
        block = x_ref[src].astype(F32)
        for c in range(plan.stride):
            side = c * plan.cdev // half
            row = c * plan.cdev - side * half
            dst = seg * SEG0 + c * plan.cseg + at * plan.cdev
            xs[dst : dst + plan.cdev, 0 : 4 * hd] = block[
                row : row + plan.cdev, side * 4 * hd : (side + 1) * 4 * hd
            ]
    for seg in range(plan.segs):
        rows = slice(seg * SEG0, (seg + 1) * SEG0)
        xt = xs[rows, :].T
        q, k, v, g = (xt[i * hd : (i + 1) * hd] for i in range(4))
        n = iota((1, SEG0), 1)
        pos = base + seg * SEG0 + (n % plan.cseg) * plan.stride + reversed_bits(n // plan.cseg, plan.bits)
        one_hot = slide_rows(plan, pos, len_ref)
        key_f = key_features(plan, k, one_hot)
        query_f = query_features(plan, q, one_hot)
        kat[:, rows] = key_f.astype(BF16)
        ka[rows, :] = key_f.T.astype(BF16)
        qat[:, rows] = query_f.astype(BF16)
        qa0[rows, :] = query_f.T.astype(BF16)
        vat[:, rows] = value_features(plan, v).astype(BF16)
        gt[:, rows] = g.astype(BF16)
        qt[:, rows] = q.astype(BF16)
        ga0[rows, :] = jnp.concatenate([g, jnp.zeros((128 - hd, SEG0), F32)], axis=0).T.astype(BF16)
    for tile in range(plan.segs, len(plan.tiles)):
        for src, at, count in tile_pieces(plan, off_ref, chunk, tile):
            dst = slice(tile * SEG0 + at, tile * SEG0 + at + count)
            src = pl.ds(src, count)
            ka[dst, :] = ka[src, :]
            for ref in (kat, qat, vat, gt, qt):
                ref[:, dst] = ref[:, src]

    def step(tile, carry):
        rows = pl.ds(pl.multiple_of(tile * SEG0, SEG0), SEG0)
        res[rows, :] = forward_tile(plan, ka[rows, :], qat[:, rows], vat[:, rows])
        return carry

    lax.fori_loop(0, len(plan.tiles), step, 0)
    acc_ref[...] = res[0 : plan.rows, :]
    for tile in range(plan.segs, len(plan.tiles)):
        for src, at, count in tile_pieces(plan, off_ref, chunk, tile):
            rows = pl.ds(src, count)
            acc_ref[rows, :] = merged(
                plan, acc_ref[rows, :], res[tile * SEG0 + at : tile * SEG0 + at + count, :]
            )


def split3(x):
    a = x.astype(BF16).astype(F32)
    b = (x - a).astype(BF16).astype(F32)
    return a, b, x - a - b


def put_lanes(base, first, values):
    lane = iota(base.shape, 1)
    for i, v in enumerate(values):
        base = jnp.where(lane == first + i, v, base)
    return base


def backward_tile(plan, qa, kat, ga, vat, gt, qt, ka):
    p = jnp.exp2(dot(qa, kat))
    value_t = dot(gt, p.astype(BF16))
    ds = (p * dot(ga, vat)).astype(BF16)
    key_t = dot(qt, ds)
    n = key_t.shape[1]
    both = jnp.concatenate([key_t, value_t, jnp.zeros((128 - 2 * plan.hd, n), F32)], axis=0)
    return dot(ds, ka), both.T


def last_body(
    plan, chunk, l_ref, len_ref, off_ref, qa0, ga0, acc_ref,
    qa, ga, att_ref, dq_ref, near_ref, far_ref, acc, pair,
):
    hd, cdev = plan.hd, plan.cdev
    group = lax.axis_index("seq") // plan.near
    start, count = level_start(plan, off_ref, plan.levels - 1, chunk)
    rows_of = [
        pl.ds(pl.multiple_of(seg * SEG0 + start, plan.cseg), count) for seg in range(plan.segs)
    ]
    acc[...] = acc_ref[...]
    low = chunk * cdev
    x = jnp.concatenate([l_ref[d].astype(F32)[low : low + cdev] for d in range(plan.devices)], axis=0)
    xt = x.T
    head = chunk * plan.near + lax.rem(lax.axis_index("seq"), plan.near)
    n = iota((1, SEG0), 1)
    pos = n * plan.stride + off_ref[plan.levels - 1, head] % plan.stride
    kat2 = key_features(plan, xt[0:hd], slide_rows(plan, pos, len_ref))
    ka2 = kat2.T.astype(BF16)
    kat2 = kat2.astype(BF16)
    vat2 = value_features(plan, xt[hd : 2 * hd]).astype(BF16)
    q2t = jnp.concatenate([qa0[rows, :] for rows in rows_of], axis=0).astype(F32).T
    res = forward_tile(plan, ka2, q2t.astype(BF16), vat2)
    for seg, rows in enumerate(rows_of):
        acc[rows, :] = merged(plan, acc[rows, :], res[seg * count : (seg + 1) * count])
    for seg in range(plan.segs):
        rows = slice(seg * SEG0, (seg + 1) * SEG0)
        a = acc[rows, :]
        total = a[:, hd : hd + 1]
        att = jnp.where(iota(a.shape, 1) < hd, a / total, 0.0).astype(BF16)
        att_ref[rows, :] = att
        log_total = a[:, hd + 8 : hd + 9] + jnp.log2(total)
        g = ga0[rows, :].astype(F32)
        grad_dot = jnp.sum(g * att.astype(F32), axis=1, keepdims=True)
        query_f = put_lanes(qa0[rows, :].astype(F32), 2 * hd, split3(-log_total))
        qa[rows, :] = query_f.astype(BF16)
        ga[rows, :] = put_lanes(g, hd, split3(-grad_dot)).astype(BF16)
    for tile in range(plan.segs, len(plan.tiles)):
        for src, at, count1 in tile_pieces(plan, off_ref, chunk, tile):
            dst = slice(tile * SEG0 + at, tile * SEG0 + at + count1)
            qa[dst, :] = qa[pl.ds(src, count1), :]
            ga[dst, :] = ga[pl.ds(src, count1), :]
    qa2 = jnp.concatenate([qa[rows, :] for rows in rows_of], axis=0)
    ga2 = jnp.concatenate([ga[rows, :] for rows in rows_of], axis=0)
    g2t = ga2.astype(F32).T[0:hd].astype(BF16)
    q2 = (q2t[0:hd] + q2t[hd : 2 * hd]) * (1.0 / (plan.hd**-0.5 * LOG2E))
    dq, both = backward_tile(plan, qa2, kat2, ga2[:, 0:64], vat2, g2t, q2.astype(BF16), ka2)
    dq_ref[...] = dq
    pair[...] = both
    n2 = plan.last_rows
    near_ref[...] = pair[pl.ds(pl.multiple_of(group * n2, n2), n2), :]
    for s in range(1, plan.far):
        to = lax.rem(group + s, plan.far)
        far_ref[s - 1] = pair[pl.ds(pl.multiple_of(to * n2, n2), n2), :].astype(BF16)


def backward_body(
    plan, chunk, off_ref, qa, kat, ga, vat, gt, qt, ka, att_ref, dq2, near2, *rest,
):
    far_refs, (out_ref, dq, pair) = rest[: plan.far - 1], rest[plan.far - 1 :]
    hd = plan.hd

    def step(tile, carry):
        rows = pl.ds(pl.multiple_of(tile * SEG0, SEG0), SEG0)
        dq[rows, :], pair[rows, :] = backward_tile(
            plan, qa[rows, :], kat[:, rows], ga[rows, 0:64], vat[:, rows], gt[:, rows], qt[:, rows], ka[rows, :]
        )
        return carry

    lax.fori_loop(0, len(plan.tiles), step, 0)
    for tile in range(plan.segs, len(plan.tiles)):
        for src, at, count in tile_pieces(plan, off_ref, chunk, tile):
            rows = pl.ds(src, count)
            part = slice(tile * SEG0 + at, tile * SEG0 + at + count)
            dq[rows, :] = dq[rows, :] + dq[part, :]
            pair[rows, :] = pair[rows, :] + pair[part, :]
    start, count = level_start(plan, off_ref, plan.levels - 1, chunk)
    for seg in range(plan.segs):
        rows = pl.ds(pl.multiple_of(seg * SEG0 + start, plan.cseg), count)
        part = slice(seg * count, (seg + 1) * count)
        dq[rows, :] = dq[rows, :] + dq2[part, :]
        more = near2[part, :]
        for ref in far_refs:
            more = more + ref[part, :].astype(F32)
        pair[rows, :] = pair[rows, :] + more
    scale = hd**-0.5
    for src in range(plan.near):
        seg, at = src // plan.seg_dev, src % plan.seg_dev
        blocks = []
        for c in range(plan.stride):
            first = seg * SEG0 + c * plan.cseg + at * plan.cdev
            rows = slice(first, first + plan.cdev)
            blocks.append((att_ref[rows, :].astype(F32), dq[rows, :] * scale, pair[rows, :]))
        att, dqs, pairs = (jnp.concatenate(list(x), axis=0) for x in zip(*blocks))
        half = plan.half
        parts = []
        for h in range(2):
            r = slice(h * half, (h + 1) * half)
            parts += [att[r, 0:hd], dqs[r, 0:hd], pairs[r, 0:hd] * scale, pairs[r, hd : 2 * hd]]
        out_ref[src] = jnp.concatenate(parts, axis=1).astype(BF16)


def unpack_body(plan, *refs):
    ins, outs = refs[: plan.chunks], refs[plan.chunks :]
    hd = plan.hd
    order = class_of_token(plan, (plan.tok, plan.tok), 1, 0)
    for chunk in range(plan.chunks):
        got = [ins[chunk][d].astype(F32) for d in range(plan.near)]
        for i in range(4):
            halves = []
            for h in range(2):
                col = (4 * h + i) * hd
                halves.append(jnp.concatenate([x[:, col : col + hd] for x in got], axis=1))
            block = jnp.concatenate(halves, axis=0).astype(BF16)
            width = plan.near * hd
            outs[i][:, chunk * width : (chunk + 1) * width] = dot(order, block).astype(BF16)


def body(queries, keys, values, out_grad, slide_lengths, head_offsets):
    tok_rows, model_width = queries.shape
    level_count, head_count = head_offsets.shape
    device_count = lax.axis_size("seq")
    plan = Plan(tok_rows, model_width, level_count, head_count, slide_lengths.shape[0], device_count)
    near_groups = [
        list(range(i, i + plan.near)) for i in range(0, device_count, plan.near)
    ]
    sds = jax.ShapeDtypeStruct
    chunk_shape = sds((plan.near, plan.half, 8 * plan.hd), BF16)
    packed = kernel_call(
        partial(pack_body, plan),
        [chunk_shape] * plan.chunks + [sds((device_count, plan.chunks * plan.cdev, 128), BF16)],
        [VMEM] * 4 + [SMEM],
        name="pack",
    )(queries, keys, values, out_grad, head_offsets)
    swap = partial(lax.all_to_all, axis_name="seq", split_axis=0, concat_axis=0, tiled=True)
    blocks = [swap(packed[0], axis_index_groups=near_groups)]
    last = swap(packed[-1])
    blocks += [swap(x, axis_index_groups=near_groups) for x in packed[1:-1]]

    n, n3, n2 = plan.rows, plan.all_rows, plan.last_rows
    pair_flops = 2 * 128 * SEG0 * SEG0
    states = []
    for chunk in range(plan.chunks):
        ka, kat, qa0, ga0, vat, gt, qt, acc = kernel_call(
            partial(forward_body, plan, chunk),
            [
                sds((n3, 128), BF16),
                sds((128, n3), BF16),
                sds((n, 128), BF16),
                sds((n, 128), BF16),
                sds((64, n3), BF16),
                sds((plan.hd, n3), BF16),
                sds((plan.hd, n3), BF16),
                sds((n, 128), F32),
            ],
            [VMEM, SMEM, SMEM],
            [pltpu.VMEM((n, 256), F32), pltpu.VMEM((128, n3), BF16), pltpu.VMEM((n3, 128), F32)],
            flops=len(plan.tiles) * 2 * pair_flops,
            name=f"forward{chunk}",
        )(blocks[chunk], slide_lengths, head_offsets)
        qa, ga, att, dq2, near2, far2 = kernel_call(
            partial(last_body, plan, chunk),
            [
                sds((n3, 128), BF16),
                sds((n3, 128), BF16),
                sds((n, 128), BF16),
                sds((n2, 128), F32),
                sds((n2, 128), F32),
                sds((max(plan.far - 1, 1), n2, 128), BF16),
            ],
            [VMEM, SMEM, SMEM, VMEM, VMEM, VMEM],
            [pltpu.VMEM((n, 128), F32), pltpu.VMEM((SEG0, 128), F32)],
            flops=4 * pair_flops,
            name=f"last{chunk}",
        )(last, slide_lengths, head_offsets, qa0, ga0, acc)
        back = []
        for s in range(1, plan.far):
            pairs = [(i, (i + s * plan.near) % device_count) for i in range(device_count)]
            back.append(lax.ppermute(far2[s - 1], "seq", pairs))
        states.append((qa, kat, ga, vat, gt, qt, ka, att, dq2, near2, *back))
    results = []
    for chunk in range(plan.chunks):
        out = kernel_call(
            partial(backward_body, plan, chunk),
            chunk_shape,
            [SMEM] + [VMEM] * len(states[chunk]),
            [pltpu.VMEM((n3, 128), F32), pltpu.VMEM((n3, 128), F32)],
            flops=len(plan.tiles) * 5 * pair_flops,
            name=f"backward{chunk}",
        )(head_offsets, *states[chunk])
        results.append(swap(out, axis_index_groups=near_groups))
    return kernel_call(
        partial(unpack_body, plan),
        [sds((tok_rows, model_width), BF16)] * 4,
        [VMEM] * plan.chunks,
        name="unpack",
    )(*results)


def solution(mesh):
    rows = P(("groups", "seq"), None)
    return jax.shard_map(
        body,
        mesh=mesh,
        in_specs=(rows, rows, rows, rows, P("groups"), P()),
        out_specs=(rows, rows, rows, rows),
        check_vma=False,
    )
```

profile of v0, /device:TPU:0, one launch (start us, length us, event | category | flops | bytes accessed | tf_op | source)
XLA Modules:
  0.0 135.9 jit_solution(13585559650612319200)
XLA Ops:
  0.6 0.0 copy-start
  0.6 1.0 copy-done
  1.6 0.0 copy-start.1
  1.6 1.0 copy-done.1
  2.6 0.0 copy-start.2
  2.6 1.0 copy-done.2
  3.6 0.0 copy-start.3
  3.6 1.0 copy-done.3
  4.6 0.0 copy-start.4
  4.6 0.7 copy-done.4
  5.3 3.4 %pack.1 = (bf16[8,128,384]{2,1,0:T(8,128)(2,1)}, bf16[8,128,384]{2,1,0:T(8,128)(2,1)S(1)}, bf16[16,128,128]{2,1,0:T(8,128)(2,1)S(1)}) custom-call(bf16[256,768]{1,0:T(8,128)(2,1)S(1)} %copy-done, bf16[256,768]{1,0:T(8,128)(2,1)S(1)} %copy-done.1, bf16[256,768]{1,0:T(8,128)(2,1)S(1)} %copy-done.2, bf16[256,768]{1,0:T(8,128)(2,1)S(1)} %copy-done.3, ...), custom_call_target="tpu_custom_call" | custom-call | bytes 1048576 | tf_op jit(solution)/shard_map/pack/pallas_call | solution.py:392
  8.7 21.6 %all_to_all.25.l_ref = bf16[16,128,128]{2,1,0:T(8,128)(2,1)S(1)} all-to-all(bf16[16,128,128]{2,1,0:T(8,128)(2,1)S(1)} %get-tuple-element.35), channel_id=1, replica_groups=mesh['groups'=2,'seq'=16] {'seq'}, dimensions={0} | all-to-all | bytes 1048576 | tf_op jit(solution)/shard_map/all_to_all | solution.py:400
  30.3 14.6 %all_to_all.26.x_ref = bf16[8,128,384]{2,1,0:T(8,128)(2,1)S(1)} all-to-all(bf16[8,128,384]{2,1,0:T(8,128)(2,1)S(1)} %get-tuple-element.51), channel_id=1, replica_groups={{0,1,2,3,4,5,6,7},{8,9,10,11,12,13,14,15},{16,17,18,19,20,21,22,23},{24..., dimensions={0} | all-to-all | bytes 1572864 | tf_op jit(solution)/shard_map/all_to_all | solution.py:401
  44.9 0.0 copy-start.5
  44.9 0.0 copy-start.6
  44.9 3.9 %all-to-all-start.1 = ((bf16[8,128,384]{2,1,0:T(8,128)(2,1)}), bf16[8,128,384]{2,1,0:T(8,128)(2,1)S(1)}, u32[]{:S(2)}, u32[]{:S(2)}) async-start(bf16[8,128,384]{2,1,0:T(8,128)(2,1)} %get-tuple-element.36), calls=%async_computation.1 | async-start | bytes 1572864 | tf_op jit(solution)/shard_map/all_to_all | solution.py:399
  48.8 0.0 copy-done.5
  48.8 0.0 copy-done.6
  48.8 7.1 %forward1.1 = (bf16[3072,128]{1,0:T(8,128)(2,1)S(1)}, bf16[128,3072]{1,0:T(8,128)(2,1)S(1)}, bf16[2048,128]{1,0:T(8,128)(2,1)S(1)}, bf16[2048,128]{1,0:T(8,128)(...) custom-call(bf16[8,128,384]{2,1,0:T(8,128)(2,1)S(1)} %all_to_all.26., ...), custom_call_target="tpu_custom_call" | custom-call | flops 1610612736 | bytes 1048576 | tf_op jit(solution)/shard_map/forward1/pallas_call | solution.py:407
  55.9 5.4 %last1.1 = (bf16[3072,128]{1,0:T(8,128)(2,1)S(1)}, bf16[3072,128]{1,0:T(8,128)(2,1)S(1)}, bf16[2048,128]{1,0:T(8,128)(2,1)S(1)}, f32[512,128]{1,0:T(8,128)S(1)},...) custom-call(bf16[16,128,128]{2,1,0:T(8,128)(2,1)S(1)} %all_to_all.25.l_ref, s32[8]{0:T(128)S(1)} %copy-done.6, ...), custom_call_target="tpu_custom_call" | custom-call | flops 1073741824 | bytes 1048576 | tf_op jit(solution)/shard_map/last1/pallas_call | solution.py:424
  61.3 1.9 %collective-permute-start.1 = (bf16[512,128]{1,0:T(8,128)(2,1)S(1)}, bf16[512,128]{1,0:T(8,128)(2,1)S(1)}, u32[]{:S(2)}, u32[]{:S(2)}) collective-permute-start(bf16[512,128]{1,0:T(8,128)(2,1)S(1)} %bitcast.3), channel_id=1, source_target_pairs={{0,8},{1,9},{2,10},{3,11},{4,12},{5,13},{6,14},{7,15},{8,0},{9,1},... | collective-permute-start | bytes 393224 | tf_op jit(solution)/shard_map/ppermute | solution.py:442
  63.2 7.5 %collective-permute-done.1.rest_0_ = bf16[512,128]{1,0:T(8,128)(2,1)S(1)} collective-permute-done((bf16[512,128]{1,0:T(8,128)(2,1)S(1)}, bf16[512,128]{1,0:T(8,128)(2,1)S(1)}, u32[]{:S(2)}, u32[]{:S(2)}) %collective-permute-start.1) | collective-permute-done | bytes 131104 | tf_op jit(solution)/shard_map/ppermute | solution.py:442
  70.7 11.6 %backward1.1 = bf16[8,128,384]{2,1,0:T(8,128)(2,1)} custom-call(s32[3,16]{1,0:T(4,128)S(1)} %copy-done.5, bf16[3072,128]{1,0:T(8,128)(2,1)S(1)} %get-tuple-element.55.qa, bf16[128,3072]{1,0:T(8,128)(2,1)S(1)} %get-tuple-element.56.kat, bf16[3072,128]{1,0:T(8,128)(2,1)S(1)} %get-tuple-element.57.ga, bf16[64,3072]{1,0:T(8,128)(2,1)S(1)} %get-tuple-element.58.vat, ...), custom_call_target="tpu_custom_call" | custom-call | flops 4026531840 | bytes 1048576 | tf_op jit(solution)/shard_map/backward1/pallas_call | solution.py:446
  82.4 0.0 all-to-all-done.1.x_ref
  82.4 3.8 %all-to-all-start.4 = ((bf16[8,128,384]{2,1,0:T(8,128)(2,1)}), bf16[8,128,384]{2,1,0:T(8,128)(2,1)S(1)}, u32[]{:S(2)}, u32[]{:S(2)}) async-start(bf16[8,128,384]{2,1,0:T(8,128)(2,1)} %backward1.1), calls=%async_computation.4 | async-start | bytes 1572864 | tf_op jit(solution)/shard_map/all_to_all | solution.py:454
  86.1 7.0 %forward0.1 = (bf16[3072,128]{1,0:T(8,128)(2,1)S(1)}, bf16[128,3072]{1,0:T(8,128)(2,1)S(1)}, bf16[2048,128]{1,0:T(8,128)(2,1)S(1)}, bf16[2048,128]{1,0:T(8,128)(...) custom-call(bf16[8,128,384]{2,1,0:T(8,128)(2,1)S(1)} %all-to-all-don, ...), custom_call_target="tpu_custom_call" | custom-call | flops 1610612736 | bytes 1048576 | tf_op jit(solution)/shard_map/forward0/pallas_call | solution.py:407
  93.2 5.4 %last0.1 = (bf16[3072,128]{1,0:T(8,128)(2,1)S(1)}, bf16[3072,128]{1,0:T(8,128)(2,1)S(1)}, bf16[2048,128]{1,0:T(8,128)(2,1)S(1)}, f32[512,128]{1,0:T(8,128)S(1)},...) custom-call(bf16[16,128,128]{2,1,0:T(8,128)(2,1)S(1)} %all_to_all.25.l_ref, s32[8]{0:T(128)S(1)} %copy-done.6, ...), custom_call_target="tpu_custom_call" | custom-call | flops 1073741824 | bytes 1048576 | tf_op jit(solution)/shard_map/last0/pallas_call | solution.py:424
  98.6 1.9 %collective-permute-start = (bf16[512,128]{1,0:T(8,128)(2,1)S(1)}, bf16[512,128]{1,0:T(8,128)(2,1)S(1)}, u32[]{:S(2)}, u32[]{:S(2)}) collective-permute-start(bf16[512,128]{1,0:T(8,128)(2,1)S(1)} %bitcast.2), channel_id=1, source_target_pairs={{0,8},{1,9},{2,10},{3,11},{4,12},{5,13},{6,14},{7,15},{8,0},{9,1},... | collective-permute-start | bytes 393224 | tf_op jit(solution)/shard_map/ppermute | solution.py:442
  100.5 7.6 %collective-permute-done.rest_0_ = bf16[512,128]{1,0:T(8,128)(2,1)S(1)} collective-permute-done((bf16[512,128]{1,0:T(8,128)(2,1)S(1)}, bf16[512,128]{1,0:T(8,128)(2,1)S(1)}, u32[]{:S(2)}, u32[]{:S(2)}) %collective-permute-start) | collective-permute-done | bytes 131104 | tf_op jit(solution)/shard_map/ppermute | solution.py:442
  108.0 10.8 %backward0.1 = bf16[8,128,384]{2,1,0:T(8,128)(2,1)S(1)} custom-call(s32[3,16]{1,0:T(4,128)S(1)} %copy-done.5, bf16[3072,128]{1,0:T(8,128)(2,1)S(1)} %get-tuple-element.40.qa, bf16[128,3072]{1,0:T(8,128)(2,1)S(1)} %get-tuple-element.41.kat, bf16[3072,128]{1,0:T(8,128)(2,1)S(1)} %get-tuple-element.42.ga, bf16[64,3072]{1,0:T(8,128)(2,1)S(1)} %get-tuple-element.43.vat, ...), custom_call_target="tpu_custom_call" | custom-call | flops 4026531840 | bytes 1048576 | tf_op jit(solution)/shard_map/backward0/pallas_call | solution.py:446
  118.8 0.0 all-to-all-done.4.refs_1_
  118.8 14.5 %all_to_all.27.refs_0_ = bf16[8,128,384]{2,1,0:T(8,128)(2,1)S(1)} all-to-all(bf16[8,128,384]{2,1,0:T(8,128)(2,1)S(1)} %backward0.1), channel_id=1, replica_groups={{0,1,2,3,4,5,6,7},{8,9,10,11,12,13,14,15},{16,17,18,19,20,21,22,23},{24..., dimensions={0} | all-to-all | bytes 1572864 | tf_op jit(solution)/shard_map/all_to_all | solution.py:454
  133.3 2.6 %unpack.1 = (bf16[256,768]{1,0:T(8,128)(2,1)}, bf16[256,768]{1,0:T(8,128)(2,1)}, bf16[256,768]{1,0:T(8,128)(2,1)}, bf16[256,768]{1,0:T(8,128)(2,1)}) custom-call(bf16[8,128,384]{2,1,0:T(8,128)(2,1)S(1)} %all_to_all.27.refs_0_, bf16[8,128,384]{2,1,0:T(8,128)(2,1)S(1)} %all-to-all-done.4.refs_1_), custom_call_target="tpu_custom_call" | custom-call | bytes 1048576 | tf_op jit(solution)/shard_map/unpack/pallas_call | solution.py:455
Async XLA Ops:
  0.6 1.0 copy-start
  1.6 1.0 copy-start.1
  2.6 1.0 copy-start.2
  3.6 1.0 copy-start.3
  4.6 0.7 copy-start.4
  44.9 3.9 %copy-start.5 = (s32[3,16]{1,0:T(4,128)S(1)}, s32[3,16]{1,0:T(4,128)}, u32[]{:S(2)}) copy-start(s32[3,16]{1,0:T(4,128)} %off_ref.13) | copy-start | bytes 580
  44.9 3.9 %copy-start.6 = (s32[8]{0:T(128)S(1)}, s32[8]{0:T(128)}, u32[]{:S(2)}) copy-start(s32[8]{0:T(128)} %len_ref.7) | copy-start | bytes 100
  44.9 37.5 %all-to-all-start.1 = ((bf16[8,128,384]{2,1,0:T(8,128)(2,1)}), bf16[8,128,384]{2,1,0:T(8,128)(2,1)S(1)}, u32[]{:S(2)}, u32[]{:S(2)}) async-start(bf16[8,128,384]{2,1,0:T(8,128)(2,1)} %get-tuple-element.36), calls=%async_computation.1 | async-start | bytes 1572864 | tf_op jit(solution)/shard_map/all_to_all | solution.py:399
  61.3 9.4 %collective-permute-start.1 = (bf16[512,128]{1,0:T(8,128)(2,1)S(1)}, bf16[512,128]{1,0:T(8,128)(2,1)S(1)}, u32[]{:S(2)}, u32[]{:S(2)}) collective-permute-start(bf16[512,128]{1,0:T(8,128)(2,1)S(1)} %bitcast.3), channel_id=1, source_target_pairs={{0,8},{1,9},{2,10},{3,11},{4,12},{5,13},{6,14},{7,15},{8,0},{9,1},... | collective-permute-start | bytes 393224 | tf_op jit(solution)/shard_map/ppermute | solution.py:442
  82.4 36.4 %all-to-all-start.4 = ((bf16[8,128,384]{2,1,0:T(8,128)(2,1)}), bf16[8,128,384]{2,1,0:T(8,128)(2,1)S(1)}, u32[]{:S(2)}, u32[]{:S(2)}) async-start(bf16[8,128,384]{2,1,0:T(8,128)(2,1)} %backward1.1), calls=%async_computation.4 | async-start | bytes 1572864 | tf_op jit(solution)/shard_map/all_to_all | solution.py:454
  98.6 9.4 %collective-permute-start = (bf16[512,128]{1,0:T(8,128)(2,1)S(1)}, bf16[512,128]{1,0:T(8,128)(2,1)S(1)}, u32[]{:S(2)}, u32[]{:S(2)}) collective-permute-start(bf16[512,128]{1,0:T(8,128)(2,1)S(1)} %bitcast.2), channel_id=1, source_target_pairs={{0,8},{1,9},{2,10},{3,11},{4,12},{5,13},{6,14},{7,15},{8,0},{9,1},... | collective-permute-start | bytes 393224 | tf_op jit(solution)/shard_map/ppermute | solution.py:442
where the time goes:
time: 136 us
  Pallas kernels  53.3 us (39%)
  blocking collectives  50.7 us (37%)
  waiting for transfers between devices  15.1 us (11%)
  starting transfers between devices  11.3 us (8%)
  local copies, waits for them, and re-layouts  4.66 us (3%)
    pallas_call x2, Pallas kernels, body(): kernel_call(partial(backward_body, plan, chunk), chunk_shape, [SMEM] + [V...  22.4 us
    all_to_all x1, blocking collectives, body(): last = swap(packed[-1])  21.6 us
    ppermute x2, waiting for transfers between devices, body(): back.append(lax.ppermute(far2[s - 1], 'seq', pairs))  15.1 us
    all_to_all x1, blocking collectives, body(): blocks += [swap(x, axis_index_groups=near_groups) for x in packed[1:-1]]  14.6 us
    all_to_all x1, blocking collectives, body(): results.append(swap(out, axis_index_groups=near_groups))  14.5 us
    pallas_call x2, Pallas kernels, body(): kernel_call(partial(forward_body, plan, chunk), [sds((n3, 128), BF16), sd...  14.1 us
    pallas_call x2, Pallas kernels, body(): kernel_call(partial(last_body, plan, chunk), [sds((n3, 128), BF16), sds((...  10.8 us
    unnamed x14, local copies, waits for them, and re-layouts  4.66 us
  transfers between devices with their start and end apart: 4, of which 2 were waited for; matrix products, arithmetic and copies ran while one was open for 0% of the time, Pallas kernels for 35%

commit v1 on v0

v1 whole, which is shorter than its diff:
```python
from functools import partial
import math

import jax
import jax.numpy as jnp
from jax import lax
from jax.experimental import pallas as pl
from jax.experimental.pallas import tpu as pltpu
from jax.sharding import PartitionSpec as P

SEG0 = 1024
BIG = 2.0**100
LOG2E = math.log2(math.e)
BF16 = jnp.bfloat16
F32 = jnp.float32
VMEM_LIMIT = 36 << 20


class Plan:
    def __init__(self, tok_rows, model_width, level_count, head_count, slide_count, device_count):
        self.tok = tok_rows
        self.width = model_width
        self.levels = level_count
        self.hd = model_width // head_count
        self.slides = slide_count
        self.devices = device_count
        self.stride = device_count * tok_rows // SEG0
        self.bits = self.stride.bit_length() - 1
        self.near = min((SEG0 << (level_count - 2)) // tok_rows, device_count)
        self.far = device_count // self.near
        self.chunks = head_count // self.near
        self.segs = self.near * tok_rows // SEG0
        self.seg_dev = SEG0 // tok_rows
        self.cdev = tok_rows // self.stride
        self.cseg = SEG0 // self.stride
        self.rows = self.near * tok_rows
        self.last = self.segs * self.cseg
        self.tiles = []
        for level in range(level_count - 1):
            for first in range(0, self.segs, 1 << level):
                self.tiles.append((level, first))
        self.all_rows = len(self.tiles) * SEG0
        self.slide_pad = -(-slide_count // 8) * 8
        self.rest = 128 - 2 * self.hd - 8 - self.slide_pad
        self.aligned = self.cseg % 128 == 0
        assert self.rest >= 0 and self.hd + 16 <= 64


def reversed_bits(value, bits):
    out = value * 0
    for b in range(bits):
        out = out + ((value >> b) & 1) * (1 << (bits - 1 - b))
    return out


def dot(a, b, ca=1, cb=0, precision=None):
    return lax.dot_general(
        a, b, (((ca,), (cb,)), ((), ())), preferred_element_type=F32, precision=precision
    )


def iota(shape, axis):
    return lax.broadcasted_iota(jnp.int32, shape, axis)


def kernel_call(body, out_shape, in_specs, scratch=(), flops=0, name=None, **more):
    return pl.pallas_call(
        body,
        out_shape=out_shape,
        in_specs=in_specs,
        scratch_shapes=list(scratch),
        name=name,
        compiler_params=pltpu.CompilerParams(vmem_limit_bytes=VMEM_LIMIT),
        cost_estimate=pl.CostEstimate(flops=flops, bytes_accessed=1 << 20, transcendentals=0),
        **more,
    )


VMEM = pl.BlockSpec(memory_space=pltpu.VMEM)
SMEM = pl.BlockSpec(memory_space=pltpu.SMEM)
ANY = pl.BlockSpec(memory_space=pl.ANY)
TOKEN = jax.ShapeDtypeStruct((8, 128), F32)


def class_order(count, stride, shape, axis_row, axis_tok):
    row, tok = iota(shape, axis_row), iota(shape, axis_tok)
    size = count // stride
    want = (row % size) * stride + reversed_bits(row // size, stride.bit_length() - 1)
    return jnp.where(want == tok, 1.0, 0.0).astype(BF16)


def pack_body(plan, *refs):
    out_ref, ins = refs[-1], refs[:-1]
    order = class_order(plan.tok, plan.stride, (plan.tok, plan.tok), 0, 1)
    hd = plan.hd
    for i, ref in enumerate(ins):
        x = dot(ref[...], order, 0, 1).astype(BF16)
        for dest in range(plan.near):
            out_ref[dest, i * hd : (i + 1) * hd, :] = x[dest * hd : (dest + 1) * hd, :]


def segment_from(plan, blocks):
    if plan.cdev % 64 == 0:
        return jnp.concatenate(
            [x[:, c * plan.cdev : (c + 1) * plan.cdev] for c in range(plan.stride) for x in blocks],
            axis=1,
        )
    x = jnp.concatenate(blocks, axis=1).astype(BF16)
    return dot(x, device_lanes(plan, 1, 0))


def device_lanes(plan, axis_dev, axis_seg):
    shape = (SEG0, SEG0)
    seg, dev = iota(shape, axis_dev), iota(shape, axis_seg)
    cls, inside = seg // plan.cseg, seg % plan.cseg
    want = inside // plan.cdev * plan.tok + cls * plan.cdev + inside % plan.cdev
    return jnp.where(want == dev, 1.0, 0.0).astype(BF16)


def segment_to(plan, x):
    if plan.cdev % 64 == 0:
        return [
            jnp.concatenate(
                [
                    x[:, c * plan.cseg + d * plan.cdev : c * plan.cseg + (d + 1) * plan.cdev]
                    for c in range(plan.stride)
                ],
                axis=1,
            )
            for d in range(plan.seg_dev)
        ]
    x = dot(x.astype(BF16), device_lanes(plan, 0, 1))
    return [x[:, d * plan.tok : (d + 1) * plan.tok] for d in range(plan.seg_dev)]


def slide_rows(plan, pos, len_ref):
    slide = jnp.zeros(pos.shape, jnp.int32)
    end = 0
    for i in range(plan.slides):
        end = end + len_ref[i]
        slide = slide + jnp.where(pos >= end, 1, 0)
    shape = (plan.slide_pad, pos.shape[1])
    return jnp.where(iota(shape, 0) == slide, 1.0, 0.0)


def key_features(plan, k, one_hot):
    n = k.shape[1]
    return jnp.concatenate(
        [k, k, jnp.ones((8, n), F32), one_hot, jnp.zeros((plan.rest, n), F32)], axis=0
    )


def query_features(plan, q, one_hot):
    n = q.shape[1]
    q = q * (plan.hd**-0.5 * LOG2E)
    high = q.astype(BF16).astype(F32)
    mask = (one_hot - 1.0) * BIG
    return jnp.concatenate(
        [high, q - high, jnp.zeros((8, n), F32), mask, jnp.zeros((plan.rest, n), F32)], axis=0
    )


def value_features(plan, v):
    n = v.shape[1]
    return jnp.concatenate([v, jnp.ones((8, n), F32), jnp.zeros((56 - plan.hd, n), F32)], axis=0)


def three_rows(x):
    a = x.astype(BF16).astype(F32)
    b = (x - a).astype(BF16).astype(F32)
    row = iota((8, x.shape[1]), 0)
    return jnp.where(row == 0, a, jnp.where(row == 1, b, jnp.where(row == 2, x - a - b, 0.0)))


def forward_tile(plan, keys, queries_t, values_t):
    s = dot(keys, queries_t)
    peak = jnp.max(s, axis=0, keepdims=True)
    p = jnp.exp2(s - peak).astype(BF16)
    o = dot(values_t, p)
    return jnp.concatenate(
        [o[: plan.hd + 8], jnp.broadcast_to(peak, (56 - plan.hd, o.shape[1]))], axis=0
    )


def merged(plan, a, b):
    at = plan.hd + 8
    peak_a, peak_b = a[at : at + 1], b[at : at + 1]
    peak = jnp.maximum(peak_a, peak_b)
    both = a[:at] * jnp.exp2(peak_a - peak) + b[:at] * jnp.exp2(peak_b - peak)
    return jnp.concatenate([both, jnp.broadcast_to(peak, (64 - at, a.shape[1]))], axis=0)


def backward_tile(plan, qa, kat, ga, vat, gt, qt):
    p = jnp.exp2(dot(qa, kat))
    value_t = dot(gt, p.astype(BF16))
    ds = (p * dot(ga, vat)).astype(BF16)
    key_t = dot(qt, ds)
    return dot(kat[: plan.hd], ds, 1, 1), key_t, value_t


def level_start(plan, off_ref, level, chunk):
    head = chunk * plan.near + lax.rem(lax.axis_index("seq"), plan.near)
    bits = level if level < plan.levels - 1 else plan.bits
    rows = SEG0 >> bits
    return reversed_bits(off_ref[level, head] % (1 << bits), bits) * rows, rows


def tile_pieces(plan, off_ref, chunk, tile):
    level, first = plan.tiles[tile]
    start, rows = level_start(plan, off_ref, level, chunk)
    out = []
    for i in range(1 << level):
        src = pl.ds(pl.multiple_of((first + i) * SEG0 + start, 128), rows)
        out.append((src, slice(tile * SEG0 + i * rows, tile * SEG0 + (i + 1) * rows)))
    return out


def last_slices(plan, off_ref, chunk):
    start, count = level_start(plan, off_ref, plan.levels - 1, chunk)
    return [
        pl.ds(pl.multiple_of(seg * SEG0 + start, plan.cseg), count) for seg in range(plan.segs)
    ]


def last_places(plan, off_ref, chunk, shape, axis_seg, axis_last):
    start, _ = level_start(plan, off_ref, plan.levels - 1, chunk)
    hit = iota(shape, axis_seg) == start + iota(shape, axis_last)
    return jnp.where(hit, 1.0, 0.0)


def last_lanes(plan, off_ref, chunk, ref):
    if plan.aligned:
        return jnp.concatenate([ref[:, s] for s in last_slices(plan, off_ref, chunk)], axis=1)
    place = last_places(plan, off_ref, chunk, (SEG0, plan.cseg), 0, 1)
    exact = lax.Precision.HIGHEST
    parts = [
        dot(ref[:, g * SEG0 : (g + 1) * SEG0].astype(F32), place, precision=exact)
        for g in range(plan.segs)
    ]
    return jnp.concatenate(parts, axis=1).astype(ref.dtype)


def last_update(plan, off_ref, chunk, ref, rows, part, update, fill):
    if plan.aligned:
        for seg, s in enumerate(last_slices(plan, off_ref, chunk)):
            ref[rows, s] = update(ref[rows, s], part[:, seg * plan.cseg : (seg + 1) * plan.cseg])
        return
    place = last_places(plan, off_ref, chunk, (plan.cseg, SEG0), 1, 0)
    hit = jnp.max(place, axis=0, keepdims=True) > 0
    for seg in range(plan.segs):
        own = part[:, seg * plan.cseg : (seg + 1) * plan.cseg]
        own = jnp.where(hit, dot(own, place, precision=lax.Precision.HIGHEST), fill)
        s = slice(seg * SEG0, (seg + 1) * SEG0)
        ref[rows, s] = update(ref[rows, s], own)


def no_level(plan):
    return jnp.where(iota((64, 1), 0) >= plan.hd + 8, -BIG, 0.0)


def segment_of(plan, x_ref, first, count, seg):
    return segment_from(
        plan,
        [
            x_ref[seg * plan.seg_dev + d, first : first + count * plan.hd, :].astype(F32)
            for d in range(plan.seg_dev)
        ],
    )


def segment_slides(plan, seg, len_ref):
    base = lax.axis_index("seq") // plan.near * plan.rows + seg * SEG0
    n = iota((1, SEG0), 1)
    pos = base + (n % plan.cseg) * plan.stride + reversed_bits(n // plan.cseg, plan.bits)
    return slide_rows(plan, pos, len_ref)


def forward_body(
    plan, chunk, first, x_ref, len_ref, off_ref, tok_in, acc_ref, q2, kv2, tok_out, ka, qat, vat, raw, res
):
    hd = plan.hd
    tok_out[...] = jnp.zeros_like(tok_out)
    for seg in range(plan.segs):
        rows = slice(seg * SEG0, (seg + 1) * SEG0)
        xt = segment_of(plan, x_ref, first, 3, seg)
        raw[:, rows] = xt.astype(BF16)
        q, k, v = (xt[i * hd : (i + 1) * hd] for i in range(3))
        one_hot = segment_slides(plan, seg, len_ref)
        ka[rows, :] = key_features(plan, k, one_hot).T.astype(BF16)
        qat[:, rows] = query_features(plan, q, one_hot).astype(BF16)
        vat[:, rows] = value_features(plan, v).astype(BF16)
    for tile in range(plan.segs, len(plan.tiles)):
        for src, dst in tile_pieces(plan, off_ref, chunk, tile):
            ka[dst, :] = ka[src, :]
            for ref in (qat, vat):
                ref[:, dst] = ref[:, src]
    last = last_lanes(plan, off_ref, chunk, raw)
    q2[...] = last[0:hd]
    kv2[...] = last[hd:]

    def step(tile, carry):
        rows = pl.ds(pl.multiple_of(tile * SEG0, SEG0), SEG0)
        res[:, rows] = forward_tile(plan, ka[rows, :], qat[:, rows], vat[:, rows])
        return carry

    lax.fori_loop(0, len(plan.tiles), step, 0)
    acc_ref[...] = res[:, 0 : plan.rows]
    for tile in range(plan.segs, len(plan.tiles)):
        for src, dst in tile_pieces(plan, off_ref, chunk, tile):
            acc_ref[:, src] = merged(plan, acc_ref[:, src], res[:, dst])


def last_body(plan, chunk, first, g_ref, len_ref, off_ref, tok_in, acc_ref, q2, kv2, *rest):
    far_in, (att_ref, ld_ref, grad_ref, far_ref, tok_out, acc, gt) = (
        rest[: plan.far - 1],
        rest[plan.far - 1 :],
    )
    hd = plan.hd
    tok_out[...] = jnp.zeros_like(tok_out)
    group = lax.axis_index("seq") // plan.near
    head = chunk * plan.near + lax.rem(lax.axis_index("seq"), plan.near)
    acc[...] = acc_ref[...]
    x = jnp.concatenate([ref[...].astype(F32) for ref in (kv2,) + far_in], axis=1)
    n = iota((1, SEG0), 1)
    owner = group - n // plan.last
    owner = jnp.where(owner < 0, owner + plan.far, owner)
    pos = owner * plan.rows + (n % plan.last) * plan.stride + off_ref[plan.levels - 1, head] % plan.stride
    one_hot = slide_rows(plan, pos, len_ref)
    key_f = key_features(plan, x[0:hd], one_hot)
    query_f = query_features(plan, q2[...].astype(F32), one_hot[:, 0 : plan.last])
    vat2 = value_features(plan, x[hd : 2 * hd]).astype(BF16)
    res = forward_tile(plan, key_f.T.astype(BF16), query_f.astype(BF16), vat2)
    last_update(plan, off_ref, chunk, acc, slice(None), res, partial(merged, plan), no_level(plan))
    for seg in range(plan.segs):
        rows = slice(seg * SEG0, (seg + 1) * SEG0)
        a = acc[:, rows]
        total = a[hd : hd + 1]
        att = (a[0:hd] / total).astype(BF16)
        att_ref[:, rows] = att
        log_total = a[hd + 8 : hd + 9] + jnp.log2(total)
        g = segment_of(plan, g_ref, first, 1, seg)
        gt[:, rows] = g.astype(BF16)
        grad_dot = jnp.sum(g * att.astype(F32), axis=0, keepdims=True)
        ld_ref[:, rows] = jnp.where(iota((8, SEG0), 0) == 0, log_total, grad_dot)
    g2 = last_lanes(plan, off_ref, chunk, gt)
    ld2 = last_lanes(plan, off_ref, chunk, ld_ref)
    qa2, ga2 = backward_queries(plan, query_f, g2.astype(F32), ld2)
    dq, dk, dv = backward_tile(plan, qa2, key_f.astype(BF16), ga2[:, 0:64], vat2, g2, q2[...])
    grad_ref[...] = jnp.concatenate(
        [dq, dk[:, 0 : plan.last], dv[:, 0 : plan.last]], axis=0
    )
    both = jnp.concatenate([dk, dv], axis=0)
    for s in range(1, plan.far):
        far_ref[s - 1] = both[:, s * plan.last : (s + 1) * plan.last].astype(BF16)


def backward_queries(plan, query_f, g, ld):
    hd = plan.hd
    query_f = jnp.concatenate(
        [query_f[0 : 2 * hd], three_rows(-ld[0:1]), query_f[2 * hd + 8 :]], axis=0
    )
    grad_f = jnp.concatenate(
        [g, three_rows(-ld[1:2]), jnp.zeros((120 - hd, g.shape[1]), F32)], axis=0
    )
    return query_f.T.astype(BF16), grad_f.T.astype(BF16)


def backward_body(plan, chunk, places, atts, x_ref, g_ref, len_ref, off_ref, tok_in, *refs):
    att_refs, refs = refs[:atts], refs[atts:]
    (ld_ref, grad2), refs = refs[:2], refs[2:]
    far_refs, refs = refs[: plan.far - 1], refs[plan.far - 1 :]
    out_ref, tok_out, qa, kat, ga, vat, gt, qt, grads = refs
    hd = plan.hd
    tok_out[...] = jnp.zeros_like(tok_out)
    for seg in range(plan.segs):
        rows = slice(seg * SEG0, (seg + 1) * SEG0)
        xt = segment_of(plan, x_ref, places[0], 3, seg)
        q, k, v = (xt[i * hd : (i + 1) * hd] for i in range(3))
        g = segment_of(plan, g_ref, places[1], 1, seg)
        one_hot = segment_slides(plan, seg, len_ref)
        kat[:, rows] = key_features(plan, k, one_hot).astype(BF16)
        vat[:, rows] = value_features(plan, v).astype(BF16)
        qt[:, rows] = q.astype(BF16)
        gt[:, rows] = g.astype(BF16)
        qa[rows, :], ga[rows, :] = backward_queries(
            plan, query_features(plan, q, one_hot), g, ld_ref[:, rows]
        )
    for tile in range(plan.segs, len(plan.tiles)):
        for src, dst in tile_pieces(plan, off_ref, chunk, tile):
            qa[dst, :] = qa[src, :]
            ga[dst, :] = ga[src, :]
            for ref in (kat, vat, gt, qt):
                ref[:, dst] = ref[:, src]

    def step(tile, carry):
        rows = pl.ds(pl.multiple_of(tile * SEG0, SEG0), SEG0)
        parts = backward_tile(
            plan, qa[rows, :], kat[:, rows], ga[rows, 0:64], vat[:, rows], gt[:, rows], qt[:, rows]
        )
        for i, part in enumerate(parts):
            grads[i * hd : (i + 1) * hd, rows] = part
        return carry

    lax.fori_loop(0, len(plan.tiles), step, 0)
    for tile in range(plan.segs, len(plan.tiles)):
        for src, dst in tile_pieces(plan, off_ref, chunk, tile):
            grads[:, src] = grads[:, src] + grads[:, dst]
    more = grad2[...]
    if far_refs:
        far = sum(ref[...].astype(F32) for ref in far_refs)
        more = jnp.concatenate([more[0:hd], more[hd:] + far], axis=0)
    last_update(plan, off_ref, chunk, grads, slice(None), more, jnp.add, 0.0)
    scale = hd**-0.5
    for seg in range(plan.segs):
        rows = slice(seg * SEG0, (seg + 1) * SEG0)
        parts = [ref[:, rows].astype(F32) for ref in att_refs]
        parts += [grads[0 : 2 * hd, rows] * scale, grads[2 * hd : 3 * hd, rows]]
        for d, x in enumerate(segment_to(plan, jnp.concatenate(parts, axis=0))):
            out_ref[seg * plan.seg_dev + d] = x.astype(BF16)


def unpack_body(plan, places, y_ref, *refs):
    outs = refs[-len(places) :]
    hd, width = plan.hd, plan.near * plan.hd
    order = class_order(plan.tok, plan.stride, (plan.tok, plan.tok), 1, 0)
    for out_ref, first in zip(outs, places):
        for col in range(out_ref.shape[1] // width):
            i = first + col
            x = jnp.concatenate([y_ref[d, i * hd : (i + 1) * hd, :] for d in range(plan.near)], axis=0)
            out_ref[:, col * width : (col + 1) * width] = dot(order, x, 1, 1).astype(BF16)


def body(queries, keys, values, out_grad, slide_lengths, head_offsets):
    tok_rows, model_width = queries.shape
    level_count, head_count = head_offsets.shape
    device_count = lax.axis_size("seq")
    plan = Plan(tok_rows, model_width, level_count, head_count, slide_lengths.shape[0], device_count)
    hd, chunks = plan.hd, plan.chunks
    groups = [list(range(i, i + plan.near)) for i in range(0, device_count, plan.near)]
    sds = jax.ShapeDtypeStruct
    swap = partial(
        lax.all_to_all, axis_name="seq", split_axis=0, concat_axis=0, tiled=True, axis_index_groups=groups
    )

    def shifted(x, steps):
        shift = steps * plan.near
        return lax.ppermute(x, "seq", [(i, (i + shift) % device_count) for i in range(device_count)])

    exchanges = [[(c, i) for i in range(3)] for c in range(chunks)]
    for c in range(chunks):
        exchanges[min(c + 1, chunks - 1)].append((c, 3))
    arrays = (queries, keys, values, out_grad)
    width = plan.near * hd
    received, where = [], {}
    for pieces in exchanges:
        packed = kernel_call(
            partial(pack_body, plan),
            sds((plan.near, len(pieces) * hd, plan.tok), BF16),
            [pl.BlockSpec((plan.tok, width), lambda i, c=c: (0, c)) for c, _ in pieces],
            name="pack",
            grid=(1,),
            out_specs=pl.BlockSpec((plan.near, len(pieces) * hd, plan.tok), lambda i: (0, 0, 0)),
        )(*(arrays[i] for _, i in pieces))
        for place, piece in enumerate(pieces):
            where[piece] = (len(received), place * hd)
        received.append(swap(packed))

    n, n3, n2 = plan.rows, plan.all_rows, plan.last
    pair_flops = 20 * 2 * 128 * SEG0 * SEG0
    scalars = (slide_lengths, head_offsets)
    token = jnp.zeros(TOKEN.shape, TOKEN.dtype)
    fronts = []
    for chunk in range(chunks):
        source, first = where[chunk, 0]
        acc, q2, kv2, token = kernel_call(
            partial(forward_body, plan, chunk, first),
            [sds((64, n), F32), sds((hd, n2), BF16), sds((2 * hd, n2), BF16), TOKEN],
            [VMEM, SMEM, SMEM, ANY],
            [
                pltpu.VMEM((n3, 128), BF16),
                pltpu.VMEM((128, n3), BF16),
                pltpu.VMEM((64, n3), BF16),
                pltpu.VMEM((3 * hd, n), BF16),
                pltpu.VMEM((64, n3), F32),
            ],
            flops=len(plan.tiles) * 2 * pair_flops,
            name=f"forward{chunk}",
        )(received[source], *scalars, token)
        fronts.append((acc, q2, kv2, *(shifted(kv2, s) for s in range(1, plan.far))))
    states = []
    for chunk, front in enumerate(fronts):
        source, first = where[chunk, 3]
        att, ld, grad2, far2, token = kernel_call(
            partial(last_body, plan, chunk, first),
            [
                sds((hd, n), BF16),
                sds((8, n), F32),
                sds((3 * hd, n2), F32),
                sds((max(plan.far - 1, 1), 2 * hd, n2), BF16),
                TOKEN,
            ],
            [VMEM, SMEM, SMEM, ANY] + [VMEM] * len(front),
            [pltpu.VMEM((64, n), F32), pltpu.VMEM((hd, n), BF16)],
            flops=4 * pair_flops,
            name=f"last{chunk}",
        )(received[source], *scalars, token, *front)
        states.append((att, (ld, grad2, *(shifted(far2[s - 1], -s) for s in range(1, plan.far)))))
    for chunk, (_, state) in enumerate(states):
        atts = [s[0] for s in states] if chunk == 0 else []
        count = len(atts) + 3
        sources = [where[chunk, 0], where[chunk, 3]]
        out, token = kernel_call(
            partial(backward_body, plan, chunk, [first for _, first in sources], len(atts)),
            [sds((plan.near, count * hd, plan.tok), BF16), TOKEN],
            [VMEM, VMEM, SMEM, SMEM, ANY] + [VMEM] * (len(atts) + len(state)),
            [
                pltpu.VMEM((n3, 128), BF16),
                pltpu.VMEM((128, n3), BF16),
                pltpu.VMEM((n3, 128), BF16),
                pltpu.VMEM((64, n3), BF16),
                pltpu.VMEM((hd, n3), BF16),
                pltpu.VMEM((hd, n3), BF16),
                pltpu.VMEM((3 * hd, n3), F32),
            ],
            flops=len(plan.tiles) * 5 * pair_flops,
            name=f"backward{chunk}",
        )(*(received[source] for source, _ in sources), *scalars, token, *atts, *state)
        y = swap(out)
        full = sds((tok_rows, model_width), BF16)
        whole = pl.BlockSpec(out.shape, lambda i: (0, 0, 0))
        column = pl.BlockSpec((tok_rows, width), lambda i, c=chunk: (0, c))
        if chunk == 0:
            attended, *outs = kernel_call(
                partial(unpack_body, plan, [0] + [chunks + i for i in range(3)]),
                [full] * 4,
                [whole],
                name="unpack",
                grid=(1,),
                out_specs=[pl.BlockSpec(full.shape, lambda i: (0, 0))] + [column] * 3,
            )(y)
        else:
            outs = kernel_call(
                partial(unpack_body, plan, list(range(3))),
                [full] * 3,
                [whole] + [ANY] * 3,
                name="unpack",
                grid=(1,),
                out_specs=[column] * 3,
                input_output_aliases={1: 0, 2: 1, 3: 2},
            )(y, *outs)
    return (attended, *outs)


def solution(mesh):
    rows = P(("groups", "seq"), None)
    return jax.shard_map(
        body,
        mesh=mesh,
        in_specs=(rows, rows, rows, rows, P("groups"), P()),
        out_specs=(rows, rows, rows, rows),
        check_vma=False,
    )
```

time: 136 us -> 99.2 us (0.73)
  blocking collectives: 50.7 us -> 0 us
  waiting for transfers between devices: 15.1 us -> 28.1 us
  starting transfers between devices: 11.3 us -> 22 us
  Pallas kernels: 53.3 us -> 44.2 us
    all_to_all x3 -> x0, blocking collectives: 50.7 us -> none  [the longest x1 21.6 us: body(): last = swap(packed[-1])]
    all_to_all x2 -> x4, waiting for transfers between devices: 0.01 us -> 25.9 us  [the longest x2 14.7 us: body(): received.append(swap(packed))]
    ppermute x2 -> x4, waiting for transfers between devices: 15.1 us -> 2.18 us  [shifted(): lax.ppermute(x, 'seq', [(i, (i + shift) % device_count) for i in range(de...]
    pallas_call x8 -> x10, Pallas kernels: 53.3 us -> 44.2 us  [the longest x2 21.3 us: body(): kernel_call(partial(backward_body, plan, chunk, [first for _, first in so...]
    all_to_all x2 -> x4, starting transfers between devices: 7.63 us -> 16.2 us  [the longest x2 8.91 us: body(): received.append(swap(packed))]
    ppermute x2 -> x4, starting transfers between devices: 3.71 us -> 5.78 us  [shifted(): lax.ppermute(x, 'seq', [(i, (i + shift) % device_count) for i in range(de...]
    unnamed x14 -> x18, local copies, waits for them, and re-layouts: 4.66 us -> 3.66 us
  transfers between devices with their start and end apart: 4 -> 8, of which waited for: 2 -> 6; matrix products, arithmetic and copies ran while one was open for 0% -> 0% of each run, Pallas kernels for 35% -> 43%
where the time goes in v1:
time: 99.2 us; the launch traced here: 98.6 us
  Pallas kernels  44.2 us (45%)
  waiting for transfers between devices  28.1 us (28%)
  starting transfers between devices  22 us (22%)
  local copies, waits for them, and re-layouts  3.66 us (4%)
    pallas_call x2, Pallas kernels, body(): kernel_call(partial(backward_body, plan, chunk, [first for _, first in so...  21.3 us
    all_to_all x2, waiting for transfers between devices, body(): received.append(swap(packed))  14.7 us
    pallas_call x2, Pallas kernels, body(): kernel_call(partial(forward_body, plan, chunk, first), [sds((64, n), F32)...  11.5 us
    all_to_all x2, waiting for transfers between devices, body(): y = swap(out)  11.2 us
    all_to_all x2, starting transfers between devices, body(): received.append(swap(packed))  8.91 us
    all_to_all x2, starting transfers between devices, body(): y = swap(out)  7.27 us
    pallas_call x2, Pallas kernels, body(): kernel_call(partial(last_body, plan, chunk, first), [sds((hd, n), BF16),...  6.37 us
    ppermute x4, starting transfers between devices, shifted(): lax.ppermute(x, 'seq', [(i, (i + shift) % device_count) for i in range(de...  5.78 us
  transfers between devices with their start and end apart: 8, of which 6 were waited for; matrix products, arithmetic and copies ran while one was open for 0% of the time, Pallas kernels for 43%

profile of v1, /device:TPU:0, one launch (start us, length us, event | category | flops | bytes accessed | tf_op | source)
XLA Modules:
  0.0 98.6 jit_solution(13461391115059520856)
XLA Ops:
  0.6 0.0 copy-start
  0.6 1.0 %copy-done = bf16[256,768]{1,0:T(8,128)(2,1)S(1)} copy-done((bf16[256,768]{1,0:T(8,128)(2,1)S(1)}, bf16[256,768]{1,0:T(8,128)(2,1)}, u32[]{:S(2)}) %copy-start) | copy-done | bytes 393240
  1.6 0.0 copy-start.2
  1.6 1.0 %copy-done.2 = bf16[256,768]{1,0:T(8,128)(2,1)S(1)} copy-done((bf16[256,768]{1,0:T(8,128)(2,1)S(1)}, bf16[256,768]{1,0:T(8,128)(2,1)}, u32[]{:S(2)}) %copy-start.2) | copy-done | bytes 393240
  2.6 0.0 copy-start.4
  2.6 1.0 %copy-done.4 = bf16[256,768]{1,0:T(8,128)(2,1)S(1)} copy-done((bf16[256,768]{1,0:T(8,128)(2,1)S(1)}, bf16[256,768]{1,0:T(8,128)(2,1)}, u32[]{:S(2)}) %copy-start.4) | copy-done | bytes 393240
  3.6 0.0 copy-start.6
  3.6 1.2 %pack.2 = bf16[8,144,256]{2,1,0:T(8,128)(2,1)} custom-call(bf16[256,768]{1,0:T(8,128)(2,1)S(1)} %copy-done, bf16[256,768]{1,0:T(8,128)(2,1)S(1)} %copy-done.2, bf16[256,768]{1,0:T(8,128)(2,1)S(1)} %copy-done.4), custom_call_target="tpu_custom_call" | custom-call | bytes 1048576 | tf_op jit(solution)/shard_map/pack/pallas_call | solution.py:456
  4.8 0.0 copy-start.1
  4.8 0.0 copy-start.3
  4.8 0.0 copy-start.5
  4.8 5.4 %all-to-all-start = ((bf16[8,144,256]{2,1,0:T(8,128)(2,1)}), bf16[8,144,256]{2,1,0:T(8,128)(2,1)S(1)}, u32[]{:S(2)}, u32[]{:S(2)}) async-start(bf16[8,144,256]{2,1,0:T(8,128)(2,1)} %pack.2), calls=%async_computation | async-start | bytes 1179648 | tf_op jit(solution)/shard_map/all_to_all | solution.py:466
  10.2 0.0 copy-done.6
  10.2 0.0 copy-done.1
  10.2 0.0 copy-done.3
  10.2 0.0 copy-done.5
  10.2 1.5 %pack.3 = bf16[8,240,256]{2,1,0:T(8,128)(2,1)} custom-call(bf16[256,768]{1,0:T(8,128)(2,1)S(1)} %copy-done.1, bf16[256,768]{1,0:T(8,128)(2,1)S(1)} %copy-done.3, bf16[256,768]{1,0:T(8,128)(2,1)S(1)} %copy-done.5, bf16[256,768]{1,0:T(8,128)(2,1)S(1)} %copy-done.6, bf16[256,768]{1,0:T(8,128)(2,1)S(1)} %copy-done.6), custom_call_target="tpu_custom_call" | custom-call | bytes 1048576 | tf_op jit(solution)/shard_map/pack/pallas_call | solution.py:456
  11.7 8.0 %all-to-all-done.x_ref = bf16[8,144,256]{2,1,0:T(8,128)(2,1)S(1)} async-done(((bf16[8,144,256]{2,1,0:T(8,128)(2,1)}), bf16[8,144,256]{2,1,0:T(8,128)(2,1)S(1)}, u32[]{:S(2)}, u32[]{:S(2)}) %all-to-all-start) | async-done | bytes 589856 | tf_op jit(solution)/shard_map/all_to_all | solution.py:466
  19.7 3.6 %all-to-all-start.1 = ((bf16[8,240,256]{2,1,0:T(8,128)(2,1)}), bf16[8,240,256]{2,1,0:T(8,128)(2,1)S(1)}, u32[]{:S(2)}, u32[]{:S(2)}) async-start(bf16[8,240,256]{2,1,0:T(8,128)(2,1)} %pack.3), calls=%async_computation.1 | async-start | bytes 1966080 | tf_op jit(solution)/shard_map/all_to_all | solution.py:466
  23.3 0.0 copy-start.7
  23.3 0.0 copy-start.8
  23.3 0.7 copy-done.7
  24.0 0.0 copy-done.8
  24.0 5.8 %forward0.1 = (f32[64,2048]{1,0:T(8,128)S(1)}, bf16[48,512]{1,0:T(8,128)(2,1)S(1)}, bf16[96,512]{1,0:T(8,128)(2,1)S(1)}, f32[8,128]{1,0:T(8,128)S(1)}) custom-call(bf16[8,144,256]{2,1,0:T(8,128)(2,1)S(1)} %all-to-all-done.x_ref, s32[8]{0:T(128)S(1)} %copy-done.8, s32[3,16]{1,0:T(4,128)S(1)} %copy-done.7, f32[8,128]{1,0:T(8,128)S(1)} %broadcast_in_dim.3.tok_in), custom_call_target="tpu_custom_call" | custom-call | flops 32212254720 | bytes 1048576 | tf_op jit(solution)/shard_map/forward0/pallas_call | solution.py:475
  29.8 2.7 %collective-permute-start = (bf16[96,512]{1,0:T(8,128)(2,1)S(1)}, bf16[96,512]{1,0:T(8,128)(2,1)S(1)}, u32[]{:S(2)}, u32[]{:S(2)}) collective-permute-start(bf16[96,512]{1,0:T(8,128)(2,1)S(1)} %get-tuple-element.36.kv2), channel_id=1, source_target_pairs={{0,8},{1,9},{2,10},{3,11},{4,12},{5,13},{6,14},{7,15},{8,0},{9,1},... | collective-permute-start | bytes 294920 | tf_op jit(solution)/shard_map/ppermute | solution.py:447
  32.4 6.7 %all-to-all-done.1.x_ref.g_ref = bf16[8,240,256]{2,1,0:T(8,128)(2,1)S(1)} async-done(((bf16[8,240,256]{2,1,0:T(8,128)(2,1)}), bf16[8,240,256]{2,1,0:T(8,128)(2,1)S(1)}, u32[]{:S(2)}, u32[]{:S(2)}) %all-to-all-start.1) | async-done | bytes 983072 | tf_op jit(solution)/shard_map/all_to_all | solution.py:466
  39.1 5.8 %forward1.1 = (f32[64,2048]{1,0:T(8,128)S(1)}, bf16[48,512]{1,0:T(8,128)(2,1)S(1)}, bf16[96,512]{1,0:T(8,128)(2,1)S(1)}, f32[8,128]{1,0:T(8,128)S(1)}) custom-call(bf16[8,240,256]{2,1,0:T(8,128)(2,1)S(1)} %all-to-all-done.1.x_ref.g_ref, s32[8]{0:T(128)S(1)} %copy-done.8, s32[3,16]{1,0:T(4,128)S(1)} %copy-done.7, f32[8,128]{1,0:T(8,128)S(1)} %get-tuple-element.32.tok_in), custom_call_target="tpu_custom_call" | custom-call | flops 32212254720 | bytes 1048576 | tf_op jit(solution)/shard_map/forward1/pallas_call | solution.py:475
  44.9 1.0 %collective-permute-start.1 = (bf16[96,512]{1,0:T(8,128)(2,1)S(1)}, bf16[96,512]{1,0:T(8,128)(2,1)S(1)}, u32[]{:S(2)}, u32[]{:S(2)}) collective-permute-start(bf16[96,512]{1,0:T(8,128)(2,1)S(1)} %get-tuple-element.40.kv2), channel_id=1, source_target_pairs={{0,8},{1,9},{2,10},{3,11},{4,12},{5,13},{6,14},{7,15},{8,0},{9,1},... | collective-permute-start | bytes 294920 | tf_op jit(solution)/shard_map/ppermute | solution.py:447
  45.9 0.0 collective-permute-done.rest_0_
  45.9 3.2 %last0.1 = (bf16[48,2048]{1,0:T(8,128)(2,1)S(1)}, f32[8,2048]{1,0:T(8,128)S(1)}, f32[144,512]{1,0:T(8,128)S(1)}, bf16[1,96,512]{2,1,0:T(8,128)(2,1)S(1)}, f32[8,128]{1,0:T(8,128)S(1)}) custom-call(bf16[8,240,256]{2,1,0:T(8,128)(2,1)S(1)} %all-to-all-done.1.x_ref.g_ref, s32[8]{0:T(128)S(1)} %copy-done.8, s32[3,16]{1,0:T(4,128)S(1)} %copy-done.7, ...), custom_call_target="tpu_custom_call" | custom-call | flops 21474836480 | bytes 1048576 | tf_op jit(solution)/shard_map/last0/pallas_call | solution.py:493
  49.1 2.0 %collective-permute-start.2 = (bf16[96,512]{1,0:T(8,128)(2,1)S(1)}, bf16[96,512]{1,0:T(8,128)(2,1)S(1)}, u32[]{:S(2)}, u32[]{:S(2)}) collective-permute-start(bf16[96,512]{1,0:T(8,128)(2,1)S(1)} %bitcast.2), channel_id=1, source_target_pairs={{0,8},{1,9},{2,10},{3,11},{4,12},{5,13},{6,14},{7,15},{8,0},{9,1},... | collective-permute-start | bytes 294920 | tf_op jit(solution)/shard_map/ppermute | solution.py:447
  51.1 1.0 collective-permute-done.1.rest_0_
  52.1 3.2 %last1.1 = (bf16[48,2048]{1,0:T(8,128)(2,1)S(1)}, f32[8,2048]{1,0:T(8,128)S(1)}, f32[144,512]{1,0:T(8,128)S(1)}, bf16[1,96,512]{2,1,0:T(8,128)(2,1)S(1)}, f32[8,128]{1,0:T(8,128)S(1)}) custom-call(bf16[8,240,256]{2,1,0:T(8,128)(2,1)S(1)} %all-to-all-done.1.x_ref.g_ref, s32[8]{0:T(128)S(1)} %copy-done.8, s32[3,16]{1,0:T(4,128)S(1)} %copy-done.7, ...), custom_call_target="tpu_custom_call" | custom-call | flops 21474836480 | bytes 1048576 | tf_op jit(solution)/shard_map/last1/pallas_call | solution.py:493
  55.3 0.1 collective-permute-start.3
  55.4 1.2 %collective-permute-done.2.refs_4_ = bf16[96,512]{1,0:T(8,128)(2,1)S(1)} collective-permute-done((bf16[96,512]{1,0:T(8,128)(2,1)S(1)}, bf16[96,512]{1,0:T(8,128)(2,1)S(1)}, u32[]{:S(2)}, u32[]{:S(2)}) %collective-permute-start.2) | collective-permute-done | bytes 98336 | tf_op jit(solution)/shard_map/ppermute | solution.py:447
  56.6 10.8 %backward0.1 = (bf16[8,240,256]{2,1,0:T(8,128)(2,1)}, f32[8,128]{1,0:T(8,128)S(1)}) custom-call(bf16[8,144,256]{2,1,0:T(8,128)(2,1)S(1)} %all-to-all-done.x_ref, bf16[8,240,256]{2,1,0:T(8,128)(2,1)S(1)} %all-to-all-done.1.x_ref.g_ref, s32[8]{0:T(128)S(1)} %copy-done.8, s32[3,16]{1,0:T(4,128)S(1)} %copy-done.7, f32[8,128]{1,0:T(8,128)S(1)} %get-tuple-element.41.tok_in, ...), custom_call_target="tpu_custom_call" | custom-call | flops 80530636800 | bytes 1048576 | tf_op jit(solution)/shard_map/backward0/pallas_call | solution.py:512
  67.3 3.7 %all-to-all-start.2 = ((bf16[8,240,256]{2,1,0:T(8,128)(2,1)}), bf16[8,240,256]{2,1,0:T(8,128)(2,1)S(1)}, u32[]{:S(2)}, u32[]{:S(2)}) async-start(bf16[8,240,256]{2,1,0:T(8,128)(2,1)} %get-tuple-element.47), calls=%async_computation.2 | async-start | bytes 1966080 | tf_op jit(solution)/shard_map/all_to_all | solution.py:528
  71.1 0.0 collective-permute-done.3.refs_2_
  71.1 10.5 %backward1.1 = (bf16[8,144,256]{2,1,0:T(8,128)(2,1)}, f32[8,128]{1,0:T(8,128)}) custom-call(bf16[8,240,256]{2,1,0:T(8,128)(2,1)S(1)} %all-to-all-done.1.x_ref.g_ref, bf16[8,240,256]{2,1,0:T(8,128)(2,1)S(1)} %all-to-all-done.1.x_ref.g_ref, s32[8]{0:T(128)S(1)} %copy-done.8, s32[3,16]{1,0:T(4,128)S(1)} %copy-done.7, f32[8,128]{1,0:T(8,128)S(1)} %get-tuple-element.49.tok_in, ...), custom_call_target="tpu_custom_call" | custom-call | flops 80530636800 | bytes 1048576 | tf_op jit(solution)/shard_map/backward1/pallas_call | solution.py:512
  81.6 3.0 %all-to-all-done.2.y_ref = bf16[8,240,256]{2,1,0:T(8,128)(2,1)S(1)} async-done(((bf16[8,240,256]{2,1,0:T(8,128)(2,1)}), bf16[8,240,256]{2,1,0:T(8,128)(2,1)S(1)}, u32[]{:S(2)}, u32[]{:S(2)}) %all-to-all-start.2) | async-done | bytes 983072 | tf_op jit(solution)/shard_map/all_to_all | solution.py:528
  84.6 3.5 %all-to-all-start.3 = ((bf16[8,144,256]{2,1,0:T(8,128)(2,1)}), bf16[8,144,256]{2,1,0:T(8,128)(2,1)S(1)}, u32[]{:S(2)}, u32[]{:S(2)}) async-start(bf16[8,144,256]{2,1,0:T(8,128)(2,1)} %get-tuple-element.53), calls=%async_computation.3 | async-start | bytes 1179648 | tf_op jit(solution)/shard_map/all_to_all | solution.py:528
  88.1 1.3 %unpack.2 = (bf16[256,768]{1,0:T(8,128)(2,1)}, bf16[256,768]{1,0:T(8,128)(2,1)}, bf16[256,768]{1,0:T(8,128)(2,1)}, bf16[256,768]{1,0:T(8,128)(2,1)}) custom-call(bf16[8,240,256]{2,1,0:T(8,128)(2,1)S(1)} %all-to-all-done.2.y_ref), custom_call_target="tpu_custom_call" | custom-call | bytes 1048576 | tf_op jit(solution)/shard_map/unpack/pallas_call | solution.py:533
  89.4 8.2 %all-to-all-done.3.y_ref = bf16[8,144,256]{2,1,0:T(8,128)(2,1)S(1)} async-done(((bf16[8,144,256]{2,1,0:T(8,128)(2,1)}), bf16[8,144,256]{2,1,0:T(8,128)(2,1)S(1)}, u32[]{:S(2)}, u32[]{:S(2)}) %all-to-all-start.3) | async-done | bytes 589856 | tf_op jit(solution)/shard_map/all_to_all | solution.py:528
  97.6 1.1 %unpack.3 = (bf16[256,768]{1,0:T(8,128)(2,1)}, bf16[256,768]{1,0:T(8,128)(2,1)}, bf16[256,768]{1,0:T(8,128)(2,1)}) custom-call(bf16[8,144,256]{2,1,0:T(8,128)(2,1)S(1)} %all-to-all-done.3.y_ref, bf16[256,768]{1,0:T(8,128)(2,1)} %get-tuple-element.54.refs_0_, ...), custom_call_target="tpu_custom_call", output_to_operand_aliasing={{0}: (1, {}), {1}: (2, {}), {2}: (3, {})} | custom-call | bytes 1048576 | tf_op jit(solution)/shard_map/unpack/pallas_call | solution.py:542
  (1 shorter events, 0.0 us)
Async XLA Ops:
  0.6 1.0 %copy-start = (bf16[256,768]{1,0:T(8,128)(2,1)S(1)}, bf16[256,768]{1,0:T(8,128)(2,1)}, u32[]{:S(2)}) copy-start(bf16[256,768]{1,0:T(8,128)(2,1)} %refs_0_.3) | copy-start | bytes 1179652
  1.6 1.0 %copy-start.2 = (bf16[256,768]{1,0:T(8,128)(2,1)S(1)}, bf16[256,768]{1,0:T(8,128)(2,1)}, u32[]{:S(2)}) copy-start(bf16[256,768]{1,0:T(8,128)(2,1)} %refs_1_.3) | copy-start | bytes 1179652
  2.6 1.0 %copy-start.4 = (bf16[256,768]{1,0:T(8,128)(2,1)S(1)}, bf16[256,768]{1,0:T(8,128)(2,1)}, u32[]{:S(2)}) copy-start(bf16[256,768]{1,0:T(8,128)(2,1)} %refs_2_.3) | copy-start | bytes 1179652
  3.6 6.6 %copy-start.6 = (bf16[256,768]{1,0:T(8,128)(2,1)S(1)}, bf16[256,768]{1,0:T(8,128)(2,1)}, u32[]{:S(2)}) copy-start(bf16[256,768]{1,0:T(8,128)(2,1)} %refs_4_.1) | copy-start | bytes 1179652
  4.8 5.4 %copy-start.1 = (bf16[256,768]{1,0:T(8,128)(2,1)S(1)}, bf16[256,768]{1,0:T(8,128)(2,1)}, u32[]{:S(2)}) copy-start(bf16[256,768]{1,0:T(8,128)(2,1)} %refs_0_.3) | copy-start | bytes 1179652
  4.8 5.4 %copy-start.3 = (bf16[256,768]{1,0:T(8,128)(2,1)S(1)}, bf16[256,768]{1,0:T(8,128)(2,1)}, u32[]{:S(2)}) copy-start(bf16[256,768]{1,0:T(8,128)(2,1)} %refs_1_.3) | copy-start | bytes 1179652
  4.8 5.4 %copy-start.5 = (bf16[256,768]{1,0:T(8,128)(2,1)S(1)}, bf16[256,768]{1,0:T(8,128)(2,1)}, u32[]{:S(2)}) copy-start(bf16[256,768]{1,0:T(8,128)(2,1)} %refs_2_.3) | copy-start | bytes 1179652
  4.8 14.9 %all-to-all-start = ((bf16[8,144,256]{2,1,0:T(8,128)(2,1)}), bf16[8,144,256]{2,1,0:T(8,128)(2,1)S(1)}, u32[]{:S(2)}, u32[]{:S(2)}) async-start(bf16[8,144,256]{2,1,0:T(8,128)(2,1)} %pack.2), calls=%async_computation | async-start | bytes 1179648 | tf_op jit(solution)/shard_map/all_to_all | solution.py:466
  19.7 19.3 %all-to-all-start.1 = ((bf16[8,240,256]{2,1,0:T(8,128)(2,1)}), bf16[8,240,256]{2,1,0:T(8,128)(2,1)S(1)}, u32[]{:S(2)}, u32[]{:S(2)}) async-start(bf16[8,240,256]{2,1,0:T(8,128)(2,1)} %pack.3), calls=%async_computation.1 | async-start | bytes 1966080 | tf_op jit(solution)/shard_map/all_to_all | solution.py:466
  23.3 0.7 copy-start.7
  23.3 0.7 copy-start.8
  29.8 16.1 %collective-permute-start = (bf16[96,512]{1,0:T(8,128)(2,1)S(1)}, bf16[96,512]{1,0:T(8,128)(2,1)S(1)}, u32[]{:S(2)}, u32[]{:S(2)}) collective-permute-start(bf16[96,512]{1,0:T(8,128)(2,1)S(1)} %get-tuple-element.36.kv2), channel_id=1, source_target_pairs={{0,8},{1,9},{2,10},{3,11},{4,12},{5,13},{6,14},{7,15},{8,0},{9,1},... | collective-permute-start | bytes 294920 | tf_op jit(solution)/shard_map/ppermute | solution.py:447
  44.9 7.2 %collective-permute-start.1 = (bf16[96,512]{1,0:T(8,128)(2,1)S(1)}, bf16[96,512]{1,0:T(8,128)(2,1)S(1)}, u32[]{:S(2)}, u32[]{:S(2)}) collective-permute-start(bf16[96,512]{1,0:T(8,128)(2,1)S(1)} %get-tuple-element.40.kv2), channel_id=1, source_target_pairs={{0,8},{1,9},{2,10},{3,11},{4,12},{5,13},{6,14},{7,15},{8,0},{9,1},... | collective-permute-start | bytes 294920 | tf_op jit(solution)/shard_map/ppermute | solution.py:447
  49.1 7.5 %collective-permute-start.2 = (bf16[96,512]{1,0:T(8,128)(2,1)S(1)}, bf16[96,512]{1,0:T(8,128)(2,1)S(1)}, u32[]{:S(2)}, u32[]{:S(2)}) collective-permute-start(bf16[96,512]{1,0:T(8,128)(2,1)S(1)} %bitcast.2), channel_id=1, source_target_pairs={{0,8},{1,9},{2,10},{3,11},{4,12},{5,13},{6,14},{7,15},{8,0},{9,1},... | collective-permute-start | bytes 294920 | tf_op jit(solution)/shard_map/ppermute | solution.py:447
  55.3 15.8 %collective-permute-start.3 = (bf16[96,512]{1,0:T(8,128)(2,1)S(1)}, bf16[96,512]{1,0:T(8,128)(2,1)S(1)}, u32[]{:S(2)}, u32[]{:S(2)}) collective-permute-start(bf16[96,512]{1,0:T(8,128)(2,1)S(1)} %bitcast.3), channel_id=1, source_target_pairs={{0,8},{1,9},{2,10},{3,11},{4,12},{5,13},{6,14},{7,15},{8,0},{9,1},... | collective-permute-start | bytes 294920 | tf_op jit(solution)/shard_map/ppermute | solution.py:447
  67.3 17.2 %all-to-all-start.2 = ((bf16[8,240,256]{2,1,0:T(8,128)(2,1)}), bf16[8,240,256]{2,1,0:T(8,128)(2,1)S(1)}, u32[]{:S(2)}, u32[]{:S(2)}) async-start(bf16[8,240,256]{2,1,0:T(8,128)(2,1)} %get-tuple-element.47), calls=%async_computation.2 | async-start | bytes 1966080 | tf_op jit(solution)/shard_map/all_to_all | solution.py:528
  84.6 13.0 %all-to-all-start.3 = ((bf16[8,144,256]{2,1,0:T(8,128)(2,1)}), bf16[8,144,256]{2,1,0:T(8,128)(2,1)S(1)}, u32[]{:S(2)}, u32[]{:S(2)}) async-start(bf16[8,144,256]{2,1,0:T(8,128)(2,1)} %get-tuple-element.53), calls=%async_computation.3 | async-start | bytes 1179648 | tf_op jit(solution)/shard_map/all_to_all | solution.py:528

commit v2 on v1

--- a/solution.py
+++ b/solution.py
@@ -14,6 +14,7 @@
 BF16 = jnp.bfloat16
 F32 = jnp.float32
 VMEM_LIMIT = 36 << 20
+PACK_LIMIT = 63 << 20
 
 
 class Plan:
@@ -43,7 +44,7 @@
         self.slide_pad = -(-slide_count // 8) * 8
         self.rest = 128 - 2 * self.hd - 8 - self.slide_pad
         self.aligned = self.cseg % 128 == 0
-        assert self.rest >= 0 and self.hd + 16 <= 64
+        assert self.rest >= 0 and self.hd + 16 <= 64 and self.hd % 16 == 0
 
 
 def reversed_bits(value, bits):
@@ -63,14 +64,14 @@
     return lax.broadcasted_iota(jnp.int32, shape, axis)
 
 
-def kernel_call(body, out_shape, in_specs, scratch=(), flops=0, name=None, **more):
+def kernel_call(body, out_shape, in_specs, scratch=(), flops=0, name=None, limit=VMEM_LIMIT, **more):
     return pl.pallas_call(
         body,
         out_shape=out_shape,
         in_specs=in_specs,
         scratch_shapes=list(scratch),
         name=name,
-        compiler_params=pltpu.CompilerParams(vmem_limit_bytes=VMEM_LIMIT),
+        compiler_params=pltpu.CompilerParams(vmem_limit_bytes=limit),
         cost_estimate=pl.CostEstimate(flops=flops, bytes_accessed=1 << 20, transcendentals=0),
         **more,
     )
@@ -89,14 +90,32 @@
     return jnp.where(want == tok, 1.0, 0.0).astype(BF16)
 
 
-def pack_body(plan, *refs):
-    out_ref, ins = refs[-1], refs[:-1]
+def near_index(plan):
+    return lax.rem(lax.axis_index("seq"), plan.near)
+
+
+def pack_body(plan, columns, count_out, *refs):
+    count = len(columns)
+    ins, outs, (tok_out, rows, turned, sems) = refs[:count], refs[-4 - count_out : -4], refs[-4:]
+    tok_out[...] = jnp.zeros_like(tok_out)
+    hd, width = plan.hd, plan.near * plan.hd
+    copies = [
+        pltpu.make_async_copy(ref.at[:, c * width : (c + 1) * width], rows.at[i], sems.at[i])
+        for i, (ref, c) in enumerate(zip(ins, columns))
+    ]
+    for copy in copies:
+        copy.start()
     order = class_order(plan.tok, plan.stride, (plan.tok, plan.tok), 0, 1)
-    hd = plan.hd
-    for i, ref in enumerate(ins):
-        x = dot(ref[...], order, 0, 1).astype(BF16)
-        for dest in range(plan.near):
-            out_ref[dest, i * hd : (i + 1) * hd, :] = x[dest * hd : (dest + 1) * hd, :]
+    me = near_index(plan)
+    for i, copy in enumerate(copies):
+        copy.wait()
+        turned[...] = dot(rows[i], order, 0, 1).astype(BF16)
+        for j in range(plan.near):
+            if len(outs) == 1:
+                outs[0][j, i * hd : (i + 1) * hd, :] = turned[j * hd : (j + 1) * hd, :]
+            else:
+                first = pl.multiple_of((me ^ j) * hd, 16)
+                outs[j][i * hd : (i + 1) * hd, :] = turned[pl.ds(first, hd), :]
 
 
 def segment_from(plan, blocks):
@@ -258,31 +277,45 @@
     return jnp.where(iota((64, 1), 0) >= plan.hd + 8, -BIG, 0.0)
 
 
-def segment_of(plan, x_ref, first, count, seg):
+def slots_of(plan, refs):
+    if len(refs) > 1:
+        return refs
+    return [refs[0].at[near_index(plan) ^ j] for j in range(plan.near)]
+
+
+def segment_of(plan, slots, first, count, seg):
     return segment_from(
         plan,
         [
-            x_ref[seg * plan.seg_dev + d, first : first + count * plan.hd, :].astype(F32)
+            slots[seg * plan.seg_dev + d][first : first + count * plan.hd, :].astype(F32)
             for d in range(plan.seg_dev)
         ],
     )
 
 
+def slot_tokens(plan, seg, slot, inside):
+    me = near_index(plan)
+    seg = (me // plan.seg_dev) ^ seg
+    return seg * SEG0 + (lax.rem(me, plan.seg_dev) ^ slot) * plan.tok + inside
+
+
 def segment_slides(plan, seg, len_ref):
-    base = lax.axis_index("seq") // plan.near * plan.rows + seg * SEG0
     n = iota((1, SEG0), 1)
-    pos = base + (n % plan.cseg) * plan.stride + reversed_bits(n // plan.cseg, plan.bits)
-    return slide_rows(plan, pos, len_ref)
+    inside = (n % plan.cdev) * plan.stride + reversed_bits(n // plan.cseg, plan.bits)
+    pos = slot_tokens(plan, seg, n % plan.cseg // plan.cdev, inside)
+    return slide_rows(plan, lax.axis_index("seq") // plan.near * plan.rows + pos, len_ref)
 
 
 def forward_body(
-    plan, chunk, first, x_ref, len_ref, off_ref, tok_in, acc_ref, q2, kv2, tok_out, ka, qat, vat, raw, res
+    plan, chunk, first, blocks, len_ref, off_ref, tok_in, *refs
 ):
+    acc_ref, q2, kv2, tok_out, ka, qat, vat, raw, res = refs[blocks:]
+    slots = slots_of(plan, refs[:blocks])
     hd = plan.hd
     tok_out[...] = jnp.zeros_like(tok_out)
     for seg in range(plan.segs):
         rows = slice(seg * SEG0, (seg + 1) * SEG0)
-        xt = segment_of(plan, x_ref, first, 3, seg)
+        xt = segment_of(plan, slots, first, 3, seg)
         raw[:, rows] = xt.astype(BF16)
         q, k, v = (xt[i * hd : (i + 1) * hd] for i in range(3))
         one_hot = segment_slides(plan, seg, len_ref)
@@ -310,7 +343,8 @@
             acc_ref[:, src] = merged(plan, acc_ref[:, src], res[:, dst])
 
 
-def last_body(plan, chunk, first, g_ref, len_ref, off_ref, tok_in, acc_ref, q2, kv2, *rest):
+def last_body(plan, chunk, first, blocks, len_ref, off_ref, tok_in, acc_ref, q2, kv2, *rest):
+    slots, rest = slots_of(plan, rest[:blocks]), rest[blocks:]
     far_in, (att_ref, ld_ref, grad_ref, far_ref, tok_out, acc, gt) = (
         rest[: plan.far - 1],
         rest[plan.far - 1 :],
@@ -324,7 +358,9 @@
     n = iota((1, SEG0), 1)
     owner = group - n // plan.last
     owner = jnp.where(owner < 0, owner + plan.far, owner)
-    pos = owner * plan.rows + (n % plan.last) * plan.stride + off_ref[plan.levels - 1, head] % plan.stride
+    inside = (n % plan.cdev) * plan.stride + off_ref[plan.levels - 1, head] % plan.stride
+    seg, slot = n % plan.last // plan.cseg, n % plan.cseg // plan.cdev
+    pos = owner * plan.rows + slot_tokens(plan, seg, slot, inside)
     one_hot = slide_rows(plan, pos, len_ref)
     key_f = key_features(plan, x[0:hd], one_hot)
     query_f = query_features(plan, q2[...].astype(F32), one_hot[:, 0 : plan.last])
@@ -338,7 +374,7 @@
         att = (a[0:hd] / total).astype(BF16)
         att_ref[:, rows] = att
         log_total = a[hd + 8 : hd + 9] + jnp.log2(total)
-        g = segment_of(plan, g_ref, first, 1, seg)
+        g = segment_of(plan, slots, first, 1, seg)
         gt[:, rows] = g.astype(BF16)
         grad_dot = jnp.sum(g * att.astype(F32), axis=0, keepdims=True)
         ld_ref[:, rows] = jnp.where(iota((8, SEG0), 0) == 0, log_total, grad_dot)
@@ -365,18 +401,20 @@
     return query_f.T.astype(BF16), grad_f.T.astype(BF16)
 
 
-def backward_body(plan, chunk, places, atts, x_ref, g_ref, len_ref, off_ref, tok_in, *refs):
+def backward_body(plan, chunk, places, blocks, atts, slotted, len_ref, off_ref, tok_in, *refs):
+    slots, refs = slots_of(plan, refs[: blocks[0]]), refs[blocks[0] :]
+    g_slots, refs = slots_of(plan, refs[: blocks[1]]), refs[blocks[1] :]
     att_refs, refs = refs[:atts], refs[atts:]
     (ld_ref, grad2), refs = refs[:2], refs[2:]
     far_refs, refs = refs[: plan.far - 1], refs[plan.far - 1 :]
-    out_ref, tok_out, qa, kat, ga, vat, gt, qt, grads = refs
+    outs, (tok_out, qa, kat, ga, vat, gt, qt, grads) = refs[:-8], refs[-8:]
     hd = plan.hd
     tok_out[...] = jnp.zeros_like(tok_out)
     for seg in range(plan.segs):
         rows = slice(seg * SEG0, (seg + 1) * SEG0)
-        xt = segment_of(plan, x_ref, places[0], 3, seg)
+        xt = segment_of(plan, slots, places[0], 3, seg)
         q, k, v = (xt[i * hd : (i + 1) * hd] for i in range(3))
-        g = segment_of(plan, g_ref, places[1], 1, seg)
+        g = segment_of(plan, g_slots, places[1], 1, seg)
         one_hot = segment_slides(plan, seg, len_ref)
         kat[:, rows] = key_features(plan, k, one_hot).astype(BF16)
         vat[:, rows] = value_features(plan, v).astype(BF16)
@@ -416,11 +454,20 @@
         parts = [ref[:, rows].astype(F32) for ref in att_refs]
         parts += [grads[0 : 2 * hd, rows] * scale, grads[2 * hd : 3 * hd, rows]]
         for d, x in enumerate(segment_to(plan, jnp.concatenate(parts, axis=0))):
-            out_ref[seg * plan.seg_dev + d] = x.astype(BF16)
-
-
-def unpack_body(plan, places, y_ref, *refs):
-    outs = refs[-len(places) :]
+            slot = seg * plan.seg_dev + d
+            if slotted:
+                outs[slot][...] = x.astype(BF16)
+            else:
+                outs[0][near_index(plan) ^ slot] = x.astype(BF16)
+
+
+def unpack_body(plan, places, slotted, *refs):
+    if slotted:
+        y_ref, outs = refs[-1], refs[-1 - len(places) : -1]
+        for j in range(plan.near):
+            y_ref[near_index(plan) ^ j] = refs[j][...]
+    else:
+        y_ref, outs = refs[0], refs[-len(places) :]
     hd, width = plan.hd, plan.near * plan.hd
     order = class_order(plan.tok, plan.stride, (plan.tok, plan.tok), 1, 0)
     for out_ref, first in zip(outs, places):
@@ -438,44 +485,58 @@
     hd, chunks = plan.hd, plan.chunks
     groups = [list(range(i, i + plan.near)) for i in range(0, device_count, plan.near)]
     sds = jax.ShapeDtypeStruct
-    swap = partial(
-        lax.all_to_all, axis_name="seq", split_axis=0, concat_axis=0, tiled=True, axis_index_groups=groups
-    )
+    near = plan.near
+
+    def permuted(x, target):
+        return lax.ppermute(x, "seq", [(i, target(i)) for i in range(device_count)])
+
+    def swap(x):
+        return lax.all_to_all(x, "seq", 0, 0, tiled=True, axis_index_groups=groups)
 
     def shifted(x, steps):
-        shift = steps * plan.near
-        return lax.ppermute(x, "seq", [(i, (i + shift) % device_count) for i in range(device_count)])
+        return permuted(x, lambda i: (i + steps * near) % device_count)
+
+    def traded(slots):
+        return [slots[0]] + [permuted(slots[j], lambda i, j=j: i ^ j) for j in range(near - 1, 0, -1)][::-1]
 
     exchanges = [[(c, i) for i in range(3)] for c in range(chunks)]
     for c in range(chunks):
         exchanges[min(c + 1, chunks - 1)].append((c, 3))
     arrays = (queries, keys, values, out_grad)
-    width = plan.near * hd
+    width = near * hd
     received, where = [], {}
+    token = ()
     for pieces in exchanges:
-        packed = kernel_call(
-            partial(pack_body, plan),
-            sds((plan.near, len(pieces) * hd, plan.tok), BF16),
-            [pl.BlockSpec((plan.tok, width), lambda i, c=c: (0, c)) for c, _ in pieces],
+        slotted = len(received) > 0
+        block = (len(pieces) * hd, tok_rows)
+        *packed, tok = kernel_call(
+            partial(pack_body, plan, [c for c, _ in pieces], near if slotted else 1),
+            ([sds(block, BF16)] * near if slotted else [sds((near,) + block, BF16)]) + [TOKEN],
+            [ANY] * (len(pieces) + len(token)),
+            [
+                pltpu.VMEM((len(pieces), tok_rows, width), BF16),
+                pltpu.VMEM((width, tok_rows), BF16),
+                pltpu.SemaphoreType.DMA((len(pieces),)),
+            ],
             name="pack",
-            grid=(1,),
-            out_specs=pl.BlockSpec((plan.near, len(pieces) * hd, plan.tok), lambda i: (0, 0, 0)),
-        )(*(arrays[i] for _, i in pieces))
+            limit=PACK_LIMIT,
+        )(*(arrays[i] for _, i in pieces), *token)
+        token = (tok,)
         for place, piece in enumerate(pieces):
             where[piece] = (len(received), place * hd)
-        received.append(swap(packed))
+        received.append(traded(packed) if slotted else [swap(packed[0])])
 
     n, n3, n2 = plan.rows, plan.all_rows, plan.last
     pair_flops = 20 * 2 * 128 * SEG0 * SEG0
     scalars = (slide_lengths, head_offsets)
-    token = jnp.zeros(TOKEN.shape, TOKEN.dtype)
+    (token,) = token
     fronts = []
     for chunk in range(chunks):
         source, first = where[chunk, 0]
         acc, q2, kv2, token = kernel_call(
-            partial(forward_body, plan, chunk, first),
+            partial(forward_body, plan, chunk, first, len(received[source])),
             [sds((64, n), F32), sds((hd, n2), BF16), sds((2 * hd, n2), BF16), TOKEN],
-            [VMEM, SMEM, SMEM, ANY],
+            [SMEM, SMEM, ANY] + [VMEM] * len(received[source]),
             [
                 pltpu.VMEM((n3, 128), BF16),
                 pltpu.VMEM((128, n3), BF16),
@@ -483,15 +544,14 @@
                 pltpu.VMEM((3 * hd, n), BF16),
                 pltpu.VMEM((64, n3), F32),
             ],
-            flops=len(plan.tiles) * 2 * pair_flops,
             name=f"forward{chunk}",
-        )(received[source], *scalars, token)
+        )(*scalars, token, *received[source])
         fronts.append((acc, q2, kv2, *(shifted(kv2, s) for s in range(1, plan.far))))
     states = []
     for chunk, front in enumerate(fronts):
         source, first = where[chunk, 3]
         att, ld, grad2, far2, token = kernel_call(
-            partial(last_body, plan, chunk, first),
+            partial(last_body, plan, chunk, first, len(received[source])),
             [
                 sds((hd, n), BF16),
                 sds((8, n), F32),
@@ -499,20 +559,26 @@
                 sds((max(plan.far - 1, 1), 2 * hd, n2), BF16),
                 TOKEN,
             ],
-            [VMEM, SMEM, SMEM, ANY] + [VMEM] * len(front),
+            [SMEM, SMEM, ANY] + [VMEM] * (len(front) + len(received[source])),
             [pltpu.VMEM((64, n), F32), pltpu.VMEM((hd, n), BF16)],
             flops=4 * pair_flops,
             name=f"last{chunk}",
-        )(received[source], *scalars, token, *front)
+        )(*scalars, token, *front[:3], *received[source], *front[3:])
         states.append((att, (ld, grad2, *(shifted(far2[s - 1], -s) for s in range(1, plan.far)))))
+    full = sds((tok_rows, model_width), BF16)
     for chunk, (_, state) in enumerate(states):
         atts = [s[0] for s in states] if chunk == 0 else []
+        slotted = chunk == chunks - 1
         count = len(atts) + 3
         sources = [where[chunk, 0], where[chunk, 3]]
-        out, token = kernel_call(
-            partial(backward_body, plan, chunk, [first for _, first in sources], len(atts)),
-            [sds((plan.near, count * hd, plan.tok), BF16), TOKEN],
-            [VMEM, VMEM, SMEM, SMEM, ANY] + [VMEM] * (len(atts) + len(state)),
+        blocks = [len(received[x[0]]) for x in sources]
+        block = sds((count * hd, tok_rows), BF16)
+        *out, token = kernel_call(
+            partial(
+                backward_body, plan, chunk, [x[1] for x in sources], blocks, len(atts), slotted
+            ),
+            ([block] * near if slotted else [sds((near,) + block.shape, BF16)]) + [TOKEN],
+            [SMEM, SMEM, ANY] + [VMEM] * (sum(blocks) + len(atts) + len(state)),
             [
                 pltpu.VMEM((n3, 128), BF16),
                 pltpu.VMEM((128, n3), BF16),
@@ -524,30 +590,32 @@
             ],
             flops=len(plan.tiles) * 5 * pair_flops,
             name=f"backward{chunk}",
-        )(*(received[source] for source, _ in sources), *scalars, token, *atts, *state)
-        y = swap(out)
-        full = sds((tok_rows, model_width), BF16)
-        whole = pl.BlockSpec(out.shape, lambda i: (0, 0, 0))
+        )(*scalars, token, *received[sources[0][0]], *received[sources[1][0]], *atts, *state)
+        y = traded(out) if slotted else [swap(out[0])]
+        scratch = [pltpu.VMEM((near,) + block.shape, BF16)] if slotted else []
         column = pl.BlockSpec((tok_rows, width), lambda i, c=chunk: (0, c))
+        specs = [pl.BlockSpec(v.shape, lambda i, r=len(v.shape): (0,) * r) for v in y]
         if chunk == 0:
             attended, *outs = kernel_call(
-                partial(unpack_body, plan, [0] + [chunks + i for i in range(3)]),
+                partial(unpack_body, plan, [0] + [chunks + i for i in range(3)], slotted),
                 [full] * 4,
-                [whole],
+                specs,
+                scratch,
                 name="unpack",
                 grid=(1,),
                 out_specs=[pl.BlockSpec(full.shape, lambda i: (0, 0))] + [column] * 3,
-            )(y)
+            )(*y)
         else:
             outs = kernel_call(
-                partial(unpack_body, plan, list(range(3))),
+                partial(unpack_body, plan, list(range(3)), slotted),
                 [full] * 3,
-                [whole] + [ANY] * 3,
+                specs + [ANY] * 3,
+                scratch,
                 name="unpack",
                 grid=(1,),
                 out_specs=[column] * 3,
-                input_output_aliases={1: 0, 2: 1, 3: 2},
-            )(y, *outs)
+                input_output_aliases={len(y) + i: i for i in range(3)},
+            )(*y, *outs)
     return (attended, *outs)
 
 

time: 99.2 us -> 87.6 us (0.88)
  waiting for transfers between devices: 28.1 us -> 9.99 us
  starting transfers between devices: 22 us -> 29.2 us
  local copies, waits for them, and re-layouts: 3.66 us -> 0.23 us
  Pallas kernels: 44.2 us -> 47.2 us
    all_to_all x4 -> x2, waiting for transfers between devices: 25.9 us -> 0.01 us  [swap(): return lax.all_to_all(x, 'seq', 0, 0, tiled=True, axis_index_groups=groups)]
    ppermute x4 -> x18, starting transfers between devices: 5.78 us -> 19.9 us  [permuted(): return lax.ppermute(x, 'seq', [(i, target(i)) for i in range(device_count)])]
    ppermute x4 -> x18, waiting for transfers between devices: 2.18 us -> 9.98 us  [permuted(): return lax.ppermute(x, 'seq', [(i, target(i)) for i in range(device_count)])]
    all_to_all x4 -> x2, starting transfers between devices: 16.2 us -> 9.34 us  [swap(): return lax.all_to_all(x, 'seq', 0, 0, tiled=True, axis_index_groups=groups)]
    unnamed x18 -> x8, local copies, waits for them, and re-layouts: 3.66 us -> 0.23 us
    pallas_call x9, Pallas kernels: 42.9 us -> 45.9 us  [the longest x2 20.8 us: body(): kernel_call(partial(backward_body, plan, chunk, [x[1] for x in sources],...]
  transfers between devices with their start and end apart: 8 -> 20, of which waited for: 6 -> 5; matrix products, arithmetic and copies ran while one was open for 0% -> 0% of each run, Pallas kernels for 43% -> 50%
where the time goes in v2:
time: 87.6 us; the launch traced here: 87.4 us
  Pallas kernels  47.2 us (54%)
  starting transfers between devices  29.2 us (33%)
  waiting for transfers between devices  9.99 us (11%)
    pallas_call x2, Pallas kernels, body(): kernel_call(partial(backward_body, plan, chunk, [x[1] for x in sources],...  20.8 us
    ppermute x18, starting transfers between devices, permuted(): return lax.ppermute(x, 'seq', [(i, target(i)) for i in range(device_count)])  19.9 us
    pallas_call x2, Pallas kernels, body(): kernel_call(partial(forward_body, plan, chunk, first, len(received[source...  11.6 us
    ppermute x18, waiting for transfers between devices, permuted(): return lax.ppermute(x, 'seq', [(i, target(i)) for i in range(device_count)])  9.98 us
    all_to_all x2, starting transfers between devices, swap(): return lax.all_to_all(x, 'seq', 0, 0, tiled=True, axis_index_groups=groups)  9.34 us
    pallas_call x2, Pallas kernels, body(): kernel_call(partial(last_body, plan, chunk, first, len(received[source]))...  6.39 us
    pallas_call x2, Pallas kernels, body(): kernel_call(partial(pack_body, plan, [c for c, _ in pieces], near if slot...  5.94 us
  transfers between devices with their start and end apart: 20, of which 5 were waited for; matrix products, arithmetic and copies ran while one was open for 0% of the time, Pallas kernels for 50%

profile of v2, /device:TPU:0, one launch (start us, length us, event | category | flops | bytes accessed | tf_op | source)
XLA Modules:
  0.0 87.4 jit_solution(3172608986026150383)
XLA Ops:
  0.6 2.6 %pack.2 = (bf16[8,144,256]{2,1,0:T(8,128)(2,1)}, f32[8,128]{1,0:T(8,128)}) custom-call(bf16[256,768]{1,0:T(8,128)(2,1)} %refs_0_.3, bf16[256,768]{1,0:T(8,128)(2,1)} %refs_1_.3, bf16[256,768]{1,0:T(8,128)(2,1)} %refs_2_.3), custom_call_target="tpu_custom_call" | custom-call | bytes 1048576 | tf_op jit(solution)/shard_map/pack/pallas_call | solution.py:512
  3.2 5.2 %all-to-all-start = ((bf16[8,144,256]{2,1,0:T(8,128)(2,1)}), bf16[8,144,256]{2,1,0:T(8,128)(2,1)S(1)}, u32[]{:S(2)}, u32[]{:S(2)}) async-start(bf16[8,144,256]{2,1,0:T(8,128)(2,1)} %get-tuple-element.52), calls=%async_computation | async-start | bytes 1179648 | tf_op jit(solution)/shard_map/all_to_all | solution.py:494
  8.5 3.4 %pack.3 = (bf16[240,256]{1,0:T(8,128)(2,1)}, bf16[240,256]{1,0:T(8,128)(2,1)}, bf16[240,256]{1,0:T(8,128)(2,1)}, bf16[240,256]{1,0:T(8,128)(2,1)}, bf16[240,256]...) custom-call(bf16[256,768]{1,0:T(8,128)(2,1)} %refs_0_.3, ...), custom_call_target="tpu_custom_call" | custom-call | bytes 1048576 | tf_op jit(solution)/shard_map/pack/pallas_call | solution.py:512
  11.8 0.6 collective-permute-start
  12.4 1.7 %collective-permute-start.1 = (bf16[240,256]{1,0:T(8,128)(2,1)}, bf16[240,256]{1,0:T(8,128)(2,1)S(1)}, u32[]{:S(2)}, u32[]{:S(2)}) collective-permute-start(bf16[240,256]{1,0:T(8,128)(2,1)} %get-tuple-element.56), channel_id=1, source_target_pairs={{0,2},{1,3},{2,0},{3,1},{4,6},{5,7},{6,4},{7,5},{8,10},{9,11},{10,... | collective-permute-start | bytes 368648 | tf_op jit(solution)/shard_map/ppermute | solution.py:491
  14.1 0.0 collective-permute-start.2
  14.1 1.7 %collective-permute-start.3 = (bf16[240,256]{1,0:T(8,128)(2,1)}, bf16[240,256]{1,0:T(8,128)(2,1)S(1)}, u32[]{:S(2)}, u32[]{:S(2)}) collective-permute-start(bf16[240,256]{1,0:T(8,128)(2,1)} %get-tuple-element.58), channel_id=1, source_target_pairs={{0,4},{1,5},{2,6},{3,7},{4,0},{5,1},{6,2},{7,3},{8,12},{9,13},{10,... | collective-permute-start | bytes 368648 | tf_op jit(solution)/shard_map/ppermute | solution.py:491
  15.8 0.1 collective-permute-start.4
  15.9 0.0 collective-permute-done.refs_1_.rest_1_.refs_2_.refs_9_
  15.9 2.6 %collective-permute-start.5 = (bf16[240,256]{1,0:T(8,128)(2,1)}, bf16[240,256]{1,0:T(8,128)(2,1)S(1)}, u32[]{:S(2)}, u32[]{:S(2)}) collective-permute-start(bf16[240,256]{1,0:T(8,128)(2,1)} %get-tuple-element.60), channel_id=1, source_target_pairs={{0,6},{1,7},{2,4},{3,5},{4,2},{5,3},{6,0},{7,1},{8,14},{9,15},{10,... | collective-permute-start | bytes 368648 | tf_op jit(solution)/shard_map/ppermute | solution.py:491
  18.5 2.6 %collective-permute-done.1.refs_2_.rest_2_.refs_3_.refs_10_ = bf16[240,256]{1,0:T(8,128)(2,1)S(1)} collective-permute-done((bf16[240,256]{1,0:T(8,128)(2,1)}, bf16[240,256]{1,0:T(8,128)(2,1)S(1)}, u32[]{:S(2)}, u32[]{:S(2)}) %collective-permute-start.1) | collective-permute-done | bytes 122912 | tf_op jit(solution)/shard_map/ppermute | solution.py:491
  21.1 0.4 collective-permute-start.6
  21.5 0.0 all-to-all-done.refs_0_
  21.6 0.2 copy-done.3
  21.8 5.8 %forward0.1 = (f32[64,2048]{1,0:T(8,128)S(1)}, bf16[48,512]{1,0:T(8,128)(2,1)S(1)}, bf16[96,512]{1,0:T(8,128)(2,1)S(1)}, f32[8,128]{1,0:T(8,128)S(1)}) custom-call(s32[8]{0:T(128)S(1)} %copy-done.3, s32[3,16]{1,0:T(4,128)S(1)} %copy-done.1, f32[8,128]{1,0:T(8,128)S(1)} %copy-done.2, bf16[8,144,256]{2,1,0:T(8,128)(2,1)S(1)} %all-to-all-done.refs_0_), custom_call_target="tpu_custom_call" | custom-call | bytes 1048576 | tf_op jit(solution)/shard_map/forward0/pallas_call | solution.py:536
  27.6 0.0 collective-permute-done.2.refs_3_.rest_3_.refs_4_.refs_11_
  27.6 2.7 %collective-permute-start.7 = (bf16[96,512]{1,0:T(8,128)(2,1)S(1)}, bf16[96,512]{1,0:T(8,128)(2,1)S(1)}, u32[]{:S(2)}, u32[]{:S(2)}) collective-permute-start(bf16[96,512]{1,0:T(8,128)(2,1)S(1)} %get-tuple-element.65.kv2), channel_id=1, source_target_pairs={{0,8},{1,9},{2,10},{3,11},{4,12},{5,13},{6,14},{7,15},{8,0},{9,1},... | collective-permute-start | bytes 294920 | tf_op jit(solution)/shard_map/ppermute | solution.py:491
  30.3 0.0 collective-permute-done.3.refs_4_.rest_4_.refs_5_.refs_12_
  30.3 0.0 collective-permute-done.4.refs_5_.rest_5_.refs_6_.refs_13_
  30.3 0.0 collective-permute-done.5.refs_6_.rest_6_.refs_7_.refs_14_
  30.3 0.0 collective-permute-done.6.refs_7_.rest_7_.refs_8_.refs_15_
  30.3 5.8 %forward1.1 = (f32[64,2048]{1,0:T(8,128)S(1)}, bf16[48,512]{1,0:T(8,128)(2,1)S(1)}, bf16[96,512]{1,0:T(8,128)(2,1)S(1)}, f32[8,128]{1,0:T(8,128)S(1)}) custom-call(s32[8]{0:T(128)S(1)} %copy-done.3, s32[3,16]{1,0:T(4,128)S(1)} %copy-done.1, f32[8,128]{1,0:T(8,128)S(1)} %get-tuple-element.53.tok_in, bf16[240,256]{1,0:T(8,128)(2,1)S(1)} %copy-done, ...), custom_call_target="tpu_custom_call" | custom-call | bytes 1048576 | tf_op jit(solution)/shard_map/forward1/pallas_call | solution.py:536
  36.1 1.4 %collective-permute-start.8 = (bf16[96,512]{1,0:T(8,128)(2,1)S(1)}, bf16[96,512]{1,0:T(8,128)(2,1)S(1)}, u32[]{:S(2)}, u32[]{:S(2)}) collective-permute-start(bf16[96,512]{1,0:T(8,128)(2,1)S(1)} %get-tuple-element.69.kv2), channel_id=1, source_target_pairs={{0,8},{1,9},{2,10},{3,11},{4,12},{5,13},{6,14},{7,15},{8,0},{9,1},... | collective-permute-start | bytes 294920 | tf_op jit(solution)/shard_map/ppermute | solution.py:491
  37.6 0.0 collective-permute-done.7.rest_8_
  37.6 3.2 %last0.1 = (bf16[48,2048]{1,0:T(8,128)(2,1)S(1)}, f32[8,2048]{1,0:T(8,128)S(1)}, f32[144,512]{1,0:T(8,128)S(1)}, bf16[1,96,512]{2,1,0:T(8,128)(2,1)S(1)}, f32[8,128]{1,0:T(8,128)S(1)}) custom-call(s32[8]{0:T(128)S(1)} %copy-done.3, s32[3,16]{1,0:T(4,128)S(1)} %copy-done.1, f32[8,128]{1,0:T(8,128)S(1)} %get-tuple-element.62.tok_in, ...), custom_call_target="tpu_custom_call" | custom-call | flops 21474836480 | bytes 1048576 | tf_op jit(solution)/shard_map/last0/pallas_call | solution.py:553
  40.8 1.6 %collective-permute-start.9 = (bf16[96,512]{1,0:T(8,128)(2,1)S(1)}, bf16[96,512]{1,0:T(8,128)(2,1)S(1)}, u32[]{:S(2)}, u32[]{:S(2)}) collective-permute-start(bf16[96,512]{1,0:T(8,128)(2,1)S(1)} %bitcast.2), channel_id=1, source_target_pairs={{0,8},{1,9},{2,10},{3,11},{4,12},{5,13},{6,14},{7,15},{8,0},{9,1},... | collective-permute-start | bytes 294920 | tf_op jit(solution)/shard_map/ppermute | solution.py:491
  42.4 1.7 %collective-permute-done.8.rest_8_ = bf16[96,512]{1,0:T(8,128)(2,1)S(1)} collective-permute-done((bf16[96,512]{1,0:T(8,128)(2,1)S(1)}, bf16[96,512]{1,0:T(8,128)(2,1)S(1)}, u32[]{:S(2)}, u32[]{:S(2)}) %collective-permute-start.8) | collective-permute-done | bytes 98336 | tf_op jit(solution)/shard_map/ppermute | solution.py:491
  44.1 3.2 %last1.1 = (bf16[48,2048]{1,0:T(8,128)(2,1)S(1)}, f32[8,2048]{1,0:T(8,128)S(1)}, f32[144,512]{1,0:T(8,128)S(1)}, bf16[1,96,512]{2,1,0:T(8,128)(2,1)S(1)}, f32[8,128]{1,0:T(8,128)S(1)}) custom-call(s32[8]{0:T(128)S(1)} %copy-done.3, s32[3,16]{1,0:T(4,128)S(1)} %copy-done.1, f32[8,128]{1,0:T(8,128)S(1)} %get-tuple-element.66.tok_in, ...), custom_call_target="tpu_custom_call" | custom-call | flops 21474836480 | bytes 1048576 | tf_op jit(solution)/shard_map/last1/pallas_call | solution.py:553
  47.3 0.1 collective-permute-start.10
  47.3 1.1 %collective-permute-done.9.refs_13_ = bf16[96,512]{1,0:T(8,128)(2,1)S(1)} collective-permute-done((bf16[96,512]{1,0:T(8,128)(2,1)S(1)}, bf16[96,512]{1,0:T(8,128)(2,1)S(1)}, u32[]{:S(2)}, u32[]{:S(2)}) %collective-permute-start.9) | collective-permute-done | bytes 98336 | tf_op jit(solution)/shard_map/ppermute | solution.py:491
  48.4 10.9 %backward0.1 = (bf16[8,240,256]{2,1,0:T(8,128)(2,1)}, f32[8,128]{1,0:T(8,128)S(1)}) custom-call(s32[8]{0:T(128)S(1)} %copy-done.3, s32[3,16]{1,0:T(4,128)S(1)} %copy-done.1, f32[8,128]{1,0:T(8,128)S(1)} %get-tuple-element.70.tok_in, bf16[8,144,256]{2,1,0:T(8,128)(2,1)S(1)} %all-to-all-done.refs_0_, bf16[240,256]{1,0:T(8,128)(2,1)S(1)} %copy-done, ...), custom_call_target="tpu_custom_call" | custom-call | flops 80530636800 | bytes 1048576 | tf_op jit(solution)/shard_map/backward0/pallas_call | solution.py:576
  59.4 4.1 %all-to-all-start.1 = ((bf16[8,240,256]{2,1,0:T(8,128)(2,1)}), bf16[8,240,256]{2,1,0:T(8,128)(2,1)S(1)}, u32[]{:S(2)}, u32[]{:S(2)}) async-start(bf16[8,240,256]{2,1,0:T(8,128)(2,1)} %get-tuple-element.76), calls=%async_computation.1 | async-start | bytes 1966080 | tf_op jit(solution)/shard_map/all_to_all | solution.py:494
  63.5 0.0 collective-permute-done.10.refs_18_
  63.5 9.9 %backward1.1 = (bf16[144,256]{1,0:T(8,128)(2,1)S(1)}, bf16[144,256]{1,0:T(8,128)(2,1)S(1)}, bf16[144,256]{1,0:T(8,128)(2,1)S(1)}, bf16[144,256]{1,0:T(8,128)(2,1...) custom-call(s32[8]{0:T(128)S(1)} %copy-done.3, ...), custom_call_target="tpu_custom_call" | custom-call | flops 80530636800 | bytes 1048576 | tf_op jit(solution)/shard_map/backward1/pallas_call | solution.py:576
  73.3 0.4 collective-permute-start.11
  73.8 2.2 %collective-permute-start.12 = (bf16[144,256]{1,0:T(8,128)(2,1)S(1)}, bf16[144,256]{1,0:T(8,128)(2,1)S(1)}, u32[]{:S(2)}, u32[]{:S(2)}) collective-permute-start(bf16[144,256]{1,0:T(8,128)(2,1)S(1)} %get-tuple-element.84), channel_id=1, source_target_pairs={{0,2},{1,3},{2,0},{3,1},{4,6},{5,7},{6,4},{7,5},{8,10},{9,11},{10,... | collective-permute-start | bytes 221192 | tf_op jit(solution)/shard_map/ppermute | solution.py:491
  76.0 0.0 collective-permute-start.13
  76.0 1.1 %collective-permute-start.14 = (bf16[144,256]{1,0:T(8,128)(2,1)S(1)}, bf16[144,256]{1,0:T(8,128)(2,1)S(1)}, u32[]{:S(2)}, u32[]{:S(2)}) collective-permute-start(bf16[144,256]{1,0:T(8,128)(2,1)S(1)} %get-tuple-element.86), channel_id=1, source_target_pairs={{0,4},{1,5},{2,6},{3,7},{4,0},{5,1},{6,2},{7,3},{8,12},{9,13},{10,... | collective-permute-start | bytes 221192 | tf_op jit(solution)/shard_map/ppermute | solution.py:491
  77.1 0.4 collective-permute-start.15
  77.5 0.0 collective-permute-done.11.refs_1_
  77.5 2.4 %collective-permute-start.16 = (bf16[144,256]{1,0:T(8,128)(2,1)S(1)}, bf16[144,256]{1,0:T(8,128)(2,1)S(1)}, u32[]{:S(2)}, u32[]{:S(2)}) collective-permute-start(bf16[144,256]{1,0:T(8,128)(2,1)S(1)} %get-tuple-element.88), channel_id=1, source_target_pairs={{0,6},{1,7},{2,4},{3,5},{4,2},{5,3},{6,0},{7,1},{8,14},{9,15},{10,... | collective-permute-start | bytes 221192 | tf_op jit(solution)/shard_map/ppermute | solution.py:491
  79.9 0.0 collective-permute-done.12.refs_2_
  79.9 0.5 collective-permute-start.17
  80.4 0.0 all-to-all-done.1.refs_0_
  80.4 1.3 %unpack.2 = (bf16[256,768]{1,0:T(8,128)(2,1)}, bf16[256,768]{1,0:T(8,128)(2,1)}, bf16[256,768]{1,0:T(8,128)(2,1)}, bf16[256,768]{1,0:T(8,128)(2,1)}) custom-call(bf16[8,240,256]{2,1,0:T(8,128)(2,1)S(1)} %all-to-all-done.1.refs_0_), custom_call_target="tpu_custom_call" | custom-call | bytes 1048576 | tf_op jit(solution)/shard_map/unpack/pallas_call | solution.py:599
  81.6 3.5 %collective-permute-done.16.refs_6_ = bf16[144,256]{1,0:T(8,128)(2,1)S(1)} collective-permute-done((bf16[144,256]{1,0:T(8,128)(2,1)S(1)}, bf16[144,256]{1,0:T(8,128)(2,1)S(1)}, u32[]{:S(2)}, u32[]{:S(2)}) %collective-permute-start.16) | collective-permute-done | bytes 73760 | tf_op jit(solution)/shard_map/ppermute | solution.py:491
  85.1 1.1 %collective-permute-done.17.refs_7_ = bf16[144,256]{1,0:T(8,128)(2,1)S(1)} collective-permute-done((bf16[144,256]{1,0:T(8,128)(2,1)S(1)}, bf16[144,256]{1,0:T(8,128)(2,1)S(1)}, u32[]{:S(2)}, u32[]{:S(2)}) %collective-permute-start.17) | collective-permute-done | bytes 73760 | tf_op jit(solution)/shard_map/ppermute | solution.py:491
  86.2 1.1 %unpack.3 = (bf16[256,768]{1,0:T(8,128)(2,1)}, bf16[256,768]{1,0:T(8,128)(2,1)}, bf16[256,768]{1,0:T(8,128)(2,1)}) custom-call(bf16[144,256]{1,0:T(8,128)(2,1)S(1)} %get-tuple-element.82.refs_0_, bf16[144,256]{1,0:T(8,128)(2,1)S(1)} %collective-permute-done.11.refs_1_, ...), custom_call_target="tpu_custom_call", output_to_operand_aliasing={{0}: (8, {}), {1}: (9, {}), {2}: (10, {})} | custom-call | bytes 1048576 | tf_op jit(solution)/shard_map/unpack/pallas_call | solution.py:609
  (10 shorter events, 0.0 us)
Async XLA Ops:
  3.2 18.3 %all-to-all-start = ((bf16[8,144,256]{2,1,0:T(8,128)(2,1)}), bf16[8,144,256]{2,1,0:T(8,128)(2,1)S(1)}, u32[]{:S(2)}, u32[]{:S(2)}) async-start(bf16[8,144,256]{2,1,0:T(8,128)(2,1)} %get-tuple-element.52), calls=%async_computation | async-start | bytes 1179648 | tf_op jit(solution)/shard_map/all_to_all | solution.py:494
  11.8 4.1 %collective-permute-start = (bf16[240,256]{1,0:T(8,128)(2,1)}, bf16[240,256]{1,0:T(8,128)(2,1)S(1)}, u32[]{:S(2)}, u32[]{:S(2)}) collective-permute-start(bf16[240,256]{1,0:T(8,128)(2,1)} %get-tuple-element.55), channel_id=1, source_target_pairs={{0,1},{1,0},{2,3},{3,2},{4,5},{5,4},{6,7},{7,6},{8,9},{9,8},{10,11... | collective-permute-start | bytes 368648 | tf_op jit(solution)/shard_map/ppermute | solution.py:491
  12.4 8.7 %collective-permute-start.1 = (bf16[240,256]{1,0:T(8,128)(2,1)}, bf16[240,256]{1,0:T(8,128)(2,1)S(1)}, u32[]{:S(2)}, u32[]{:S(2)}) collective-permute-start(bf16[240,256]{1,0:T(8,128)(2,1)} %get-tuple-element.56), channel_id=1, source_target_pairs={{0,2},{1,3},{2,0},{3,1},{4,6},{5,7},{6,4},{7,5},{8,10},{9,11},{10,... | collective-permute-start | bytes 368648 | tf_op jit(solution)/shard_map/ppermute | solution.py:491
  14.1 13.5 %collective-permute-start.2 = (bf16[240,256]{1,0:T(8,128)(2,1)}, bf16[240,256]{1,0:T(8,128)(2,1)S(1)}, u32[]{:S(2)}, u32[]{:S(2)}) collective-permute-start(bf16[240,256]{1,0:T(8,128)(2,1)} %get-tuple-element.57), channel_id=1, source_target_pairs={{0,3},{1,2},{2,1},{3,0},{4,7},{5,6},{6,5},{7,4},{8,11},{9,10},{10,... | collective-permute-start | bytes 368648 | tf_op jit(solution)/shard_map/ppermute | solution.py:491
  14.1 7.5 %copy-start.2 = (f32[8,128]{1,0:T(8,128)S(1)}, f32[8,128]{1,0:T(8,128)}, u32[]{:S(2)}) copy-start(f32[8,128]{1,0:T(8,128)} %get-tuple-element.51.tok_in) | copy-start | bytes 12292
  14.1 16.2 %collective-permute-start.3 = (bf16[240,256]{1,0:T(8,128)(2,1)}, bf16[240,256]{1,0:T(8,128)(2,1)S(1)}, u32[]{:S(2)}, u32[]{:S(2)}) collective-permute-start(bf16[240,256]{1,0:T(8,128)(2,1)} %get-tuple-element.58), channel_id=1, source_target_pairs={{0,4},{1,5},{2,6},{3,7},{4,0},{5,1},{6,2},{7,3},{8,12},{9,13},{10,... | collective-permute-start | bytes 368648 | tf_op jit(solution)/shard_map/ppermute | solution.py:491
  15.8 14.5 %collective-permute-start.4 = (bf16[240,256]{1,0:T(8,128)(2,1)}, bf16[240,256]{1,0:T(8,128)(2,1)S(1)}, u32[]{:S(2)}, u32[]{:S(2)}) collective-permute-start(bf16[240,256]{1,0:T(8,128)(2,1)} %get-tuple-element.59), channel_id=1, source_target_pairs={{0,5},{1,4},{2,7},{3,6},{4,1},{5,0},{6,3},{7,2},{8,13},{9,12},{10,... | collective-permute-start | bytes 368648 | tf_op jit(solution)/shard_map/ppermute | solution.py:491
  15.9 5.7 %copy-start.1 = (s32[3,16]{1,0:T(4,128)S(1)}, s32[3,16]{1,0:T(4,128)}, u32[]{:S(2)}) copy-start(s32[3,16]{1,0:T(4,128)} %off_ref.11) | copy-start | bytes 580
  15.9 14.4 %collective-permute-start.5 = (bf16[240,256]{1,0:T(8,128)(2,1)}, bf16[240,256]{1,0:T(8,128)(2,1)S(1)}, u32[]{:S(2)}, u32[]{:S(2)}) collective-permute-start(bf16[240,256]{1,0:T(8,128)(2,1)} %get-tuple-element.60), channel_id=1, source_target_pairs={{0,6},{1,7},{2,4},{3,5},{4,2},{5,3},{6,0},{7,1},{8,14},{9,15},{10,... | collective-permute-start | bytes 368648 | tf_op jit(solution)/shard_map/ppermute | solution.py:491
  21.1 0.7 copy-start.3
  21.1 9.2 %collective-permute-start.6 = (bf16[240,256]{1,0:T(8,128)(2,1)}, bf16[240,256]{1,0:T(8,128)(2,1)S(1)}, u32[]{:S(2)}, u32[]{:S(2)}) collective-permute-start(bf16[240,256]{1,0:T(8,128)(2,1)} %get-tuple-element.61), channel_id=1, source_target_pairs={{0,7},{1,6},{2,5},{3,4},{4,3},{5,2},{6,1},{7,0},{8,15},{9,14},{10,... | collective-permute-start | bytes 368648 | tf_op jit(solution)/shard_map/ppermute | solution.py:491
  21.8 8.5 %copy-start = (bf16[240,256]{1,0:T(8,128)(2,1)S(1)}, bf16[240,256]{1,0:T(8,128)(2,1)}, u32[]{:S(2)}) copy-start(bf16[240,256]{1,0:T(8,128)(2,1)} %get-tuple-element.54.refs_0_.rest_0_.refs_1_.refs_8_) | copy-start | bytes 368644
  27.6 10.0 %collective-permute-start.7 = (bf16[96,512]{1,0:T(8,128)(2,1)S(1)}, bf16[96,512]{1,0:T(8,128)(2,1)S(1)}, u32[]{:S(2)}, u32[]{:S(2)}) collective-permute-start(bf16[96,512]{1,0:T(8,128)(2,1)S(1)} %get-tuple-element.65.kv2), channel_id=1, source_target_pairs={{0,8},{1,9},{2,10},{3,11},{4,12},{5,13},{6,14},{7,15},{8,0},{9,1},... | collective-permute-start | bytes 294920 | tf_op jit(solution)/shard_map/ppermute | solution.py:491
  36.1 7.9 %collective-permute-start.8 = (bf16[96,512]{1,0:T(8,128)(2,1)S(1)}, bf16[96,512]{1,0:T(8,128)(2,1)S(1)}, u32[]{:S(2)}, u32[]{:S(2)}) collective-permute-start(bf16[96,512]{1,0:T(8,128)(2,1)S(1)} %get-tuple-element.69.kv2), channel_id=1, source_target_pairs={{0,8},{1,9},{2,10},{3,11},{4,12},{5,13},{6,14},{7,15},{8,0},{9,1},... | collective-permute-start | bytes 294920 | tf_op jit(solution)/shard_map/ppermute | solution.py:491
  40.8 7.7 %collective-permute-start.9 = (bf16[96,512]{1,0:T(8,128)(2,1)S(1)}, bf16[96,512]{1,0:T(8,128)(2,1)S(1)}, u32[]{:S(2)}, u32[]{:S(2)}) collective-permute-start(bf16[96,512]{1,0:T(8,128)(2,1)S(1)} %bitcast.2), channel_id=1, source_target_pairs={{0,8},{1,9},{2,10},{3,11},{4,12},{5,13},{6,14},{7,15},{8,0},{9,1},... | collective-permute-start | bytes 294920 | tf_op jit(solution)/shard_map/ppermute | solution.py:491
  47.3 16.2 %collective-permute-start.10 = (bf16[96,512]{1,0:T(8,128)(2,1)S(1)}, bf16[96,512]{1,0:T(8,128)(2,1)S(1)}, u32[]{:S(2)}, u32[]{:S(2)}) collective-permute-start(bf16[96,512]{1,0:T(8,128)(2,1)S(1)} %bitcast.3), channel_id=1, source_target_pairs={{0,8},{1,9},{2,10},{3,11},{4,12},{5,13},{6,14},{7,15},{8,0},{9,1},... | collective-permute-start | bytes 294920 | tf_op jit(solution)/shard_map/ppermute | solution.py:491
  59.4 21.0 %all-to-all-start.1 = ((bf16[8,240,256]{2,1,0:T(8,128)(2,1)}), bf16[8,240,256]{2,1,0:T(8,128)(2,1)S(1)}, u32[]{:S(2)}, u32[]{:S(2)}) async-start(bf16[8,240,256]{2,1,0:T(8,128)(2,1)} %get-tuple-element.76), calls=%async_computation.1 | async-start | bytes 1966080 | tf_op jit(solution)/shard_map/all_to_all | solution.py:494
  73.3 4.1 %collective-permute-start.11 = (bf16[144,256]{1,0:T(8,128)(2,1)S(1)}, bf16[144,256]{1,0:T(8,128)(2,1)S(1)}, u32[]{:S(2)}, u32[]{:S(2)}) collective-permute-start(bf16[144,256]{1,0:T(8,128)(2,1)S(1)} %get-tuple-element.83), channel_id=1, source_target_pairs={{0,1},{1,0},{2,3},{3,2},{4,5},{5,4},{6,7},{7,6},{8,9},{9,8},{10,11... | collective-permute-start | bytes 221192 | tf_op jit(solution)/shard_map/ppermute | solution.py:491
  73.8 6.1 %collective-permute-start.12 = (bf16[144,256]{1,0:T(8,128)(2,1)S(1)}, bf16[144,256]{1,0:T(8,128)(2,1)S(1)}, u32[]{:S(2)}, u32[]{:S(2)}) collective-permute-start(bf16[144,256]{1,0:T(8,128)(2,1)S(1)} %get-tuple-element.84), channel_id=1, source_target_pairs={{0,2},{1,3},{2,0},{3,1},{4,6},{5,7},{6,4},{7,5},{8,10},{9,11},{10,... | collective-permute-start | bytes 221192 | tf_op jit(solution)/shard_map/ppermute | solution.py:491
  76.0 5.7 %collective-permute-start.13 = (bf16[144,256]{1,0:T(8,128)(2,1)S(1)}, bf16[144,256]{1,0:T(8,128)(2,1)S(1)}, u32[]{:S(2)}, u32[]{:S(2)}) collective-permute-start(bf16[144,256]{1,0:T(8,128)(2,1)S(1)} %get-tuple-element.85), channel_id=1, source_target_pairs={{0,3},{1,2},{2,1},{3,0},{4,7},{5,6},{6,5},{7,4},{8,11},{9,10},{10,... | collective-permute-start | bytes 221192 | tf_op jit(solution)/shard_map/ppermute | solution.py:491
  76.0 5.7 %collective-permute-start.14 = (bf16[144,256]{1,0:T(8,128)(2,1)S(1)}, bf16[144,256]{1,0:T(8,128)(2,1)S(1)}, u32[]{:S(2)}, u32[]{:S(2)}) collective-permute-start(bf16[144,256]{1,0:T(8,128)(2,1)S(1)} %get-tuple-element.86), channel_id=1, source_target_pairs={{0,4},{1,5},{2,6},{3,7},{4,0},{5,1},{6,2},{7,3},{8,12},{9,13},{10,... | collective-permute-start | bytes 221192 | tf_op jit(solution)/shard_map/ppermute | solution.py:491
  77.1 4.5 %collective-permute-start.15 = (bf16[144,256]{1,0:T(8,128)(2,1)S(1)}, bf16[144,256]{1,0:T(8,128)(2,1)S(1)}, u32[]{:S(2)}, u32[]{:S(2)}) collective-permute-start(bf16[144,256]{1,0:T(8,128)(2,1)S(1)} %get-tuple-element.87), channel_id=1, source_target_pairs={{0,5},{1,4},{2,7},{3,6},{4,1},{5,0},{6,3},{7,2},{8,13},{9,12},{10,... | collective-permute-start | bytes 221192 | tf_op jit(solution)/shard_map/ppermute | solution.py:491
  77.5 7.6 %collective-permute-start.16 = (bf16[144,256]{1,0:T(8,128)(2,1)S(1)}, bf16[144,256]{1,0:T(8,128)(2,1)S(1)}, u32[]{:S(2)}, u32[]{:S(2)}) collective-permute-start(bf16[144,256]{1,0:T(8,128)(2,1)S(1)} %get-tuple-element.88), channel_id=1, source_target_pairs={{0,6},{1,7},{2,4},{3,5},{4,2},{5,3},{6,0},{7,1},{8,14},{9,15},{10,... | collective-permute-start | bytes 221192 | tf_op jit(solution)/shard_map/ppermute | solution.py:491
  79.9 6.4 %collective-permute-start.17 = (bf16[144,256]{1,0:T(8,128)(2,1)S(1)}, bf16[144,256]{1,0:T(8,128)(2,1)S(1)}, u32[]{:S(2)}, u32[]{:S(2)}) collective-permute-start(bf16[144,256]{1,0:T(8,128)(2,1)S(1)} %get-tuple-element.89), channel_id=1, source_target_pairs={{0,7},{1,6},{2,5},{3,4},{4,3},{5,2},{6,1},{7,0},{8,15},{9,14},{10,... | collective-permute-start | bytes 221192 | tf_op jit(solution)/shard_map/ppermute | solution.py:491

commit v3 on v2

--- a/solution.py
+++ b/solution.py
@@ -191,8 +191,7 @@
     return jnp.where(row == 0, a, jnp.where(row == 1, b, jnp.where(row == 2, x - a - b, 0.0)))
 
 
-def forward_tile(plan, keys, queries_t, values_t):
-    s = dot(keys, queries_t)
+def forward_tile(plan, s, values_t):
     peak = jnp.max(s, axis=0, keepdims=True)
     p = jnp.exp2(s - peak).astype(BF16)
     o = dot(values_t, p)
@@ -210,11 +209,18 @@
 
 
 def backward_tile(plan, qa, kat, ga, vat, gt, qt):
-    p = jnp.exp2(dot(qa, kat))
-    value_t = dot(gt, p.astype(BF16))
-    ds = (p * dot(ga, vat)).astype(BF16)
-    key_t = dot(qt, ds)
-    return dot(kat[: plan.hd], ds, 1, 1), key_t, value_t
+    n = qa.shape[0]
+    step = min(n, SEG0 // 2)
+    parts = [slice(i, i + step) for i in range(0, n, step)]
+    weights = []
+    for rows in parts:
+        dp = dot(ga[rows], vat)
+        p = jnp.exp2(dot(qa[rows], kat))
+        weights.append((p.astype(BF16), (p * dp).astype(BF16)))
+    query_t = [dot(kat[: plan.hd], ds, 1, 1) for _, ds in weights]
+    key_t = sum(dot(qt[:, rows], ds) for rows, (_, ds) in zip(parts, weights))
+    value_t = sum(dot(gt[:, rows], p) for rows, (p, _) in zip(parts, weights))
+    return jnp.concatenate(query_t, axis=1), key_t, value_t
 
 
 def level_start(plan, off_ref, level, chunk):
@@ -331,12 +337,10 @@
     q2[...] = last[0:hd]
     kv2[...] = last[hd:]
 
-    def step(tile, carry):
-        rows = pl.ds(pl.multiple_of(tile * SEG0, SEG0), SEG0)
-        res[:, rows] = forward_tile(plan, ka[rows, :], qat[:, rows], vat[:, rows])
-        return carry
-
-    lax.fori_loop(0, len(plan.tiles), step, 0)
+    tiles = [slice(t * SEG0, (t + 1) * SEG0) for t in range(len(plan.tiles))]
+    scores = [dot(ka[rows, :], qat[:, rows]) for rows in tiles]
+    for s, rows in zip(scores, tiles):
+        res[:, rows] = forward_tile(plan, s, vat[:, rows])
     acc_ref[...] = res[:, 0 : plan.rows]
     for tile in range(plan.segs, len(plan.tiles)):
         for src, dst in tile_pieces(plan, off_ref, chunk, tile):
@@ -365,7 +369,7 @@
     key_f = key_features(plan, x[0:hd], one_hot)
     query_f = query_features(plan, q2[...].astype(F32), one_hot[:, 0 : plan.last])
     vat2 = value_features(plan, x[hd : 2 * hd]).astype(BF16)
-    res = forward_tile(plan, key_f.T.astype(BF16), query_f.astype(BF16), vat2)
+    res = forward_tile(plan, dot(key_f.T.astype(BF16), query_f.astype(BF16)), vat2)
     last_update(plan, off_ref, chunk, acc, slice(None), res, partial(merged, plan), no_level(plan))
     for seg in range(plan.segs):
         rows = slice(seg * SEG0, (seg + 1) * SEG0)
@@ -430,19 +434,20 @@
             for ref in (kat, vat, gt, qt):
                 ref[:, dst] = ref[:, src]
 
-    def step(tile, carry):
-        rows = pl.ds(pl.multiple_of(tile * SEG0, SEG0), SEG0)
+    for tile in range(len(plan.tiles)):
+        rows = slice(tile * SEG0, (tile + 1) * SEG0)
         parts = backward_tile(
             plan, qa[rows, :], kat[:, rows], ga[rows, 0:64], vat[:, rows], gt[:, rows], qt[:, rows]
         )
-        for i, part in enumerate(parts):
-            grads[i * hd : (i + 1) * hd, rows] = part
-        return carry
-
-    lax.fori_loop(0, len(plan.tiles), step, 0)
-    for tile in range(plan.segs, len(plan.tiles)):
+        if tile < plan.segs:
+            for i, part in enumerate(parts):
+                grads[i * hd : (i + 1) * hd, rows] = part
+            continue
         for src, dst in tile_pieces(plan, off_ref, chunk, tile):
-            grads[:, src] = grads[:, src] + grads[:, dst]
+            at = slice(dst.start - rows.start, dst.stop - rows.start)
+            for i, part in enumerate(parts):
+                own = slice(i * hd, (i + 1) * hd)
+                grads[own, src] = grads[own, src] + part[:, at]
     more = grad2[...]
     if far_refs:
         far = sum(ref[...].astype(F32) for ref in far_refs)
@@ -586,7 +591,7 @@
                 pltpu.VMEM((64, n3), BF16),
                 pltpu.VMEM((hd, n3), BF16),
                 pltpu.VMEM((hd, n3), BF16),
-                pltpu.VMEM((3 * hd, n3), F32),
+                pltpu.VMEM((3 * hd, n), F32),
             ],
             flops=len(plan.tiles) * 5 * pair_flops,
             name=f"backward{chunk}",

time: 87.6 us -> 85.6 us (0.977)
  Pallas kernels: 47.2 us -> 43.6 us
  starting transfers between devices: 29.2 us -> 30.9 us
    pallas_call x2, Pallas kernels: 20.8 us -> 18.6 us  [body(): kernel_call(partial(backward_body, plan, chunk, [x[1] for x in sources],...]
    pallas_call x2, Pallas kernels: 11.6 us -> 10.1 us  [body(): kernel_call(partial(forward_body, plan, chunk, first, len(received[source...]
    all_to_all x2, starting transfers between devices: 9.34 us -> 10.6 us  [swap(): return lax.all_to_all(x, 'seq', 0, 0, tiled=True, axis_index_groups=groups)]
  transfers between devices with their start and end apart: 20 -> 20, of which waited for: 5 -> 6; matrix products, arithmetic and copies ran while one was open for 0% -> 0% of each run, Pallas kernels for 50% -> 47%
where the time goes in v3:
time: 85.6 us; the launch traced here: 85.3 us
  Pallas kernels  43.6 us (51%)
  starting transfers between devices  30.9 us (36%)
  waiting for transfers between devices  9.81 us (11%)
    ppermute x18, starting transfers between devices, permuted(): return lax.ppermute(x, 'seq', [(i, target(i)) for i in range(device_count)])  20.3 us
    pallas_call x2, Pallas kernels, body(): kernel_call(partial(backward_body, plan, chunk, [x[1] for x in sources],...  18.6 us
    all_to_all x2, starting transfers between devices, swap(): return lax.all_to_all(x, 'seq', 0, 0, tiled=True, axis_index_groups=groups)  10.6 us
    pallas_call x2, Pallas kernels, body(): kernel_call(partial(forward_body, plan, chunk, first, len(received[source...  10.1 us
    ppermute x18, waiting for transfers between devices, permuted(): return lax.ppermute(x, 'seq', [(i, target(i)) for i in range(device_count)])  9.8 us
    pallas_call x2, Pallas kernels, body(): kernel_call(partial(last_body, plan, chunk, first, len(received[source]))...  6.59 us
    pallas_call x2, Pallas kernels, body(): kernel_call(partial(pack_body, plan, [c for c, _ in pieces], near if slot...  5.94 us
  transfers between devices with their start and end apart: 20, of which 6 were waited for; matrix products, arithmetic and copies ran while one was open for 0% of the time, Pallas kernels for 47%

profile of v3, /device:TPU:0, one launch (start us, length us, event | category | flops | bytes accessed | tf_op | source)
XLA Modules:
  0.0 85.3 jit_solution(2074868349398201929)
XLA Ops:
  0.6 2.6 %pack.2 = (bf16[8,144,256]{2,1,0:T(8,128)(2,1)}, f32[8,128]{1,0:T(8,128)}) custom-call(bf16[256,768]{1,0:T(8,128)(2,1)} %refs_0_.3, bf16[256,768]{1,0:T(8,128)(2,1)} %refs_1_.3, bf16[256,768]{1,0:T(8,128)(2,1)} %refs_2_.3), custom_call_target="tpu_custom_call" | custom-call | bytes 1048576 | tf_op jit(solution)/shard_map/pack/pallas_call | solution.py:517
  3.2 5.2 %all-to-all-start = ((bf16[8,144,256]{2,1,0:T(8,128)(2,1)}), bf16[8,144,256]{2,1,0:T(8,128)(2,1)S(1)}, u32[]{:S(2)}, u32[]{:S(2)}) async-start(bf16[8,144,256]{2,1,0:T(8,128)(2,1)} %get-tuple-element.52), calls=%async_computation | async-start | bytes 1179648 | tf_op jit(solution)/shard_map/all_to_all | solution.py:499
  8.5 3.4 %pack.3 = (bf16[240,256]{1,0:T(8,128)(2,1)}, bf16[240,256]{1,0:T(8,128)(2,1)}, bf16[240,256]{1,0:T(8,128)(2,1)}, bf16[240,256]{1,0:T(8,128)(2,1)}, bf16[240,256]...) custom-call(bf16[256,768]{1,0:T(8,128)(2,1)} %refs_0_.3, ...), custom_call_target="tpu_custom_call" | custom-call | bytes 1048576 | tf_op jit(solution)/shard_map/pack/pallas_call | solution.py:517
  11.8 0.6 collective-permute-start
  12.4 1.7 %collective-permute-start.1 = (bf16[240,256]{1,0:T(8,128)(2,1)}, bf16[240,256]{1,0:T(8,128)(2,1)S(1)}, u32[]{:S(2)}, u32[]{:S(2)}) collective-permute-start(bf16[240,256]{1,0:T(8,128)(2,1)} %get-tuple-element.56), channel_id=1, source_target_pairs={{0,2},{1,3},{2,0},{3,1},{4,6},{5,7},{6,4},{7,5},{8,10},{9,11},{10,... | collective-permute-start | bytes 368648 | tf_op jit(solution)/shard_map/ppermute | solution.py:496
  14.1 0.0 collective-permute-start.2
  14.1 1.7 %collective-permute-start.3 = (bf16[240,256]{1,0:T(8,128)(2,1)}, bf16[240,256]{1,0:T(8,128)(2,1)S(1)}, u32[]{:S(2)}, u32[]{:S(2)}) collective-permute-start(bf16[240,256]{1,0:T(8,128)(2,1)} %get-tuple-element.58), channel_id=1, source_target_pairs={{0,4},{1,5},{2,6},{3,7},{4,0},{5,1},{6,2},{7,3},{8,12},{9,13},{10,... | collective-permute-start | bytes 368648 | tf_op jit(solution)/shard_map/ppermute | solution.py:496
  15.8 0.1 collective-permute-start.4
  15.9 0.0 collective-permute-done.refs_1_.rest_1_.refs_2_.refs_9_
  15.9 2.6 %collective-permute-start.5 = (bf16[240,256]{1,0:T(8,128)(2,1)}, bf16[240,256]{1,0:T(8,128)(2,1)S(1)}, u32[]{:S(2)}, u32[]{:S(2)}) collective-permute-start(bf16[240,256]{1,0:T(8,128)(2,1)} %get-tuple-element.60), channel_id=1, source_target_pairs={{0,6},{1,7},{2,4},{3,5},{4,2},{5,3},{6,0},{7,1},{8,14},{9,15},{10,... | collective-permute-start | bytes 368648 | tf_op jit(solution)/shard_map/ppermute | solution.py:496
  18.5 2.6 %collective-permute-done.1.refs_2_.rest_2_.refs_3_.refs_10_ = bf16[240,256]{1,0:T(8,128)(2,1)S(1)} collective-permute-done((bf16[240,256]{1,0:T(8,128)(2,1)}, bf16[240,256]{1,0:T(8,128)(2,1)S(1)}, u32[]{:S(2)}, u32[]{:S(2)}) %collective-permute-start.1) | collective-permute-done | bytes 122912 | tf_op jit(solution)/shard_map/ppermute | solution.py:496
  21.1 0.4 collective-permute-start.6
  21.5 0.0 all-to-all-done.refs_0_
  21.6 0.2 copy-done.3
  21.8 5.1 %forward0.1 = (f32[64,2048]{1,0:T(8,128)S(1)}, bf16[48,512]{1,0:T(8,128)(2,1)S(1)}, bf16[96,512]{1,0:T(8,128)(2,1)S(1)}, f32[8,128]{1,0:T(8,128)S(1)}) custom-call(s32[8]{0:T(128)S(1)} %copy-done.3, s32[3,16]{1,0:T(4,128)S(1)} %copy-done.1, f32[8,128]{1,0:T(8,128)S(1)} %copy-done.2, bf16[8,144,256]{2,1,0:T(8,128)(2,1)S(1)} %all-to-all-done.refs_0_), custom_call_target="tpu_custom_call" | custom-call | bytes 1048576 | tf_op jit(solution)/shard_map/forward0/pallas_call | solution.py:541
  26.8 0.0 collective-permute-done.2.refs_3_.rest_3_.refs_4_.refs_11_
  26.8 2.7 %collective-permute-start.7 = (bf16[96,512]{1,0:T(8,128)(2,1)S(1)}, bf16[96,512]{1,0:T(8,128)(2,1)S(1)}, u32[]{:S(2)}, u32[]{:S(2)}) collective-permute-start(bf16[96,512]{1,0:T(8,128)(2,1)S(1)} %get-tuple-element.65.kv2), channel_id=1, source_target_pairs={{0,8},{1,9},{2,10},{3,11},{4,12},{5,13},{6,14},{7,15},{8,0},{9,1},... | collective-permute-start | bytes 294920 | tf_op jit(solution)/shard_map/ppermute | solution.py:496
  29.5 0.0 collective-permute-done.3.refs_4_.rest_4_.refs_5_.refs_12_
  29.5 0.0 collective-permute-done.4.refs_5_.rest_5_.refs_6_.refs_13_
  29.5 0.0 collective-permute-done.5.refs_6_.rest_6_.refs_7_.refs_14_
  29.5 0.0 collective-permute-done.6.refs_7_.rest_7_.refs_8_.refs_15_
  29.5 5.1 %forward1.1 = (f32[64,2048]{1,0:T(8,128)S(1)}, bf16[48,512]{1,0:T(8,128)(2,1)S(1)}, bf16[96,512]{1,0:T(8,128)(2,1)S(1)}, f32[8,128]{1,0:T(8,128)S(1)}) custom-call(s32[8]{0:T(128)S(1)} %copy-done.3, s32[3,16]{1,0:T(4,128)S(1)} %copy-done.1, f32[8,128]{1,0:T(8,128)S(1)} %get-tuple-element.53.tok_in, bf16[240,256]{1,0:T(8,128)(2,1)S(1)} %copy-done, ...), custom_call_target="tpu_custom_call" | custom-call | bytes 1048576 | tf_op jit(solution)/shard_map/forward1/pallas_call | solution.py:541
  34.6 2.2 %collective-permute-start.8 = (bf16[96,512]{1,0:T(8,128)(2,1)S(1)}, bf16[96,512]{1,0:T(8,128)(2,1)S(1)}, u32[]{:S(2)}, u32[]{:S(2)}) collective-permute-start(bf16[96,512]{1,0:T(8,128)(2,1)S(1)} %get-tuple-element.69.kv2), channel_id=1, source_target_pairs={{0,8},{1,9},{2,10},{3,11},{4,12},{5,13},{6,14},{7,15},{8,0},{9,1},... | collective-permute-start | bytes 294920 | tf_op jit(solution)/shard_map/ppermute | solution.py:496
  36.8 0.0 collective-permute-done.7.rest_8_
  36.8 3.2 %last0.1 = (bf16[48,2048]{1,0:T(8,128)(2,1)S(1)}, f32[8,2048]{1,0:T(8,128)S(1)}, f32[144,512]{1,0:T(8,128)S(1)}, bf16[1,96,512]{2,1,0:T(8,128)(2,1)S(1)}, f32[8,128]{1,0:T(8,128)S(1)}) custom-call(s32[8]{0:T(128)S(1)} %copy-done.3, s32[3,16]{1,0:T(4,128)S(1)} %copy-done.1, f32[8,128]{1,0:T(8,128)S(1)} %get-tuple-element.62.tok_in, ...), custom_call_target="tpu_custom_call" | custom-call | flops 21474836480 | bytes 1048576 | tf_op jit(solution)/shard_map/last0/pallas_call | solution.py:558
  40.0 0.9 %collective-permute-start.9 = (bf16[96,512]{1,0:T(8,128)(2,1)S(1)}, bf16[96,512]{1,0:T(8,128)(2,1)S(1)}, u32[]{:S(2)}, u32[]{:S(2)}) collective-permute-start(bf16[96,512]{1,0:T(8,128)(2,1)S(1)} %bitcast.2), channel_id=1, source_target_pairs={{0,8},{1,9},{2,10},{3,11},{4,12},{5,13},{6,14},{7,15},{8,0},{9,1},... | collective-permute-start | bytes 294920 | tf_op jit(solution)/shard_map/ppermute | solution.py:496
  40.9 1.6 %collective-permute-done.8.rest_8_ = bf16[96,512]{1,0:T(8,128)(2,1)S(1)} collective-permute-done((bf16[96,512]{1,0:T(8,128)(2,1)S(1)}, bf16[96,512]{1,0:T(8,128)(2,1)S(1)}, u32[]{:S(2)}, u32[]{:S(2)}) %collective-permute-start.8) | collective-permute-done | bytes 98336 | tf_op jit(solution)/shard_map/ppermute | solution.py:496
  42.5 3.4 %last1.1 = (bf16[48,2048]{1,0:T(8,128)(2,1)S(1)}, f32[8,2048]{1,0:T(8,128)S(1)}, f32[144,512]{1,0:T(8,128)S(1)}, bf16[1,96,512]{2,1,0:T(8,128)(2,1)S(1)}, f32[8,128]{1,0:T(8,128)S(1)}) custom-call(s32[8]{0:T(128)S(1)} %copy-done.3, s32[3,16]{1,0:T(4,128)S(1)} %copy-done.1, f32[8,128]{1,0:T(8,128)S(1)} %get-tuple-element.66.tok_in, ...), custom_call_target="tpu_custom_call" | custom-call | flops 21474836480 | bytes 1048576 | tf_op jit(solution)/shard_map/last1/pallas_call | solution.py:558
  45.9 0.5 collective-permute-start.10
  46.5 1.2 %collective-permute-done.9.refs_13_ = bf16[96,512]{1,0:T(8,128)(2,1)S(1)} collective-permute-done((bf16[96,512]{1,0:T(8,128)(2,1)S(1)}, bf16[96,512]{1,0:T(8,128)(2,1)S(1)}, u32[]{:S(2)}, u32[]{:S(2)}) %collective-permute-start.9) | collective-permute-done | bytes 98336 | tf_op jit(solution)/shard_map/ppermute | solution.py:496
  47.7 9.8 %backward0.1 = (bf16[8,240,256]{2,1,0:T(8,128)(2,1)}, f32[8,128]{1,0:T(8,128)S(1)}) custom-call(s32[8]{0:T(128)S(1)} %copy-done.3, s32[3,16]{1,0:T(4,128)S(1)} %copy-done.1, f32[8,128]{1,0:T(8,128)S(1)} %get-tuple-element.70.tok_in, bf16[8,144,256]{2,1,0:T(8,128)(2,1)S(1)} %all-to-all-done.refs_0_, bf16[240,256]{1,0:T(8,128)(2,1)S(1)} %copy-done, ...), custom_call_target="tpu_custom_call" | custom-call | flops 80530636800 | bytes 1048576 | tf_op jit(solution)/shard_map/backward0/pallas_call | solution.py:581
  57.5 5.3 %all-to-all-start.1 = ((bf16[8,240,256]{2,1,0:T(8,128)(2,1)}), bf16[8,240,256]{2,1,0:T(8,128)(2,1)S(1)}, u32[]{:S(2)}, u32[]{:S(2)}) async-start(bf16[8,240,256]{2,1,0:T(8,128)(2,1)} %get-tuple-element.76), calls=%async_computation.1 | async-start | bytes 1966080 | tf_op jit(solution)/shard_map/all_to_all | solution.py:499
  62.8 0.0 collective-permute-done.10.refs_18_
  62.8 8.8 %backward1.1 = (bf16[144,256]{1,0:T(8,128)(2,1)S(1)}, bf16[144,256]{1,0:T(8,128)(2,1)S(1)}, bf16[144,256]{1,0:T(8,128)(2,1)S(1)}, bf16[144,256]{1,0:T(8,128)(2,1...) custom-call(s32[8]{0:T(128)S(1)} %copy-done.3, ...), custom_call_target="tpu_custom_call" | custom-call | flops 80530636800 | bytes 1048576 | tf_op jit(solution)/shard_map/backward1/pallas_call | solution.py:581
  71.6 0.5 collective-permute-start.11
  72.1 1.7 %collective-permute-start.12 = (bf16[144,256]{1,0:T(8,128)(2,1)S(1)}, bf16[144,256]{1,0:T(8,128)(2,1)S(1)}, u32[]{:S(2)}, u32[]{:S(2)}) collective-permute-start(bf16[144,256]{1,0:T(8,128)(2,1)S(1)} %get-tuple-element.84), channel_id=1, source_target_pairs={{0,2},{1,3},{2,0},{3,1},{4,6},{5,7},{6,4},{7,5},{8,10},{9,11},{10,... | collective-permute-start | bytes 221192 | tf_op jit(solution)/shard_map/ppermute | solution.py:496
  73.7 0.1 collective-permute-start.13
  73.8 2.1 %collective-permute-start.14 = (bf16[144,256]{1,0:T(8,128)(2,1)S(1)}, bf16[144,256]{1,0:T(8,128)(2,1)S(1)}, u32[]{:S(2)}, u32[]{:S(2)}) collective-permute-start(bf16[144,256]{1,0:T(8,128)(2,1)S(1)} %get-tuple-element.86), channel_id=1, source_target_pairs={{0,4},{1,5},{2,6},{3,7},{4,0},{5,1},{6,2},{7,3},{8,12},{9,13},{10,... | collective-permute-start | bytes 221192 | tf_op jit(solution)/shard_map/ppermute | solution.py:496
  76.0 0.0 collective-permute-start.15
  76.0 0.0 collective-permute-done.11.refs_1_
  76.0 2.2 %collective-permute-start.16 = (bf16[144,256]{1,0:T(8,128)(2,1)S(1)}, bf16[144,256]{1,0:T(8,128)(2,1)S(1)}, u32[]{:S(2)}, u32[]{:S(2)}) collective-permute-start(bf16[144,256]{1,0:T(8,128)(2,1)S(1)} %get-tuple-element.88), channel_id=1, source_target_pairs={{0,6},{1,7},{2,4},{3,5},{4,2},{5,3},{6,0},{7,1},{8,14},{9,15},{10,... | collective-permute-start | bytes 221192 | tf_op jit(solution)/shard_map/ppermute | solution.py:496
  78.2 0.5 collective-permute-done.12.refs_2_
  78.6 0.4 collective-permute-start.17
  79.1 1.3 %unpack.2 = (bf16[256,768]{1,0:T(8,128)(2,1)}, bf16[256,768]{1,0:T(8,128)(2,1)}, bf16[256,768]{1,0:T(8,128)(2,1)}, bf16[256,768]{1,0:T(8,128)(2,1)}) custom-call(bf16[8,240,256]{2,1,0:T(8,128)(2,1)S(1)} %all-to-all-done.1.refs_0_), custom_call_target="tpu_custom_call" | custom-call | bytes 1048576 | tf_op jit(solution)/shard_map/unpack/pallas_call | solution.py:604
  80.3 0.0 collective-permute-done.15.refs_5_
  80.3 2.4 %collective-permute-done.16.refs_6_ = bf16[144,256]{1,0:T(8,128)(2,1)S(1)} collective-permute-done((bf16[144,256]{1,0:T(8,128)(2,1)S(1)}, bf16[144,256]{1,0:T(8,128)(2,1)S(1)}, u32[]{:S(2)}, u32[]{:S(2)}) %collective-permute-start.16) | collective-permute-done | bytes 73760 | tf_op jit(solution)/shard_map/ppermute | solution.py:496
  82.7 1.4 %collective-permute-done.17.refs_7_ = bf16[144,256]{1,0:T(8,128)(2,1)S(1)} collective-permute-done((bf16[144,256]{1,0:T(8,128)(2,1)S(1)}, bf16[144,256]{1,0:T(8,128)(2,1)S(1)}, u32[]{:S(2)}, u32[]{:S(2)}) %collective-permute-start.17) | collective-permute-done | bytes 73760 | tf_op jit(solution)/shard_map/ppermute | solution.py:496
  84.2 1.1 %unpack.3 = (bf16[256,768]{1,0:T(8,128)(2,1)}, bf16[256,768]{1,0:T(8,128)(2,1)}, bf16[256,768]{1,0:T(8,128)(2,1)}) custom-call(bf16[144,256]{1,0:T(8,128)(2,1)S(1)} %get-tuple-element.82.refs_0_, bf16[144,256]{1,0:T(8,128)(2,1)S(1)} %collective-permute-done.11.refs_1_, ...), custom_call_target="tpu_custom_call", output_to_operand_aliasing={{0}: (8, {}), {1}: (9, {}), {2}: (10, {})} | custom-call | bytes 1048576 | tf_op jit(solution)/shard_map/unpack/pallas_call | solution.py:614
  (10 shorter events, 0.0 us)
Async XLA Ops:
  3.2 18.3 %all-to-all-start = ((bf16[8,144,256]{2,1,0:T(8,128)(2,1)}), bf16[8,144,256]{2,1,0:T(8,128)(2,1)S(1)}, u32[]{:S(2)}, u32[]{:S(2)}) async-start(bf16[8,144,256]{2,1,0:T(8,128)(2,1)} %get-tuple-element.52), calls=%async_computation | async-start | bytes 1179648 | tf_op jit(solution)/shard_map/all_to_all | solution.py:499
  11.8 4.1 %collective-permute-start = (bf16[240,256]{1,0:T(8,128)(2,1)}, bf16[240,256]{1,0:T(8,128)(2,1)S(1)}, u32[]{:S(2)}, u32[]{:S(2)}) collective-permute-start(bf16[240,256]{1,0:T(8,128)(2,1)} %get-tuple-element.55), channel_id=1, source_target_pairs={{0,1},{1,0},{2,3},{3,2},{4,5},{5,4},{6,7},{7,6},{8,9},{9,8},{10,11... | collective-permute-start | bytes 368648 | tf_op jit(solution)/shard_map/ppermute | solution.py:496
  12.4 8.7 %collective-permute-start.1 = (bf16[240,256]{1,0:T(8,128)(2,1)}, bf16[240,256]{1,0:T(8,128)(2,1)S(1)}, u32[]{:S(2)}, u32[]{:S(2)}) collective-permute-start(bf16[240,256]{1,0:T(8,128)(2,1)} %get-tuple-element.56), channel_id=1, source_target_pairs={{0,2},{1,3},{2,0},{3,1},{4,6},{5,7},{6,4},{7,5},{8,10},{9,11},{10,... | collective-permute-start | bytes 368648 | tf_op jit(solution)/shard_map/ppermute | solution.py:496
  14.1 12.8 %collective-permute-start.2 = (bf16[240,256]{1,0:T(8,128)(2,1)}, bf16[240,256]{1,0:T(8,128)(2,1)S(1)}, u32[]{:S(2)}, u32[]{:S(2)}) collective-permute-start(bf16[240,256]{1,0:T(8,128)(2,1)} %get-tuple-element.57), channel_id=1, source_target_pairs={{0,3},{1,2},{2,1},{3,0},{4,7},{5,6},{6,5},{7,4},{8,11},{9,10},{10,... | collective-permute-start | bytes 368648 | tf_op jit(solution)/shard_map/ppermute | solution.py:496
  14.1 7.5 %copy-start.2 = (f32[8,128]{1,0:T(8,128)S(1)}, f32[8,128]{1,0:T(8,128)}, u32[]{:S(2)}) copy-start(f32[8,128]{1,0:T(8,128)} %get-tuple-element.51.tok_in) | copy-start | bytes 12292
  14.1 15.4 %collective-permute-start.3 = (bf16[240,256]{1,0:T(8,128)(2,1)}, bf16[240,256]{1,0:T(8,128)(2,1)S(1)}, u32[]{:S(2)}, u32[]{:S(2)}) collective-permute-start(bf16[240,256]{1,0:T(8,128)(2,1)} %get-tuple-element.58), channel_id=1, source_target_pairs={{0,4},{1,5},{2,6},{3,7},{4,0},{5,1},{6,2},{7,3},{8,12},{9,13},{10,... | collective-permute-start | bytes 368648 | tf_op jit(solution)/shard_map/ppermute | solution.py:496
  15.8 13.7 %collective-permute-start.4 = (bf16[240,256]{1,0:T(8,128)(2,1)}, bf16[240,256]{1,0:T(8,128)(2,1)S(1)}, u32[]{:S(2)}, u32[]{:S(2)}) collective-permute-start(bf16[240,256]{1,0:T(8,128)(2,1)} %get-tuple-element.59), channel_id=1, source_target_pairs={{0,5},{1,4},{2,7},{3,6},{4,1},{5,0},{6,3},{7,2},{8,13},{9,12},{10,... | collective-permute-start | bytes 368648 | tf_op jit(solution)/shard_map/ppermute | solution.py:496
  15.9 5.7 %copy-start.1 = (s32[3,16]{1,0:T(4,128)S(1)}, s32[3,16]{1,0:T(4,128)}, u32[]{:S(2)}) copy-start(s32[3,16]{1,0:T(4,128)} %off_ref.11) | copy-start | bytes 580
  15.9 13.6 %collective-permute-start.5 = (bf16[240,256]{1,0:T(8,128)(2,1)}, bf16[240,256]{1,0:T(8,128)(2,1)S(1)}, u32[]{:S(2)}, u32[]{:S(2)}) collective-permute-start(bf16[240,256]{1,0:T(8,128)(2,1)} %get-tuple-element.60), channel_id=1, source_target_pairs={{0,6},{1,7},{2,4},{3,5},{4,2},{5,3},{6,0},{7,1},{8,14},{9,15},{10,... | collective-permute-start | bytes 368648 | tf_op jit(solution)/shard_map/ppermute | solution.py:496
  21.1 0.7 copy-start.3
  21.1 8.4 %collective-permute-start.6 = (bf16[240,256]{1,0:T(8,128)(2,1)}, bf16[240,256]{1,0:T(8,128)(2,1)S(1)}, u32[]{:S(2)}, u32[]{:S(2)}) collective-permute-start(bf16[240,256]{1,0:T(8,128)(2,1)} %get-tuple-element.61), channel_id=1, source_target_pairs={{0,7},{1,6},{2,5},{3,4},{4,3},{5,2},{6,1},{7,0},{8,15},{9,14},{10,... | collective-permute-start | bytes 368648 | tf_op jit(solution)/shard_map/ppermute | solution.py:496
  21.8 7.8 %copy-start = (bf16[240,256]{1,0:T(8,128)(2,1)S(1)}, bf16[240,256]{1,0:T(8,128)(2,1)}, u32[]{:S(2)}) copy-start(bf16[240,256]{1,0:T(8,128)(2,1)} %get-tuple-element.54.refs_0_.rest_0_.refs_1_.refs_8_) | copy-start | bytes 368644
  26.8 9.9 %collective-permute-start.7 = (bf16[96,512]{1,0:T(8,128)(2,1)S(1)}, bf16[96,512]{1,0:T(8,128)(2,1)S(1)}, u32[]{:S(2)}, u32[]{:S(2)}) collective-permute-start(bf16[96,512]{1,0:T(8,128)(2,1)S(1)} %get-tuple-element.65.kv2), channel_id=1, source_target_pairs={{0,8},{1,9},{2,10},{3,11},{4,12},{5,13},{6,14},{7,15},{8,0},{9,1},... | collective-permute-start | bytes 294920 | tf_op jit(solution)/shard_map/ppermute | solution.py:496
  34.6 7.9 %collective-permute-start.8 = (bf16[96,512]{1,0:T(8,128)(2,1)S(1)}, bf16[96,512]{1,0:T(8,128)(2,1)S(1)}, u32[]{:S(2)}, u32[]{:S(2)}) collective-permute-start(bf16[96,512]{1,0:T(8,128)(2,1)S(1)} %get-tuple-element.69.kv2), channel_id=1, source_target_pairs={{0,8},{1,9},{2,10},{3,11},{4,12},{5,13},{6,14},{7,15},{8,0},{9,1},... | collective-permute-start | bytes 294920 | tf_op jit(solution)/shard_map/ppermute | solution.py:496
  40.0 7.7 %collective-permute-start.9 = (bf16[96,512]{1,0:T(8,128)(2,1)S(1)}, bf16[96,512]{1,0:T(8,128)(2,1)S(1)}, u32[]{:S(2)}, u32[]{:S(2)}) collective-permute-start(bf16[96,512]{1,0:T(8,128)(2,1)S(1)} %bitcast.2), channel_id=1, source_target_pairs={{0,8},{1,9},{2,10},{3,11},{4,12},{5,13},{6,14},{7,15},{8,0},{9,1},... | collective-permute-start | bytes 294920 | tf_op jit(solution)/shard_map/ppermute | solution.py:496
  45.9 16.9 %collective-permute-start.10 = (bf16[96,512]{1,0:T(8,128)(2,1)S(1)}, bf16[96,512]{1,0:T(8,128)(2,1)S(1)}, u32[]{:S(2)}, u32[]{:S(2)}) collective-permute-start(bf16[96,512]{1,0:T(8,128)(2,1)S(1)} %bitcast.3), channel_id=1, source_target_pairs={{0,8},{1,9},{2,10},{3,11},{4,12},{5,13},{6,14},{7,15},{8,0},{9,1},... | collective-permute-start | bytes 294920 | tf_op jit(solution)/shard_map/ppermute | solution.py:496
  57.5 21.6 %all-to-all-start.1 = ((bf16[8,240,256]{2,1,0:T(8,128)(2,1)}), bf16[8,240,256]{2,1,0:T(8,128)(2,1)S(1)}, u32[]{:S(2)}, u32[]{:S(2)}) async-start(bf16[8,240,256]{2,1,0:T(8,128)(2,1)} %get-tuple-element.76), calls=%async_computation.1 | async-start | bytes 1966080 | tf_op jit(solution)/shard_map/all_to_all | solution.py:499
  71.6 4.3 %collective-permute-start.11 = (bf16[144,256]{1,0:T(8,128)(2,1)S(1)}, bf16[144,256]{1,0:T(8,128)(2,1)S(1)}, u32[]{:S(2)}, u32[]{:S(2)}) collective-permute-start(bf16[144,256]{1,0:T(8,128)(2,1)S(1)} %get-tuple-element.83), channel_id=1, source_target_pairs={{0,1},{1,0},{2,3},{3,2},{4,5},{5,4},{6,7},{7,6},{8,9},{9,8},{10,11... | collective-permute-start | bytes 221192 | tf_op jit(solution)/shard_map/ppermute | solution.py:496
  72.1 6.5 %collective-permute-start.12 = (bf16[144,256]{1,0:T(8,128)(2,1)S(1)}, bf16[144,256]{1,0:T(8,128)(2,1)S(1)}, u32[]{:S(2)}, u32[]{:S(2)}) collective-permute-start(bf16[144,256]{1,0:T(8,128)(2,1)S(1)} %get-tuple-element.84), channel_id=1, source_target_pairs={{0,2},{1,3},{2,0},{3,1},{4,6},{5,7},{6,4},{7,5},{8,10},{9,11},{10,... | collective-permute-start | bytes 221192 | tf_op jit(solution)/shard_map/ppermute | solution.py:496
  73.7 6.6 %collective-permute-start.13 = (bf16[144,256]{1,0:T(8,128)(2,1)S(1)}, bf16[144,256]{1,0:T(8,128)(2,1)S(1)}, u32[]{:S(2)}, u32[]{:S(2)}) collective-permute-start(bf16[144,256]{1,0:T(8,128)(2,1)S(1)} %get-tuple-element.85), channel_id=1, source_target_pairs={{0,3},{1,2},{2,1},{3,0},{4,7},{5,6},{6,5},{7,4},{8,11},{9,10},{10,... | collective-permute-start | bytes 221192 | tf_op jit(solution)/shard_map/ppermute | solution.py:496
  73.8 6.5 %collective-permute-start.14 = (bf16[144,256]{1,0:T(8,128)(2,1)S(1)}, bf16[144,256]{1,0:T(8,128)(2,1)S(1)}, u32[]{:S(2)}, u32[]{:S(2)}) collective-permute-start(bf16[144,256]{1,0:T(8,128)(2,1)S(1)} %get-tuple-element.86), channel_id=1, source_target_pairs={{0,4},{1,5},{2,6},{3,7},{4,0},{5,1},{6,2},{7,3},{8,12},{9,13},{10,... | collective-permute-start | bytes 221192 | tf_op jit(solution)/shard_map/ppermute | solution.py:496
  76.0 4.4 %collective-permute-start.15 = (bf16[144,256]{1,0:T(8,128)(2,1)S(1)}, bf16[144,256]{1,0:T(8,128)(2,1)S(1)}, u32[]{:S(2)}, u32[]{:S(2)}) collective-permute-start(bf16[144,256]{1,0:T(8,128)(2,1)S(1)} %get-tuple-element.87), channel_id=1, source_target_pairs={{0,5},{1,4},{2,7},{3,6},{4,1},{5,0},{6,3},{7,2},{8,13},{9,12},{10,... | collective-permute-start | bytes 221192 | tf_op jit(solution)/shard_map/ppermute | solution.py:496
  76.0 6.8 %collective-permute-start.16 = (bf16[144,256]{1,0:T(8,128)(2,1)S(1)}, bf16[144,256]{1,0:T(8,128)(2,1)S(1)}, u32[]{:S(2)}, u32[]{:S(2)}) collective-permute-start(bf16[144,256]{1,0:T(8,128)(2,1)S(1)} %get-tuple-element.88), channel_id=1, source_target_pairs={{0,6},{1,7},{2,4},{3,5},{4,2},{5,3},{6,0},{7,1},{8,14},{9,15},{10,... | collective-permute-start | bytes 221192 | tf_op jit(solution)/shard_map/ppermute | solution.py:496
  78.6 5.5 %collective-permute-start.17 = (bf16[144,256]{1,0:T(8,128)(2,1)S(1)}, bf16[144,256]{1,0:T(8,128)(2,1)S(1)}, u32[]{:S(2)}, u32[]{:S(2)}) collective-permute-start(bf16[144,256]{1,0:T(8,128)(2,1)S(1)} %get-tuple-element.89), channel_id=1, source_target_pairs={{0,7},{1,6},{2,5},{3,4},{4,3},{5,2},{6,1},{7,0},{8,15},{9,14},{10,... | collective-permute-start | bytes 221192 | tf_op jit(solution)/shard_map/ppermute | solution.py:496

commit v4 on v3

--- a/solution.py
+++ b/solution.py
@@ -44,7 +44,15 @@
         self.slide_pad = -(-slide_count // 8) * 8
         self.rest = 128 - 2 * self.hd - 8 - self.slide_pad
         self.aligned = self.cseg % 128 == 0
-        assert self.rest >= 0 and self.hd + 16 <= 64 and self.hd % 16 == 0
+        self.table = (-(-self.table_row(self.chunks, 0) // 8) * 8, 128)
+        assert self.rest >= 0 and self.hd + 16 <= 64 and self.hd % 16 == 0 and self.chunks > 1
+
+
+    def level_bits(self, level):
+        return level if level < self.levels - 1 else self.bits
+
+    def table_row(self, chunk, level):
+        return self.slide_pad + chunk * (self.levels + 1) + level
 
 
 def reversed_bits(value, bits):
@@ -105,15 +113,20 @@
     ]
     for copy in copies:
         copy.start()
+    if count_out > 1:
+        fill_table(plan, *refs[count : count + 2], outs[-1])
+        outs = outs[:-1]
     order = class_order(plan.tok, plan.stride, (plan.tok, plan.tok), 0, 1)
     me = near_index(plan)
     for i, copy in enumerate(copies):
         copy.wait()
-        turned[...] = dot(rows[i], order, 0, 1).astype(BF16)
-        for j in range(plan.near):
-            if len(outs) == 1:
-                outs[0][j, i * hd : (i + 1) * hd, :] = turned[j * hd : (j + 1) * hd, :]
-            else:
+        x = dot(rows[i], order, 0, 1).astype(BF16)
+        if len(outs) == 1:
+            for j in range(plan.near):
+                outs[0][j, i * hd : (i + 1) * hd, :] = x[j * hd : (j + 1) * hd, :]
+        else:
+            turned[...] = x
+            for j in range(plan.near):
                 first = pl.multiple_of((me ^ j) * hd, 16)
                 outs[j][i * hd : (i + 1) * hd, :] = turned[pl.ds(first, hd), :]
 
@@ -123,9 +136,8 @@
         return jnp.concatenate(
             [x[:, c * plan.cdev : (c + 1) * plan.cdev] for c in range(plan.stride) for x in blocks],
             axis=1,
-        )
-    x = jnp.concatenate(blocks, axis=1).astype(BF16)
-    return dot(x, device_lanes(plan, 1, 0))
+        ).astype(F32)
+    return dot(jnp.concatenate(blocks, axis=1), device_lanes(plan, 1, 0))
 
 
 def device_lanes(plan, axis_dev, axis_seg):
@@ -148,16 +160,14 @@
             )
             for d in range(plan.seg_dev)
         ]
-    x = dot(x.astype(BF16), device_lanes(plan, 0, 1))
+    x = dot(x, device_lanes(plan, 0, 1)).astype(BF16)
     return [x[:, d * plan.tok : (d + 1) * plan.tok] for d in range(plan.seg_dev)]
 
 
-def slide_rows(plan, pos, len_ref):
+def slide_rows(plan, pos, table):
     slide = jnp.zeros(pos.shape, jnp.int32)
-    end = 0
     for i in range(plan.slides):
-        end = end + len_ref[i]
-        slide = slide + jnp.where(pos >= end, 1, 0)
+        slide = slide + jnp.where(pos.astype(F32) >= table[i : i + 1, 0:1], 1, 0)
     shape = (plan.slide_pad, pos.shape[1])
     return jnp.where(iota(shape, 0) == slide, 1.0, 0.0)
 
@@ -223,40 +233,31 @@
     return jnp.concatenate(query_t, axis=1), key_t, value_t
 
 
-def level_start(plan, off_ref, level, chunk):
-    head = chunk * plan.near + lax.rem(lax.axis_index("seq"), plan.near)
-    bits = level if level < plan.levels - 1 else plan.bits
-    rows = SEG0 >> bits
-    return reversed_bits(off_ref[level, head] % (1 << bits), bits) * rows, rows
-
-
-def tile_pieces(plan, off_ref, chunk, tile):
+def tile_pieces(plan, starts, tile):
     level, first = plan.tiles[tile]
-    start, rows = level_start(plan, off_ref, level, chunk)
+    rows = SEG0 >> level
     out = []
     for i in range(1 << level):
-        src = pl.ds(pl.multiple_of((first + i) * SEG0 + start, 128), rows)
+        src = pl.ds(pl.multiple_of((first + i) * SEG0 + starts[level], 128), rows)
         out.append((src, slice(tile * SEG0 + i * rows, tile * SEG0 + (i + 1) * rows)))
     return out
 
 
-def last_slices(plan, off_ref, chunk):
-    start, count = level_start(plan, off_ref, plan.levels - 1, chunk)
+def last_slices(plan, starts):
     return [
-        pl.ds(pl.multiple_of(seg * SEG0 + start, plan.cseg), count) for seg in range(plan.segs)
+        pl.ds(pl.multiple_of(seg * SEG0 + starts[-1], plan.cseg), plan.cseg) for seg in range(plan.segs)
     ]
 
 
-def last_places(plan, off_ref, chunk, shape, axis_seg, axis_last):
-    start, _ = level_start(plan, off_ref, plan.levels - 1, chunk)
-    hit = iota(shape, axis_seg) == start + iota(shape, axis_last)
+def last_places(plan, starts, shape, axis_seg, axis_last):
+    hit = iota(shape, axis_seg) == starts[-1] + iota(shape, axis_last)
     return jnp.where(hit, 1.0, 0.0)
 
 
-def last_lanes(plan, off_ref, chunk, ref):
+def last_lanes(plan, starts, ref):
     if plan.aligned:
-        return jnp.concatenate([ref[:, s] for s in last_slices(plan, off_ref, chunk)], axis=1)
-    place = last_places(plan, off_ref, chunk, (SEG0, plan.cseg), 0, 1)
+        return jnp.concatenate([ref[:, s] for s in last_slices(plan, starts)], axis=1)
+    place = last_places(plan, starts, (SEG0, plan.cseg), 0, 1)
     exact = lax.Precision.HIGHEST
     parts = [
         dot(ref[:, g * SEG0 : (g + 1) * SEG0].astype(F32), place, precision=exact)
@@ -265,12 +266,12 @@
     return jnp.concatenate(parts, axis=1).astype(ref.dtype)
 
 
-def last_update(plan, off_ref, chunk, ref, rows, part, update, fill):
+def last_update(plan, starts, ref, rows, part, update, fill):
     if plan.aligned:
-        for seg, s in enumerate(last_slices(plan, off_ref, chunk)):
+        for seg, s in enumerate(last_slices(plan, starts)):
             ref[rows, s] = update(ref[rows, s], part[:, seg * plan.cseg : (seg + 1) * plan.cseg])
         return
-    place = last_places(plan, off_ref, chunk, (plan.cseg, SEG0), 1, 0)
+    place = last_places(plan, starts, (plan.cseg, SEG0), 1, 0)
     hit = jnp.max(place, axis=0, keepdims=True) > 0
     for seg in range(plan.segs):
         own = part[:, seg * plan.cseg : (seg + 1) * plan.cseg]
@@ -283,6 +284,30 @@
     return jnp.where(iota((64, 1), 0) >= plan.hd + 8, -BIG, 0.0)
 
 
+def fill_table(plan, len_ref, off_ref, table):
+    table[...] = jnp.zeros_like(table)
+
+    def put(row, value):
+        table[row : row + 1, :] = jnp.full((1, 128), value, jnp.int32).astype(F32)
+
+    end = 0
+    for i in range(plan.slides):
+        end = end + len_ref[i]
+        put(i, end)
+    for chunk in range(plan.chunks):
+        head = chunk * plan.near + near_index(plan)
+        for level in range(plan.levels):
+            bits = plan.level_bits(level)
+            first = reversed_bits(off_ref[level, head] % (1 << bits), bits) * (SEG0 >> bits)
+            put(plan.table_row(chunk, level), first)
+        put(plan.table_row(chunk, plan.levels), off_ref[plan.levels - 1, head] % plan.stride)
+
+
+def level_starts(plan, table, chunk):
+    rows = [plan.table_row(chunk, level) for level in range(plan.levels)]
+    return [jnp.max(table[row : row + 1, :]).astype(jnp.int32) for row in rows]
+
+
 def slots_of(plan, refs):
     if len(refs) > 1:
         return refs
@@ -293,7 +318,7 @@
     return segment_from(
         plan,
         [
-            slots[seg * plan.seg_dev + d][first : first + count * plan.hd, :].astype(F32)
+            slots[seg * plan.seg_dev + d][first : first + count * plan.hd, :]
             for d in range(plan.seg_dev)
         ],
     )
@@ -305,49 +330,62 @@
     return seg * SEG0 + (lax.rem(me, plan.seg_dev) ^ slot) * plan.tok + inside
 
 
-def segment_slides(plan, seg, len_ref):
+def segment_slides(plan, seg, table):
     n = iota((1, SEG0), 1)
     inside = (n % plan.cdev) * plan.stride + reversed_bits(n // plan.cseg, plan.bits)
     pos = slot_tokens(plan, seg, n % plan.cseg // plan.cdev, inside)
-    return slide_rows(plan, lax.axis_index("seq") // plan.near * plan.rows + pos, len_ref)
-
-
-def forward_body(
-    plan, chunk, first, blocks, len_ref, off_ref, tok_in, *refs
-):
-    acc_ref, q2, kv2, tok_out, ka, qat, vat, raw, res = refs[blocks:]
-    slots = slots_of(plan, refs[:blocks])
+    return slide_rows(plan, lax.axis_index("seq") // plan.near * plan.rows + pos, table)
+
+
+def forward_body(plan, chunk, first, blocks, parts, table, tok_in, *refs):
+    slots, refs = slots_of(plan, refs[:blocks]) if blocks else None, refs[blocks:]
+    if parts == "rows":
+        q2, kv2, ka, qat, vat, tok_out, raw = refs
+    elif parts == "sums":
+        ka, qat, vat, acc_ref, tok_out, res = refs
+    else:
+        q2, kv2, acc_ref, tok_out, raw, ka, qat, vat, res = refs
+    tok_out[...] = jnp.zeros_like(tok_out)
+    starts = level_starts(plan, table, chunk)
+    if parts != "sums":
+        forward_operands(plan, first, slots, table, starts, q2, kv2, ka, qat, vat, raw)
+    if parts != "rows":
+        forward_levels(plan, starts, ka, qat, vat, acc_ref, res)
+
+
+def forward_operands(plan, first, slots, table, starts, q2, kv2, ka, qat, vat, raw):
     hd = plan.hd
-    tok_out[...] = jnp.zeros_like(tok_out)
     for seg in range(plan.segs):
         rows = slice(seg * SEG0, (seg + 1) * SEG0)
         xt = segment_of(plan, slots, first, 3, seg)
         raw[:, rows] = xt.astype(BF16)
         q, k, v = (xt[i * hd : (i + 1) * hd] for i in range(3))
-        one_hot = segment_slides(plan, seg, len_ref)
+        one_hot = segment_slides(plan, seg, table)
         ka[rows, :] = key_features(plan, k, one_hot).T.astype(BF16)
         qat[:, rows] = query_features(plan, q, one_hot).astype(BF16)
         vat[:, rows] = value_features(plan, v).astype(BF16)
     for tile in range(plan.segs, len(plan.tiles)):
-        for src, dst in tile_pieces(plan, off_ref, chunk, tile):
+        for src, dst in tile_pieces(plan, starts, tile):
             ka[dst, :] = ka[src, :]
             for ref in (qat, vat):
                 ref[:, dst] = ref[:, src]
-    last = last_lanes(plan, off_ref, chunk, raw)
+    last = last_lanes(plan, starts, raw)
     q2[...] = last[0:hd]
     kv2[...] = last[hd:]
 
+
+def forward_levels(plan, starts, ka, qat, vat, acc_ref, res):
     tiles = [slice(t * SEG0, (t + 1) * SEG0) for t in range(len(plan.tiles))]
     scores = [dot(ka[rows, :], qat[:, rows]) for rows in tiles]
     for s, rows in zip(scores, tiles):
         res[:, rows] = forward_tile(plan, s, vat[:, rows])
     acc_ref[...] = res[:, 0 : plan.rows]
     for tile in range(plan.segs, len(plan.tiles)):
-        for src, dst in tile_pieces(plan, off_ref, chunk, tile):
+        for src, dst in tile_pieces(plan, starts, tile):
             acc_ref[:, src] = merged(plan, acc_ref[:, src], res[:, dst])
 
 
-def last_body(plan, chunk, first, blocks, len_ref, off_ref, tok_in, acc_ref, q2, kv2, *rest):
+def last_body(plan, chunk, first, blocks, table, tok_in, acc_ref, q2, kv2, *rest):
     slots, rest = slots_of(plan, rest[:blocks]), rest[blocks:]
     far_in, (att_ref, ld_ref, grad_ref, far_ref, tok_out, acc, gt) = (
         rest[: plan.far - 1],
@@ -356,21 +394,22 @@
     hd = plan.hd
     tok_out[...] = jnp.zeros_like(tok_out)
     group = lax.axis_index("seq") // plan.near
-    head = chunk * plan.near + lax.rem(lax.axis_index("seq"), plan.near)
+    starts = level_starts(plan, table, chunk)
+    row = plan.table_row(chunk, plan.levels)
     acc[...] = acc_ref[...]
     x = jnp.concatenate([ref[...].astype(F32) for ref in (kv2,) + far_in], axis=1)
     n = iota((1, SEG0), 1)
     owner = group - n // plan.last
     owner = jnp.where(owner < 0, owner + plan.far, owner)
-    inside = (n % plan.cdev) * plan.stride + off_ref[plan.levels - 1, head] % plan.stride
+    inside = (n % plan.cdev) * plan.stride + table[row : row + 1, 0:1].astype(jnp.int32)
     seg, slot = n % plan.last // plan.cseg, n % plan.cseg // plan.cdev
     pos = owner * plan.rows + slot_tokens(plan, seg, slot, inside)
-    one_hot = slide_rows(plan, pos, len_ref)
+    one_hot = slide_rows(plan, pos, table)
     key_f = key_features(plan, x[0:hd], one_hot)
     query_f = query_features(plan, q2[...].astype(F32), one_hot[:, 0 : plan.last])
     vat2 = value_features(plan, x[hd : 2 * hd]).astype(BF16)
     res = forward_tile(plan, dot(key_f.T.astype(BF16), query_f.astype(BF16)), vat2)
-    last_update(plan, off_ref, chunk, acc, slice(None), res, partial(merged, plan), no_level(plan))
+    last_update(plan, starts, acc, slice(None), res, partial(merged, plan), no_level(plan))
     for seg in range(plan.segs):
         rows = slice(seg * SEG0, (seg + 1) * SEG0)
         a = acc[:, rows]
@@ -382,8 +421,8 @@
         gt[:, rows] = g.astype(BF16)
         grad_dot = jnp.sum(g * att.astype(F32), axis=0, keepdims=True)
         ld_ref[:, rows] = jnp.where(iota((8, SEG0), 0) == 0, log_total, grad_dot)
-    g2 = last_lanes(plan, off_ref, chunk, gt)
-    ld2 = last_lanes(plan, off_ref, chunk, ld_ref)
+    g2 = last_lanes(plan, starts, gt)
+    ld2 = last_lanes(plan, starts, ld_ref)
     qa2, ga2 = backward_queries(plan, query_f, g2.astype(F32), ld2)
     dq, dk, dv = backward_tile(plan, qa2, key_f.astype(BF16), ga2[:, 0:64], vat2, g2, q2[...])
     grad_ref[...] = jnp.concatenate(
@@ -405,21 +444,23 @@
     return query_f.T.astype(BF16), grad_f.T.astype(BF16)
 
 
-def backward_body(plan, chunk, places, blocks, atts, slotted, len_ref, off_ref, tok_in, *refs):
+def backward_body(plan, chunk, places, blocks, ends, table, tok_in, ld_ref, *refs):
     slots, refs = slots_of(plan, refs[: blocks[0]]), refs[blocks[0] :]
     g_slots, refs = slots_of(plan, refs[: blocks[1]]), refs[blocks[1] :]
-    att_refs, refs = refs[:atts], refs[atts:]
-    (ld_ref, grad2), refs = refs[:2], refs[2:]
-    far_refs, refs = refs[: plan.far - 1], refs[plan.far - 1 :]
-    outs, (tok_out, qa, kat, ga, vat, gt, qt, grads) = refs[:-8], refs[-8:]
+    if ends:
+        grad2, far_refs, outs, refs = refs[0], refs[1 : plan.far], refs[plan.far : -8], refs[-8:]
+        tok_out, qa, kat, ga, vat, gt, qt, grads = refs
+    else:
+        grads, tok_out, qa, kat, ga, vat, gt, qt = refs
     hd = plan.hd
     tok_out[...] = jnp.zeros_like(tok_out)
+    starts = level_starts(plan, table, chunk)
     for seg in range(plan.segs):
         rows = slice(seg * SEG0, (seg + 1) * SEG0)
         xt = segment_of(plan, slots, places[0], 3, seg)
         q, k, v = (xt[i * hd : (i + 1) * hd] for i in range(3))
         g = segment_of(plan, g_slots, places[1], 1, seg)
-        one_hot = segment_slides(plan, seg, len_ref)
+        one_hot = segment_slides(plan, seg, table)
         kat[:, rows] = key_features(plan, k, one_hot).astype(BF16)
         vat[:, rows] = value_features(plan, v).astype(BF16)
         qt[:, rows] = q.astype(BF16)
@@ -428,7 +469,7 @@
             plan, query_features(plan, q, one_hot), g, ld_ref[:, rows]
         )
     for tile in range(plan.segs, len(plan.tiles)):
-        for src, dst in tile_pieces(plan, off_ref, chunk, tile):
+        for src, dst in tile_pieces(plan, starts, tile):
             qa[dst, :] = qa[src, :]
             ga[dst, :] = ga[src, :]
             for ref in (kat, vat, gt, qt):
@@ -443,27 +484,45 @@
             for i, part in enumerate(parts):
                 grads[i * hd : (i + 1) * hd, rows] = part
             continue
-        for src, dst in tile_pieces(plan, off_ref, chunk, tile):
+        for src, dst in tile_pieces(plan, starts, tile):
             at = slice(dst.start - rows.start, dst.stop - rows.start)
             for i, part in enumerate(parts):
                 own = slice(i * hd, (i + 1) * hd)
                 grads[own, src] = grads[own, src] + part[:, at]
+    if ends:
+
+        def store(slot, x):
+            outs[slot][...] = x
+
+        finished(plan, starts, [], grad2, far_refs, grads, store)
+
+
+def finished(plan, starts, att_refs, grad2, far_refs, grads, store):
+    hd = plan.hd
     more = grad2[...]
     if far_refs:
         far = sum(ref[...].astype(F32) for ref in far_refs)
         more = jnp.concatenate([more[0:hd], more[hd:] + far], axis=0)
-    last_update(plan, off_ref, chunk, grads, slice(None), more, jnp.add, 0.0)
+    last_update(plan, starts, grads, slice(None), more, jnp.add, 0.0)
     scale = hd**-0.5
     for seg in range(plan.segs):
         rows = slice(seg * SEG0, (seg + 1) * SEG0)
-        parts = [ref[:, rows].astype(F32) for ref in att_refs]
-        parts += [grads[0 : 2 * hd, rows] * scale, grads[2 * hd : 3 * hd, rows]]
+        parts = [ref[:, rows] for ref in att_refs]
+        parts += [(grads[0 : 2 * hd, rows] * scale).astype(BF16), grads[2 * hd : 3 * hd, rows].astype(BF16)]
         for d, x in enumerate(segment_to(plan, jnp.concatenate(parts, axis=0))):
-            slot = seg * plan.seg_dev + d
-            if slotted:
-                outs[slot][...] = x.astype(BF16)
-            else:
-                outs[0][near_index(plan) ^ slot] = x.astype(BF16)
+            store(seg * plan.seg_dev + d, x)
+
+
+def finish_body(plan, chunk, atts, table, tok_in, near_ref, *refs):
+    att_refs, refs = refs[:atts], refs[atts:]
+    grad2, far_refs, (out_ref, tok_out, grads) = refs[0], refs[1 : plan.far], refs[plan.far :]
+    tok_out[...] = jnp.zeros_like(tok_out)
+    grads[...] = near_ref[...]
+
+    def store(slot, x):
+        out_ref[near_index(plan) ^ slot] = x
+
+    finished(plan, level_starts(plan, table, chunk), att_refs, grad2, far_refs, grads, store)
 
 
 def unpack_body(plan, places, slotted, *refs):
@@ -515,43 +574,67 @@
         slotted = len(received) > 0
         block = (len(pieces) * hd, tok_rows)
         *packed, tok = kernel_call(
-            partial(pack_body, plan, [c for c, _ in pieces], near if slotted else 1),
-            ([sds(block, BF16)] * near if slotted else [sds((near,) + block, BF16)]) + [TOKEN],
-            [ANY] * (len(pieces) + len(token)),
+            partial(pack_body, plan, [c for c, _ in pieces], near + 1 if slotted else 1),
+            (
+                [sds(block, BF16)] * near + [sds(plan.table, F32)]
+                if slotted
+                else [sds((near,) + block, BF16)]
+            )
+            + [TOKEN],
+            [ANY] * len(pieces) + [SMEM] * 2 * slotted + [ANY] * len(token),
             [
                 pltpu.VMEM((len(pieces), tok_rows, width), BF16),
                 pltpu.VMEM((width, tok_rows), BF16),
                 pltpu.SemaphoreType.DMA((len(pieces),)),
             ],
             name="pack",
-            limit=PACK_LIMIT,
-        )(*(arrays[i] for _, i in pieces), *token)
+            limit=VMEM_LIMIT if slotted else PACK_LIMIT,
+        )(*(arrays[i] for _, i in pieces), *(slide_lengths, head_offsets) * slotted, *token)
         token = (tok,)
+        if slotted:
+            table = packed.pop()
         for place, piece in enumerate(pieces):
             where[piece] = (len(received), place * hd)
         received.append(traded(packed) if slotted else [swap(packed[0])])
 
     n, n3, n2 = plan.rows, plan.all_rows, plan.last
     pair_flops = 20 * 2 * 128 * SEG0 * SEG0
-    scalars = (slide_lengths, head_offsets)
     (token,) = token
     fronts = []
     for chunk in range(chunks):
         source, first = where[chunk, 0]
-        acc, q2, kv2, token = kernel_call(
-            partial(forward_body, plan, chunk, first, len(received[source])),
-            [sds((64, n), F32), sds((hd, n2), BF16), sds((2 * hd, n2), BF16), TOKEN],
-            [SMEM, SMEM, ANY] + [VMEM] * len(received[source]),
-            [
-                pltpu.VMEM((n3, 128), BF16),
-                pltpu.VMEM((128, n3), BF16),
-                pltpu.VMEM((64, n3), BF16),
-                pltpu.VMEM((3 * hd, n), BF16),
-                pltpu.VMEM((64, n3), F32),
-            ],
-            name=f"forward{chunk}",
-        )(*scalars, token, *received[source])
-        fronts.append((acc, q2, kv2, *(shifted(kv2, s) for s in range(1, plan.far))))
+        near_x = received[source]
+        last_rows = [sds((hd, n2), BF16), sds((2 * hd, n2), BF16)]
+        operands = [(n3, 128), (128, n3), (64, n3)]
+        raw, res = pltpu.VMEM((3 * hd, n), BF16), pltpu.VMEM((64, n3), F32)
+        sums = sds((64, n), F32)
+        make = partial(forward_body, plan, chunk, first)
+        if chunk == 0:
+            q2, kv2, acc, token = kernel_call(
+                partial(make, len(near_x), "both"),
+                last_rows + [sums, TOKEN],
+                [VMEM, ANY] + [VMEM] * len(near_x),
+                [raw] + [pltpu.VMEM(shape, BF16) for shape in operands] + [res],
+                name=f"forward{chunk}",
+            )(table, token, *near_x)
+            far_kv = [shifted(kv2, s) for s in range(1, plan.far)]
+        else:
+            q2, kv2, *state, token = kernel_call(
+                partial(make, len(near_x), "rows"),
+                last_rows + [sds(shape, BF16) for shape in operands] + [TOKEN],
+                [VMEM, ANY] + [VMEM] * len(near_x),
+                [raw],
+                name=f"rows{chunk}",
+            )(table, token, *near_x)
+            far_kv = [shifted(kv2, s) for s in range(1, plan.far)]
+            acc, token = kernel_call(
+                partial(make, 0, "sums"),
+                [sums, TOKEN],
+                [VMEM, ANY] + [VMEM] * 3,
+                [res],
+                name=f"sums{chunk}",
+            )(table, token, *state)
+        fronts.append((acc, q2, kv2, *far_kv))
     states = []
     for chunk, front in enumerate(fronts):
         source, first = where[chunk, 3]
@@ -564,26 +647,25 @@
                 sds((max(plan.far - 1, 1), 2 * hd, n2), BF16),
                 TOKEN,
             ],
-            [SMEM, SMEM, ANY] + [VMEM] * (len(front) + len(received[source])),
+            [VMEM, ANY] + [VMEM] * (len(front) + len(received[source])),
             [pltpu.VMEM((64, n), F32), pltpu.VMEM((hd, n), BF16)],
             flops=4 * pair_flops,
             name=f"last{chunk}",
-        )(*scalars, token, *front[:3], *received[source], *front[3:])
+        )(table, token, *front[:3], *received[source], *front[3:])
         states.append((att, (ld, grad2, *(shifted(far2[s - 1], -s) for s in range(1, plan.far)))))
     full = sds((tok_rows, model_width), BF16)
-    for chunk, (_, state) in enumerate(states):
+    for chunk, (_, (ld, *tail)) in enumerate(states):
         atts = [s[0] for s in states] if chunk == 0 else []
-        slotted = chunk == chunks - 1
+        slotted = chunk == chunks - 1 and not atts
         count = len(atts) + 3
         sources = [where[chunk, 0], where[chunk, 3]]
         blocks = [len(received[x[0]]) for x in sources]
         block = sds((count * hd, tok_rows), BF16)
+        grads = pltpu.VMEM((3 * hd, n), F32)
         *out, token = kernel_call(
-            partial(
-                backward_body, plan, chunk, [x[1] for x in sources], blocks, len(atts), slotted
-            ),
-            ([block] * near if slotted else [sds((near,) + block.shape, BF16)]) + [TOKEN],
-            [SMEM, SMEM, ANY] + [VMEM] * (sum(blocks) + len(atts) + len(state)),
+            partial(backward_body, plan, chunk, [x[1] for x in sources], blocks, slotted),
+            ([block] * near if slotted else [sds((3 * hd, n), F32)]) + [TOKEN],
+            [VMEM, ANY] + [VMEM] * (1 + sum(blocks) + slotted * len(tail)),
             [
                 pltpu.VMEM((n3, 128), BF16),
                 pltpu.VMEM((128, n3), BF16),
@@ -591,11 +673,19 @@
                 pltpu.VMEM((64, n3), BF16),
                 pltpu.VMEM((hd, n3), BF16),
                 pltpu.VMEM((hd, n3), BF16),
-                pltpu.VMEM((3 * hd, n), F32),
-            ],
+            ]
+            + [grads] * slotted,
             flops=len(plan.tiles) * 5 * pair_flops,
             name=f"backward{chunk}",
-        )(*scalars, token, *received[sources[0][0]], *received[sources[1][0]], *atts, *state)
+        )(table, token, ld, *received[sources[0][0]], *received[sources[1][0]], *(tail if slotted else []))
+        if not slotted:
+            *out, token = kernel_call(
+                partial(finish_body, plan, chunk, len(atts)),
+                [sds((near,) + block.shape, BF16), TOKEN],
+                [VMEM, ANY] + [VMEM] * (1 + len(atts) + len(tail)),
+                [grads],
+                name=f"finish{chunk}",
+            )(table, token, *out, *atts, *tail)
         y = traded(out) if slotted else [swap(out[0])]
         scratch = [pltpu.VMEM((near,) + block.shape, BF16)] if slotted else []
         column = pl.BlockSpec((tok_rows, width), lambda i, c=chunk: (0, c))

time: 85.6 us -> 80.8 us (0.944)
  Pallas kernels: 43.6 us -> 39.5 us
  waiting for transfers between devices: 9.81 us -> 8.76 us
    pallas_call x2, Pallas kernels: 18.6 us -> 16.3 us  [body(): kernel_call(partial(backward_body, plan, chunk, [x[1] for x in sources],...]
    ppermute x18, starting transfers between devices: 20.3 us -> 22.2 us  [permuted(): return lax.ppermute(x, 'seq', [(i, target(i)) for i in range(device_count)])]
    all_to_all x2, starting transfers between devices: 10.6 us -> 9.15 us  [swap(): return lax.all_to_all(x, 'seq', 0, 0, tiled=True, axis_index_groups=groups)]
    pallas_call x2, Pallas kernels: 6.59 us -> 5.48 us  [body(): kernel_call(partial(last_body, plan, chunk, first, len(received[source]))...]
    ppermute x18, waiting for transfers between devices: 9.8 us -> 8.76 us  [permuted(): return lax.ppermute(x, 'seq', [(i, target(i)) for i in range(device_count)])]
    pallas_call x4 -> x6, Pallas kernels: 16.1 us -> 15.3 us  [the longest x2 4.93 us: body(): kernel_call(partial(pack_body, plan, [c for c, _ in pieces], near + 1 if...]
  transfers between devices with their start and end apart: 20 -> 20, of which waited for: 6 -> 6; matrix products, arithmetic and copies ran while one was open for 0% -> 0% of each run, Pallas kernels for 47% -> 44%
where the time goes in v4:
time: 80.8 us; the launch traced here: 80.5 us
  Pallas kernels  39.5 us (49%)
  starting transfers between devices  31.3 us (39%)
  waiting for transfers between devices  8.76 us (11%)
  between operations  0.86 us (1%)
    ppermute x18, starting transfers between devices, permuted(): return lax.ppermute(x, 'seq', [(i, target(i)) for i in range(device_count)])  22.2 us
    pallas_call x2, Pallas kernels, body(): kernel_call(partial(backward_body, plan, chunk, [x[1] for x in sources],...  16.3 us
    all_to_all x2, starting transfers between devices, swap(): return lax.all_to_all(x, 'seq', 0, 0, tiled=True, axis_index_groups=groups)  9.15 us
    ppermute x18, waiting for transfers between devices, permuted(): return lax.ppermute(x, 'seq', [(i, target(i)) for i in range(device_count)])  8.76 us
    pallas_call x2, Pallas kernels, body(): kernel_call(partial(last_body, plan, chunk, first, len(received[source]))...  5.48 us
    pallas_call x2, Pallas kernels, body(): kernel_call(partial(pack_body, plan, [c for c, _ in pieces], near + 1 if...  4.93 us
    pallas_call x1, Pallas kernels, body(): kernel_call(partial(make, len(near_x), 'both'), last_rows + [sums, TOKEN]...  4.31 us
    pallas_call x1, Pallas kernels, body(): kernel_call(partial(make, 0, 'sums'), [sums, TOKEN], [VMEM, ANY] + [VMEM]...  4.05 us
  transfers between devices with their start and end apart: 20, of which 6 were waited for; matrix products, arithmetic and copies ran while one was open for 0% of the time, Pallas kernels for 44%

profile of v4, /device:TPU:0, one launch (start us, length us, event | category | flops | bytes accessed | tf_op | source)
XLA Modules:
  0.0 80.5 jit_solution(15548762145085159064)
XLA Ops:
  0.7 2.7 %pack.2 = (bf16[8,144,256]{2,1,0:T(8,128)(2,1)}, f32[8,128]{1,0:T(8,128)}) custom-call(bf16[256,768]{1,0:T(8,128)(2,1)} %refs_0_.3, bf16[256,768]{1,0:T(8,128)(2,1)} %refs_1_.3, bf16[256,768]{1,0:T(8,128)(2,1)} %refs_2_.3), custom_call_target="tpu_custom_call" | custom-call | bytes 1048576 | tf_op jit(solution)/shard_map/pack/pallas_call | solution.py:576
  3.4 0.0 copy-start.2
  3.4 0.0 copy-start.3
  3.4 0.0 copy-start.4
  3.4 5.4 %all-to-all-start = ((bf16[8,144,256]{2,1,0:T(8,128)(2,1)}), bf16[8,144,256]{2,1,0:T(8,128)(2,1)S(1)}, u32[]{:S(2)}, u32[]{:S(2)}) async-start(bf16[8,144,256]{2,1,0:T(8,128)(2,1)} %get-tuple-element.60), calls=%async_computation | async-start | bytes 1179648 | tf_op jit(solution)/shard_map/all_to_all | solution.py:558
  8.8 2.3 %pack.3 = (bf16[240,256]{1,0:T(8,128)(2,1)S(1)}, bf16[240,256]{1,0:T(8,128)(2,1)S(1)}, bf16[240,256]{1,0:T(8,128)(2,1)S(1)}, bf16[240,256]{1,0:T(8,128)(2,1)S(1)...) custom-call(bf16[256,768]{1,0:T(8,128)(2,1)S(1)} %copy-done.1, ...), custom_call_target="tpu_custom_call" | custom-call | bytes 1048576 | tf_op jit(solution)/shard_map/pack/pallas_call | solution.py:576
  11.1 0.6 collective-permute-start
  11.7 1.7 %collective-permute-start.1 = (bf16[240,256]{1,0:T(8,128)(2,1)S(1)}, bf16[240,256]{1,0:T(8,128)(2,1)S(1)}, u32[]{:S(2)}, u32[]{:S(2)}) collective-permute-start(bf16[240,256]{1,0:T(8,128)(2,1)S(1)} %get-tuple-element.64), channel_id=1, source_target_pairs={{0,2},{1,3},{2,0},{3,1},{4,6},{5,7},{6,4},{7,5},{8,10},{9,11},{10,... | collective-permute-start | bytes 368648 | tf_op jit(solution)/shard_map/ppermute | solution.py:555
  13.3 1.7 %collective-permute-start.3 = (bf16[240,256]{1,0:T(8,128)(2,1)S(1)}, bf16[240,256]{1,0:T(8,128)(2,1)S(1)}, u32[]{:S(2)}, u32[]{:S(2)}) collective-permute-start(bf16[240,256]{1,0:T(8,128)(2,1)S(1)} %get-tuple-element.66), channel_id=1, source_target_pairs={{0,4},{1,5},{2,6},{3,7},{4,0},{5,1},{6,2},{7,3},{8,12},{9,13},{10,... | collective-permute-start | bytes 368648 | tf_op jit(solution)/shard_map/ppermute | solution.py:555
  15.0 0.1 collective-permute-start.4
  15.1 2.6 %collective-permute-start.5 = (bf16[240,256]{1,0:T(8,128)(2,1)S(1)}, bf16[240,256]{1,0:T(8,128)(2,1)S(1)}, u32[]{:S(2)}, u32[]{:S(2)}) collective-permute-start(bf16[240,256]{1,0:T(8,128)(2,1)S(1)} %get-tuple-element.68), channel_id=1, source_target_pairs={{0,6},{1,7},{2,4},{3,5},{4,2},{5,3},{6,0},{7,1},{8,14},{9,15},{10,... | collective-permute-start | bytes 368648 | tf_op jit(solution)/shard_map/ppermute | solution.py:555
  17.7 3.7 %collective-permute-done.1.refs_2_.rest_2_.refs_3_.refs_10_ = bf16[240,256]{1,0:T(8,128)(2,1)S(1)} collective-permute-done((bf16[240,256]{1,0:T(8,128)(2,1)S(1)}, bf16[240,256]{1,0:T(8,128)(2,1)S(1)}, u32[]{:S(2)}, u32[]{:S(2)}) %collective-permute-start.1) | collective-permute-done | bytes 122912 | tf_op jit(solution)/shard_map/ppermute | solution.py:555
  21.4 0.4 collective-permute-start.6
  21.8 4.3 %forward0.1 = (bf16[48,512]{1,0:T(8,128)(2,1)S(1)}, bf16[96,512]{1,0:T(8,128)(2,1)S(1)}, f32[64,2048]{1,0:T(8,128)S(1)}, f32[8,128]{1,0:T(8,128)S(1)}) custom-call(f32[16,128]{1,0:T(8,128)S(1)} %get-tuple-element.58.table, f32[8,128]{1,0:T(8,128)S(1)} %get-tuple-element.59.tok_in, bf16[8,144,256]{2,1,0:T(8,128)(2,1)S(1)} %all-to-all-done.refs_0_), custom_call_target="tpu_custom_call" | custom-call | bytes 1048576 | tf_op jit(solution)/shard_map/forward0/pallas_call | solution.py:613
  26.2 0.0 collective-permute-done.2.refs_3_.rest_3_.refs_4_.refs_11_
  26.2 2.6 %collective-permute-start.7 = (bf16[96,512]{1,0:T(8,128)(2,1)S(1)}, bf16[96,512]{1,0:T(8,128)(2,1)S(1)}, u32[]{:S(2)}, u32[]{:S(2)}) collective-permute-start(bf16[96,512]{1,0:T(8,128)(2,1)S(1)} %get-tuple-element.77.kv2), channel_id=1, source_target_pairs={{0,8},{1,9},{2,10},{3,11},{4,12},{5,13},{6,14},{7,15},{8,0},{9,1},... | collective-permute-start | bytes 294920 | tf_op jit(solution)/shard_map/ppermute | solution.py:555
  28.8 0.0 collective-permute-done.5.refs_6_.rest_6_.refs_7_.refs_14_
  28.8 0.4 collective-permute-done.6.refs_7_.rest_7_.refs_8_.refs_15_
  29.3 0.6 rows1.1
  29.9 2.7 %collective-permute-start.8 = (bf16[96,512]{1,0:T(8,128)(2,1)S(1)}, bf16[96,512]{1,0:T(8,128)(2,1)S(1)}, u32[]{:S(2)}, u32[]{:S(2)}) collective-permute-start(bf16[96,512]{1,0:T(8,128)(2,1)S(1)} %get-tuple-element.81.kv2), channel_id=1, source_target_pairs={{0,8},{1,9},{2,10},{3,11},{4,12},{5,13},{6,14},{7,15},{8,0},{9,1},... | collective-permute-start | bytes 294920 | tf_op jit(solution)/shard_map/ppermute | solution.py:555
  32.6 4.1 %sums1.1 = (f32[64,2048]{1,0:T(8,128)S(1)}, f32[8,128]{1,0:T(8,128)S(1)}) custom-call(f32[16,128]{1,0:T(8,128)S(1)} %get-tuple-element.58.table, f32[8,128]{1,0:T(8,128)S(1)} %get-tuple-element.70.tok_in, bf16[3072,128]{1,0:T(8,128)(2,1)S(1)} %get-tuple-element.71.refs_0_, bf16[128,3072]{1,0:T(8,128)(2,1)S(1)} %get-tuple-element.72.refs_1_, ...), custom_call_target="tpu_custom_call" | custom-call | bytes 1048576 | tf_op jit(solution)/shard_map/sums1/pallas_call | solution.py:630
  36.6 0.3 collective-permute-done.7.rest_8_
  36.9 2.6 %last0.1 = (bf16[48,2048]{1,0:T(8,128)(2,1)S(1)}, f32[8,2048]{1,0:T(8,128)S(1)}, f32[144,512]{1,0:T(8,128)S(1)}, bf16[1,96,512]{2,1,0:T(8,128)(2,1)S(1)}, f32[8,128]{1,0:T(8,128)S(1)}) custom-call(f32[16,128]{1,0:T(8,128)S(1)} %get-tuple-element.58.table, f32[8,128]{1,0:T(8,128)S(1)} %get-tuple-element.74.tok_in, f32[64,2048]{1,0:T(8,128)S(1)} %get-tuple-element.75.acc_ref, ...), custom_call_target="tpu_custom_call" | custom-call | flops 21474836480 | bytes 1048576 | tf_op jit(solution)/shard_map/last0/pallas_call | solution.py:641
  39.5 0.1 collective-permute-start.9
  39.7 0.0 collective-permute-done.8.rest_8_
  39.7 2.8 %last1.1 = (bf16[48,2048]{1,0:T(8,128)(2,1)S(1)}, f32[8,2048]{1,0:T(8,128)S(1)}, f32[144,512]{1,0:T(8,128)S(1)}, bf16[1,96,512]{2,1,0:T(8,128)(2,1)S(1)}, f32[8,128]{1,0:T(8,128)S(1)}) custom-call(f32[16,128]{1,0:T(8,128)S(1)} %get-tuple-element.58.table, f32[8,128]{1,0:T(8,128)S(1)} %get-tuple-element.78.tok_in, f32[64,2048]{1,0:T(8,128)S(1)} %get-tuple-element.79.acc_ref, ...), custom_call_target="tpu_custom_call" | custom-call | flops 21474836480 | bytes 1048576 | tf_op jit(solution)/shard_map/last1/pallas_call | solution.py:641
  42.5 2.9 %collective-permute-start.10 = (bf16[96,512]{1,0:T(8,128)(2,1)S(1)}, bf16[96,512]{1,0:T(8,128)(2,1)S(1)}, u32[]{:S(2)}, u32[]{:S(2)}) collective-permute-start(bf16[96,512]{1,0:T(8,128)(2,1)S(1)} %bitcast.3), channel_id=1, source_target_pairs={{0,8},{1,9},{2,10},{3,11},{4,12},{5,13},{6,14},{7,15},{8,0},{9,1},... | collective-permute-start | bytes 294920 | tf_op jit(solution)/shard_map/ppermute | solution.py:555
  45.5 8.0 %backward0.1 = (f32[144,2048]{1,0:T(8,128)S(1)}, f32[8,128]{1,0:T(8,128)S(1)}) custom-call(f32[16,128]{1,0:T(8,128)S(1)} %get-tuple-element.58.table, f32[8,128]{1,0:T(8,128)S(1)} %get-tuple-element.82.tok_in, f32[8,2048]{1,0:T(8,128)S(1)} %get-tuple-element.83.ld_ref, bf16[8,144,256]{2,1,0:T(8,128)(2,1)S(1)} %all-to-all-done.refs_0_, ...), custom_call_target="tpu_custom_call" | custom-call | flops 80530636800 | bytes 1048576 | tf_op jit(solution)/shard_map/backward0/pallas_call | solution.py:665
  53.5 0.0 collective-permute-done.9.refs_3_
  53.5 1.4 %finish0.1 = (bf16[8,240,256]{2,1,0:T(8,128)(2,1)}, f32[8,128]{1,0:T(8,128)S(1)}) custom-call(f32[16,128]{1,0:T(8,128)S(1)} %get-tuple-element.58.table, f32[8,128]{1,0:T(8,128)S(1)} %get-tuple-element.84.tok_in, f32[144,2048]{1,0:T(8,128)S(1)} %get-tuple-element.85.near_ref, bf16[48,2048]{1,0:T(8,128)(2,1)S(1)} %get-tuple-element.86.refs_0_, ...), custom_call_target="tpu_custom_call" | custom-call | bytes 1048576 | tf_op jit(solution)/shard_map/finish0/pallas_call | solution.py:682
  54.9 3.8 %all-to-all-start.1 = ((bf16[8,240,256]{2,1,0:T(8,128)(2,1)}), bf16[8,240,256]{2,1,0:T(8,128)(2,1)S(1)}, u32[]{:S(2)}, u32[]{:S(2)}) async-start(bf16[8,240,256]{2,1,0:T(8,128)(2,1)} %get-tuple-element.90), calls=%async_computation.1 | async-start | bytes 1966080 | tf_op jit(solution)/shard_map/all_to_all | solution.py:558
  58.7 0.0 collective-permute-done.10.refs_17_
  58.7 8.3 %backward1.1 = (bf16[144,256]{1,0:T(8,128)(2,1)S(1)}, bf16[144,256]{1,0:T(8,128)(2,1)S(1)}, bf16[144,256]{1,0:T(8,128)(2,1)S(1)}, bf16[144,256]{1,0:T(8,128)(2,1...) custom-call(f32[16,128]{1,0:T(8,128)S(1)} %get-tuple-element.58.tabl, ...), custom_call_target="tpu_custom_call" | custom-call | flops 80530636800 | bytes 1048576 | tf_op jit(solution)/shard_map/backward1/pallas_call | solution.py:665
  67.0 0.2 collective-permute-start.11
  67.2 1.7 %collective-permute-start.12 = (bf16[144,256]{1,0:T(8,128)(2,1)S(1)}, bf16[144,256]{1,0:T(8,128)(2,1)S(1)}, u32[]{:S(2)}, u32[]{:S(2)}) collective-permute-start(bf16[144,256]{1,0:T(8,128)(2,1)S(1)} %get-tuple-element.98), channel_id=1, source_target_pairs={{0,2},{1,3},{2,0},{3,1},{4,6},{5,7},{6,4},{7,5},{8,10},{9,11},{10,... | collective-permute-start | bytes 221192 | tf_op jit(solution)/shard_map/ppermute | solution.py:555
  68.9 0.0 collective-permute-start.13
  68.9 1.7 %collective-permute-start.14 = (bf16[144,256]{1,0:T(8,128)(2,1)S(1)}, bf16[144,256]{1,0:T(8,128)(2,1)S(1)}, u32[]{:S(2)}, u32[]{:S(2)}) collective-permute-start(bf16[144,256]{1,0:T(8,128)(2,1)S(1)} %get-tuple-element.100), channel_id=1, source_target_pairs={{0,4},{1,5},{2,6},{3,7},{4,0},{5,1},{6,2},{7,3},{8,12},{9,13},{10,... | collective-permute-start | bytes 221192 | tf_op jit(solution)/shard_map/ppermute | solution.py:555
  70.6 0.1 collective-permute-start.15
  70.7 0.0 collective-permute-done.11.refs_1_
  70.7 2.6 %collective-permute-start.16 = (bf16[144,256]{1,0:T(8,128)(2,1)S(1)}, bf16[144,256]{1,0:T(8,128)(2,1)S(1)}, u32[]{:S(2)}, u32[]{:S(2)}) collective-permute-start(bf16[144,256]{1,0:T(8,128)(2,1)S(1)} %get-tuple-element.102), channel_id=1, source_target_pairs={{0,6},{1,7},{2,4},{3,5},{4,2},{5,3},{6,0},{7,1},{8,14},{9,15},{10,... | collective-permute-start | bytes 221192 | tf_op jit(solution)/shard_map/ppermute | solution.py:555
  73.3 0.9 %collective-permute-done.12.refs_2_ = bf16[144,256]{1,0:T(8,128)(2,1)S(1)} collective-permute-done((bf16[144,256]{1,0:T(8,128)(2,1)S(1)}, bf16[144,256]{1,0:T(8,128)(2,1)S(1)}, u32[]{:S(2)}, u32[]{:S(2)}) %collective-permute-start.12) | collective-permute-done | bytes 73760 | tf_op jit(solution)/shard_map/ppermute | solution.py:555
  74.2 0.4 collective-permute-start.17
  74.6 0.0 all-to-all-done.1.refs_0_
  74.6 1.3 %unpack.2 = (bf16[256,768]{1,0:T(8,128)(2,1)}, bf16[256,768]{1,0:T(8,128)(2,1)}, bf16[256,768]{1,0:T(8,128)(2,1)}, bf16[256,768]{1,0:T(8,128)(2,1)}) custom-call(bf16[8,240,256]{2,1,0:T(8,128)(2,1)S(1)} %all-to-all-done.1.refs_0_), custom_call_target="tpu_custom_call" | custom-call | bytes 1048576 | tf_op jit(solution)/shard_map/unpack/pallas_call | solution.py:694
  75.9 0.0 collective-permute-done.13.refs_3_
  75.9 1.9 %collective-permute-done.16.refs_6_ = bf16[144,256]{1,0:T(8,128)(2,1)S(1)} collective-permute-done((bf16[144,256]{1,0:T(8,128)(2,1)S(1)}, bf16[144,256]{1,0:T(8,128)(2,1)S(1)}, u32[]{:S(2)}, u32[]{:S(2)}) %collective-permute-start.16) | collective-permute-done | bytes 73760 | tf_op jit(solution)/shard_map/ppermute | solution.py:555
  77.8 1.6 %collective-permute-done.17.refs_7_ = bf16[144,256]{1,0:T(8,128)(2,1)S(1)} collective-permute-done((bf16[144,256]{1,0:T(8,128)(2,1)S(1)}, bf16[144,256]{1,0:T(8,128)(2,1)S(1)}, u32[]{:S(2)}, u32[]{:S(2)}) %collective-permute-start.17) | collective-permute-done | bytes 73760 | tf_op jit(solution)/shard_map/ppermute | solution.py:555
  79.4 1.1 %unpack.3 = (bf16[256,768]{1,0:T(8,128)(2,1)}, bf16[256,768]{1,0:T(8,128)(2,1)}, bf16[256,768]{1,0:T(8,128)(2,1)}) custom-call(bf16[144,256]{1,0:T(8,128)(2,1)S(1)} %get-tuple-element.96.refs_0_, bf16[144,256]{1,0:T(8,128)(2,1)S(1)} %collective-permute-done.11.refs_1_, ...), custom_call_target="tpu_custom_call", output_to_operand_aliasing={{0}: (8, {}), {1}: (9, {}), {2}: (10, {})} | custom-call | bytes 1048576 | tf_op jit(solution)/shard_map/unpack/pallas_call | solution.py:704
  (18 shorter events, 0.0 us)
Async XLA Ops:
  0.6 8.1 %copy-start.1 = (bf16[256,768]{1,0:T(8,128)(2,1)S(1)}, bf16[256,768]{1,0:T(8,128)(2,1)}, u32[]{:S(2)}) copy-start(bf16[256,768]{1,0:T(8,128)(2,1)} %refs_0_.3) | copy-start | bytes 1179652
  0.6 8.1 %copy-start.6 = (s32[8]{0:T(128)S(1)}, s32[8]{0:T(128)}, u32[]{:S(2)}) copy-start(s32[8]{0:T(128)} %refs_5_.1) | copy-start | bytes 100
  0.7 8.1 %copy-start.5 = (s32[3,16]{1,0:T(4,128)S(1)}, s32[3,16]{1,0:T(4,128)}, u32[]{:S(2)}) copy-start(s32[3,16]{1,0:T(4,128)} %refs_6_.1) | copy-start | bytes 580
  0.7 8.1 %copy-start = (bf16[256,768]{1,0:T(8,128)(2,1)S(1)}, bf16[256,768]{1,0:T(8,128)(2,1)}, u32[]{:S(2)}) copy-start(bf16[256,768]{1,0:T(8,128)(2,1)} %refs_4_.1) | copy-start | bytes 1179652
  3.4 5.4 %copy-start.2 = (bf16[256,768]{1,0:T(8,128)(2,1)S(1)}, bf16[256,768]{1,0:T(8,128)(2,1)}, u32[]{:S(2)}) copy-start(bf16[256,768]{1,0:T(8,128)(2,1)} %refs_1_.3) | copy-start | bytes 1179652
  3.4 5.4 %copy-start.3 = (bf16[256,768]{1,0:T(8,128)(2,1)S(1)}, bf16[256,768]{1,0:T(8,128)(2,1)}, u32[]{:S(2)}) copy-start(bf16[256,768]{1,0:T(8,128)(2,1)} %refs_2_.3) | copy-start | bytes 1179652
  3.4 5.4 %copy-start.4 = (f32[8,128]{1,0:T(8,128)S(1)}, f32[8,128]{1,0:T(8,128)}, u32[]{:S(2)}) copy-start(f32[8,128]{1,0:T(8,128)} %get-tuple-element.57.refs_7_) | copy-start | bytes 12292
  3.4 18.5 %all-to-all-start = ((bf16[8,144,256]{2,1,0:T(8,128)(2,1)}), bf16[8,144,256]{2,1,0:T(8,128)(2,1)S(1)}, u32[]{:S(2)}, u32[]{:S(2)}) async-start(bf16[8,144,256]{2,1,0:T(8,128)(2,1)} %get-tuple-element.60), calls=%async_computation | async-start | bytes 1179648 | tf_op jit(solution)/shard_map/all_to_all | solution.py:558
  11.1 4.1 %collective-permute-start = (bf16[240,256]{1,0:T(8,128)(2,1)S(1)}, bf16[240,256]{1,0:T(8,128)(2,1)S(1)}, u32[]{:S(2)}, u32[]{:S(2)}) collective-permute-start(bf16[240,256]{1,0:T(8,128)(2,1)S(1)} %get-tuple-element.63), channel_id=1, source_target_pairs={{0,1},{1,0},{2,3},{3,2},{4,5},{5,4},{6,7},{7,6},{8,9},{9,8},{10,11... | collective-permute-start | bytes 368648 | tf_op jit(solution)/shard_map/ppermute | solution.py:555
  11.7 9.8 %collective-permute-start.1 = (bf16[240,256]{1,0:T(8,128)(2,1)S(1)}, bf16[240,256]{1,0:T(8,128)(2,1)S(1)}, u32[]{:S(2)}, u32[]{:S(2)}) collective-permute-start(bf16[240,256]{1,0:T(8,128)(2,1)S(1)} %get-tuple-element.64), channel_id=1, source_target_pairs={{0,2},{1,3},{2,0},{3,1},{4,6},{5,7},{6,4},{7,5},{8,10},{9,11},{10,... | collective-permute-start | bytes 368648 | tf_op jit(solution)/shard_map/ppermute | solution.py:555
  13.3 12.8 %collective-permute-start.2 = (bf16[240,256]{1,0:T(8,128)(2,1)S(1)}, bf16[240,256]{1,0:T(8,128)(2,1)S(1)}, u32[]{:S(2)}, u32[]{:S(2)}) collective-permute-start(bf16[240,256]{1,0:T(8,128)(2,1)S(1)} %get-tuple-element.65), channel_id=1, source_target_pairs={{0,3},{1,2},{2,1},{3,0},{4,7},{5,6},{6,5},{7,4},{8,11},{9,10},{10,... | collective-permute-start | bytes 368648 | tf_op jit(solution)/shard_map/ppermute | solution.py:555
  13.3 15.5 %collective-permute-start.3 = (bf16[240,256]{1,0:T(8,128)(2,1)S(1)}, bf16[240,256]{1,0:T(8,128)(2,1)S(1)}, u32[]{:S(2)}, u32[]{:S(2)}) collective-permute-start(bf16[240,256]{1,0:T(8,128)(2,1)S(1)} %get-tuple-element.66), channel_id=1, source_target_pairs={{0,4},{1,5},{2,6},{3,7},{4,0},{5,1},{6,2},{7,3},{8,12},{9,13},{10,... | collective-permute-start | bytes 368648 | tf_op jit(solution)/shard_map/ppermute | solution.py:555
  15.0 13.8 %collective-permute-start.4 = (bf16[240,256]{1,0:T(8,128)(2,1)S(1)}, bf16[240,256]{1,0:T(8,128)(2,1)S(1)}, u32[]{:S(2)}, u32[]{:S(2)}) collective-permute-start(bf16[240,256]{1,0:T(8,128)(2,1)S(1)} %get-tuple-element.67), channel_id=1, source_target_pairs={{0,5},{1,4},{2,7},{3,6},{4,1},{5,0},{6,3},{7,2},{8,13},{9,12},{10,... | collective-permute-start | bytes 368648 | tf_op jit(solution)/shard_map/ppermute | solution.py:555
  15.1 13.7 %collective-permute-start.5 = (bf16[240,256]{1,0:T(8,128)(2,1)S(1)}, bf16[240,256]{1,0:T(8,128)(2,1)S(1)}, u32[]{:S(2)}, u32[]{:S(2)}) collective-permute-start(bf16[240,256]{1,0:T(8,128)(2,1)S(1)} %get-tuple-element.68), channel_id=1, source_target_pairs={{0,6},{1,7},{2,4},{3,5},{4,2},{5,3},{6,0},{7,1},{8,14},{9,15},{10,... | collective-permute-start | bytes 368648 | tf_op jit(solution)/shard_map/ppermute | solution.py:555
  21.4 7.9 %collective-permute-start.6 = (bf16[240,256]{1,0:T(8,128)(2,1)S(1)}, bf16[240,256]{1,0:T(8,128)(2,1)S(1)}, u32[]{:S(2)}, u32[]{:S(2)}) collective-permute-start(bf16[240,256]{1,0:T(8,128)(2,1)S(1)} %get-tuple-element.69), channel_id=1, source_target_pairs={{0,7},{1,6},{2,5},{3,4},{4,3},{5,2},{6,1},{7,0},{8,15},{9,14},{10,... | collective-permute-start | bytes 368648 | tf_op jit(solution)/shard_map/ppermute | solution.py:555
  26.2 10.7 %collective-permute-start.7 = (bf16[96,512]{1,0:T(8,128)(2,1)S(1)}, bf16[96,512]{1,0:T(8,128)(2,1)S(1)}, u32[]{:S(2)}, u32[]{:S(2)}) collective-permute-start(bf16[96,512]{1,0:T(8,128)(2,1)S(1)} %get-tuple-element.77.kv2), channel_id=1, source_target_pairs={{0,8},{1,9},{2,10},{3,11},{4,12},{5,13},{6,14},{7,15},{8,0},{9,1},... | collective-permute-start | bytes 294920 | tf_op jit(solution)/shard_map/ppermute | solution.py:555
  29.9 9.8 %collective-permute-start.8 = (bf16[96,512]{1,0:T(8,128)(2,1)S(1)}, bf16[96,512]{1,0:T(8,128)(2,1)S(1)}, u32[]{:S(2)}, u32[]{:S(2)}) collective-permute-start(bf16[96,512]{1,0:T(8,128)(2,1)S(1)} %get-tuple-element.81.kv2), channel_id=1, source_target_pairs={{0,8},{1,9},{2,10},{3,11},{4,12},{5,13},{6,14},{7,15},{8,0},{9,1},... | collective-permute-start | bytes 294920 | tf_op jit(solution)/shard_map/ppermute | solution.py:555
  39.5 13.9 %collective-permute-start.9 = (bf16[96,512]{1,0:T(8,128)(2,1)S(1)}, bf16[96,512]{1,0:T(8,128)(2,1)S(1)}, u32[]{:S(2)}, u32[]{:S(2)}) collective-permute-start(bf16[96,512]{1,0:T(8,128)(2,1)S(1)} %bitcast.2), channel_id=1, source_target_pairs={{0,8},{1,9},{2,10},{3,11},{4,12},{5,13},{6,14},{7,15},{8,0},{9,1},... | collective-permute-start | bytes 294920 | tf_op jit(solution)/shard_map/ppermute | solution.py:555
  42.5 16.2 %collective-permute-start.10 = (bf16[96,512]{1,0:T(8,128)(2,1)S(1)}, bf16[96,512]{1,0:T(8,128)(2,1)S(1)}, u32[]{:S(2)}, u32[]{:S(2)}) collective-permute-start(bf16[96,512]{1,0:T(8,128)(2,1)S(1)} %bitcast.3), channel_id=1, source_target_pairs={{0,8},{1,9},{2,10},{3,11},{4,12},{5,13},{6,14},{7,15},{8,0},{9,1},... | collective-permute-start | bytes 294920 | tf_op jit(solution)/shard_map/ppermute | solution.py:555
  54.9 19.7 %all-to-all-start.1 = ((bf16[8,240,256]{2,1,0:T(8,128)(2,1)}), bf16[8,240,256]{2,1,0:T(8,128)(2,1)S(1)}, u32[]{:S(2)}, u32[]{:S(2)}) async-start(bf16[8,240,256]{2,1,0:T(8,128)(2,1)} %get-tuple-element.90), calls=%async_computation.1 | async-start | bytes 1966080 | tf_op jit(solution)/shard_map/all_to_all | solution.py:558
  67.0 3.7 %collective-permute-start.11 = (bf16[144,256]{1,0:T(8,128)(2,1)S(1)}, bf16[144,256]{1,0:T(8,128)(2,1)S(1)}, u32[]{:S(2)}, u32[]{:S(2)}) collective-permute-start(bf16[144,256]{1,0:T(8,128)(2,1)S(1)} %get-tuple-element.97), channel_id=1, source_target_pairs={{0,1},{1,0},{2,3},{3,2},{4,5},{5,4},{6,7},{7,6},{8,9},{9,8},{10,11... | collective-permute-start | bytes 221192 | tf_op jit(solution)/shard_map/ppermute | solution.py:555
  67.2 7.0 %collective-permute-start.12 = (bf16[144,256]{1,0:T(8,128)(2,1)S(1)}, bf16[144,256]{1,0:T(8,128)(2,1)S(1)}, u32[]{:S(2)}, u32[]{:S(2)}) collective-permute-start(bf16[144,256]{1,0:T(8,128)(2,1)S(1)} %get-tuple-element.98), channel_id=1, source_target_pairs={{0,2},{1,3},{2,0},{3,1},{4,6},{5,7},{6,4},{7,5},{8,10},{9,11},{10,... | collective-permute-start | bytes 221192 | tf_op jit(solution)/shard_map/ppermute | solution.py:555
  68.9 7.0 %collective-permute-start.13 = (bf16[144,256]{1,0:T(8,128)(2,1)S(1)}, bf16[144,256]{1,0:T(8,128)(2,1)S(1)}, u32[]{:S(2)}, u32[]{:S(2)}) collective-permute-start(bf16[144,256]{1,0:T(8,128)(2,1)S(1)} %get-tuple-element.99), channel_id=1, source_target_pairs={{0,3},{1,2},{2,1},{3,0},{4,7},{5,6},{6,5},{7,4},{8,11},{9,10},{10,... | collective-permute-start | bytes 221192 | tf_op jit(solution)/shard_map/ppermute | solution.py:555
  68.9 7.0 %collective-permute-start.14 = (bf16[144,256]{1,0:T(8,128)(2,1)S(1)}, bf16[144,256]{1,0:T(8,128)(2,1)S(1)}, u32[]{:S(2)}, u32[]{:S(2)}) collective-permute-start(bf16[144,256]{1,0:T(8,128)(2,1)S(1)} %get-tuple-element.100), channel_id=1, source_target_pairs={{0,4},{1,5},{2,6},{3,7},{4,0},{5,1},{6,2},{7,3},{8,12},{9,13},{10,... | collective-permute-start | bytes 221192 | tf_op jit(solution)/shard_map/ppermute | solution.py:555
  70.6 5.3 %collective-permute-start.15 = (bf16[144,256]{1,0:T(8,128)(2,1)S(1)}, bf16[144,256]{1,0:T(8,128)(2,1)S(1)}, u32[]{:S(2)}, u32[]{:S(2)}) collective-permute-start(bf16[144,256]{1,0:T(8,128)(2,1)S(1)} %get-tuple-element.101), channel_id=1, source_target_pairs={{0,5},{1,4},{2,7},{3,6},{4,1},{5,0},{6,3},{7,2},{8,13},{9,12},{10,... | collective-permute-start | bytes 221192 | tf_op jit(solution)/shard_map/ppermute | solution.py:555
  70.7 7.1 %collective-permute-start.16 = (bf16[144,256]{1,0:T(8,128)(2,1)S(1)}, bf16[144,256]{1,0:T(8,128)(2,1)S(1)}, u32[]{:S(2)}, u32[]{:S(2)}) collective-permute-start(bf16[144,256]{1,0:T(8,128)(2,1)S(1)} %get-tuple-element.102), channel_id=1, source_target_pairs={{0,6},{1,7},{2,4},{3,5},{4,2},{5,3},{6,0},{7,1},{8,14},{9,15},{10,... | collective-permute-start | bytes 221192 | tf_op jit(solution)/shard_map/ppermute | solution.py:555
  74.2 5.2 %collective-permute-start.17 = (bf16[144,256]{1,0:T(8,128)(2,1)S(1)}, bf16[144,256]{1,0:T(8,128)(2,1)S(1)}, u32[]{:S(2)}, u32[]{:S(2)}) collective-permute-start(bf16[144,256]{1,0:T(8,128)(2,1)S(1)} %get-tuple-element.103), channel_id=1, source_target_pairs={{0,7},{1,6},{2,5},{3,4},{4,3},{5,2},{6,1},{7,0},{8,15},{9,14},{10,... | collective-permute-start | bytes 221192 | tf_op jit(solution)/shard_map/ppermute | solution.py:555

commit v5 on v4

--- a/solution.py
+++ b/solution.py
@@ -529,7 +529,7 @@
     if slotted:
         y_ref, outs = refs[-1], refs[-1 - len(places) : -1]
         for j in range(plan.near):
-            y_ref[near_index(plan) ^ j] = refs[j][...]
+            y_ref[near_index(plan) ^ j] = refs[plan.near - 1 - j][...]
     else:
         y_ref, outs = refs[0], refs[-len(places) :]
     hd, width = plan.hd, plan.near * plan.hd
@@ -561,7 +561,7 @@
         return permuted(x, lambda i: (i + steps * near) % device_count)
 
     def traded(slots):
-        return [slots[0]] + [permuted(slots[j], lambda i, j=j: i ^ j) for j in range(near - 1, 0, -1)][::-1]
+        return [slots[0]] + [permuted(slots[j], lambda i, j=j: i ^ j) for j in range(1, near)]
 
     exchanges = [[(c, i) for i in range(3)] for c in range(chunks)]
     for c in range(chunks):
@@ -686,7 +686,7 @@
                 [grads],
                 name=f"finish{chunk}",
             )(table, token, *out, *atts, *tail)
-        y = traded(out) if slotted else [swap(out[0])]
+        y = traded(out)[::-1] if slotted else [swap(out[0])]
         scratch = [pltpu.VMEM((near,) + block.shape, BF16)] if slotted else []
         column = pl.BlockSpec((tok_rows, width), lambda i, c=chunk: (0, c))
         specs = [pl.BlockSpec(v.shape, lambda i, r=len(v.shape): (0,) * r) for v in y]

time: 80.8 us -> 80.8 us (level)
  transfers between devices with their start and end apart: 20 -> 20, of which waited for: 6 -> 7; matrix products, arithmetic and copies ran while one was open for 0% -> 0% of each run, Pallas kernels for 44% -> 44%
where the time goes in v5:
time: 80.8 us; the launch traced here: 80.5 us
  Pallas kernels  39.5 us (49%)
  starting transfers between devices  31 us (38%)
  waiting for transfers between devices  9.07 us (11%)
  between operations  0.86 us (1%)
    ppermute x18, starting transfers between devices, permuted(): return lax.ppermute(x, 'seq', [(i, target(i)) for i in range(device_count)])  21.9 us
    pallas_call x2, Pallas kernels, body(): kernel_call(partial(backward_body, plan, chunk, [x[1] for x in sources],...  16.3 us
    all_to_all x2, starting transfers between devices, swap(): return lax.all_to_all(x, 'seq', 0, 0, tiled=True, axis_index_groups=groups)  9.15 us
    ppermute x18, waiting for transfers between devices, permuted(): return lax.ppermute(x, 'seq', [(i, target(i)) for i in range(device_count)])  9.07 us
    pallas_call x2, Pallas kernels, body(): kernel_call(partial(last_body, plan, chunk, first, len(received[source]))...  5.49 us
    pallas_call x2, Pallas kernels, body(): kernel_call(partial(pack_body, plan, [c for c, _ in pieces], near + 1 if...  4.93 us
    pallas_call x1, Pallas kernels, body(): kernel_call(partial(make, len(near_x), 'both'), last_rows + [sums, TOKEN]...  4.31 us
    pallas_call x1, Pallas kernels, body(): kernel_call(partial(make, 0, 'sums'), [sums, TOKEN], [VMEM, ANY] + [VMEM]...  4.05 us
  transfers between devices with their start and end apart: 20, of which 7 were waited for; matrix products, arithmetic and copies ran while one was open for 0% of the time, Pallas kernels for 44%

profile of v5, /device:TPU:0, one launch (start us, length us, event | category | flops | bytes accessed | tf_op | source)
XLA Modules:
  0.0 80.5 jit_solution(3006456959843869483)
XLA Ops:
  0.7 2.7 %pack.2 = (bf16[8,144,256]{2,1,0:T(8,128)(2,1)}, f32[8,128]{1,0:T(8,128)}) custom-call(bf16[256,768]{1,0:T(8,128)(2,1)} %refs_0_.3, bf16[256,768]{1,0:T(8,128)(2,1)} %refs_1_.3, bf16[256,768]{1,0:T(8,128)(2,1)} %refs_2_.3), custom_call_target="tpu_custom_call" | custom-call | bytes 1048576 | tf_op jit(solution)/shard_map/pack/pallas_call | solution.py:576
  3.4 0.0 copy-start.2
  3.4 0.0 copy-start.3
  3.4 0.0 copy-start.4
  3.4 5.4 %all-to-all-start = ((bf16[8,144,256]{2,1,0:T(8,128)(2,1)}), bf16[8,144,256]{2,1,0:T(8,128)(2,1)S(1)}, u32[]{:S(2)}, u32[]{:S(2)}) async-start(bf16[8,144,256]{2,1,0:T(8,128)(2,1)} %get-tuple-element.60), calls=%async_computation | async-start | bytes 1179648 | tf_op jit(solution)/shard_map/all_to_all | solution.py:558
  8.8 2.3 %pack.3 = (bf16[240,256]{1,0:T(8,128)(2,1)S(1)}, bf16[240,256]{1,0:T(8,128)(2,1)S(1)}, bf16[240,256]{1,0:T(8,128)(2,1)S(1)}, bf16[240,256]{1,0:T(8,128)(2,1)S(1)...) custom-call(bf16[256,768]{1,0:T(8,128)(2,1)S(1)} %copy-done.1, ...), custom_call_target="tpu_custom_call" | custom-call | bytes 1048576 | tf_op jit(solution)/shard_map/pack/pallas_call | solution.py:576
  11.1 0.6 collective-permute-start
  11.7 1.7 %collective-permute-start.1 = (bf16[240,256]{1,0:T(8,128)(2,1)S(1)}, bf16[240,256]{1,0:T(8,128)(2,1)S(1)}, u32[]{:S(2)}, u32[]{:S(2)}) collective-permute-start(bf16[240,256]{1,0:T(8,128)(2,1)S(1)} %get-tuple-element.64), channel_id=1, source_target_pairs={{0,2},{1,3},{2,0},{3,1},{4,6},{5,7},{6,4},{7,5},{8,10},{9,11},{10,... | collective-permute-start | bytes 368648 | tf_op jit(solution)/shard_map/ppermute | solution.py:555
  13.3 0.0 collective-permute-start.2
  13.3 1.7 %collective-permute-start.3 = (bf16[240,256]{1,0:T(8,128)(2,1)S(1)}, bf16[240,256]{1,0:T(8,128)(2,1)S(1)}, u32[]{:S(2)}, u32[]{:S(2)}) collective-permute-start(bf16[240,256]{1,0:T(8,128)(2,1)S(1)} %get-tuple-element.66), channel_id=1, source_target_pairs={{0,4},{1,5},{2,6},{3,7},{4,0},{5,1},{6,2},{7,3},{8,12},{9,13},{10,... | collective-permute-start | bytes 368648 | tf_op jit(solution)/shard_map/ppermute | solution.py:555
  15.0 0.1 collective-permute-start.4
  15.1 0.0 collective-permute-done.refs_1_.rest_1_.refs_2_.refs_9_
  15.1 2.6 %collective-permute-start.5 = (bf16[240,256]{1,0:T(8,128)(2,1)S(1)}, bf16[240,256]{1,0:T(8,128)(2,1)S(1)}, u32[]{:S(2)}, u32[]{:S(2)}) collective-permute-start(bf16[240,256]{1,0:T(8,128)(2,1)S(1)} %get-tuple-element.68), channel_id=1, source_target_pairs={{0,6},{1,7},{2,4},{3,5},{4,2},{5,3},{6,0},{7,1},{8,14},{9,15},{10,... | collective-permute-start | bytes 368648 | tf_op jit(solution)/shard_map/ppermute | solution.py:555
  17.7 3.7 %collective-permute-done.1.refs_2_.rest_2_.refs_3_.refs_10_ = bf16[240,256]{1,0:T(8,128)(2,1)S(1)} collective-permute-done((bf16[240,256]{1,0:T(8,128)(2,1)S(1)}, bf16[240,256]{1,0:T(8,128)(2,1)S(1)}, u32[]{:S(2)}, u32[]{:S(2)}) %collective-permute-start.1) | collective-permute-done | bytes 122912 | tf_op jit(solution)/shard_map/ppermute | solution.py:555
  21.4 0.4 collective-permute-start.6
  21.8 4.3 %forward0.1 = (bf16[48,512]{1,0:T(8,128)(2,1)S(1)}, bf16[96,512]{1,0:T(8,128)(2,1)S(1)}, f32[64,2048]{1,0:T(8,128)S(1)}, f32[8,128]{1,0:T(8,128)S(1)}) custom-call(f32[16,128]{1,0:T(8,128)S(1)} %get-tuple-element.58.table, f32[8,128]{1,0:T(8,128)S(1)} %get-tuple-element.59.tok_in, bf16[8,144,256]{2,1,0:T(8,128)(2,1)S(1)} %all-to-all-done.refs_0_), custom_call_target="tpu_custom_call" | custom-call | bytes 1048576 | tf_op jit(solution)/shard_map/forward0/pallas_call | solution.py:613
  26.2 2.7 %collective-permute-start.7 = (bf16[96,512]{1,0:T(8,128)(2,1)S(1)}, bf16[96,512]{1,0:T(8,128)(2,1)S(1)}, u32[]{:S(2)}, u32[]{:S(2)}) collective-permute-start(bf16[96,512]{1,0:T(8,128)(2,1)S(1)} %get-tuple-element.77.kv2), channel_id=1, source_target_pairs={{0,8},{1,9},{2,10},{3,11},{4,12},{5,13},{6,14},{7,15},{8,0},{9,1},... | collective-permute-start | bytes 294920 | tf_op jit(solution)/shard_map/ppermute | solution.py:555
  28.8 0.0 collective-permute-done.4.refs_5_.rest_5_.refs_6_.refs_13_
  28.8 0.0 collective-permute-done.5.refs_6_.rest_6_.refs_7_.refs_14_
  28.8 0.4 collective-permute-done.6.refs_7_.rest_7_.refs_8_.refs_15_
  29.3 0.6 rows1.1
  29.9 2.7 %collective-permute-start.8 = (bf16[96,512]{1,0:T(8,128)(2,1)S(1)}, bf16[96,512]{1,0:T(8,128)(2,1)S(1)}, u32[]{:S(2)}, u32[]{:S(2)}) collective-permute-start(bf16[96,512]{1,0:T(8,128)(2,1)S(1)} %get-tuple-element.81.kv2), channel_id=1, source_target_pairs={{0,8},{1,9},{2,10},{3,11},{4,12},{5,13},{6,14},{7,15},{8,0},{9,1},... | collective-permute-start | bytes 294920 | tf_op jit(solution)/shard_map/ppermute | solution.py:555
  32.6 4.0 %sums1.1 = (f32[64,2048]{1,0:T(8,128)S(1)}, f32[8,128]{1,0:T(8,128)S(1)}) custom-call(f32[16,128]{1,0:T(8,128)S(1)} %get-tuple-element.58.table, f32[8,128]{1,0:T(8,128)S(1)} %get-tuple-element.70.tok_in, bf16[3072,128]{1,0:T(8,128)(2,1)S(1)} %get-tuple-element.71.refs_0_, bf16[128,3072]{1,0:T(8,128)(2,1)S(1)} %get-tuple-element.72.refs_1_, ...), custom_call_target="tpu_custom_call" | custom-call | bytes 1048576 | tf_op jit(solution)/shard_map/sums1/pallas_call | solution.py:630
  36.6 0.3 collective-permute-done.7.rest_8_
  36.9 2.6 %last0.1 = (bf16[48,2048]{1,0:T(8,128)(2,1)S(1)}, f32[8,2048]{1,0:T(8,128)S(1)}, f32[144,512]{1,0:T(8,128)S(1)}, bf16[1,96,512]{2,1,0:T(8,128)(2,1)S(1)}, f32[8,128]{1,0:T(8,128)S(1)}) custom-call(f32[16,128]{1,0:T(8,128)S(1)} %get-tuple-element.58.table, f32[8,128]{1,0:T(8,128)S(1)} %get-tuple-element.74.tok_in, f32[64,2048]{1,0:T(8,128)S(1)} %get-tuple-element.75.acc_ref, ...), custom_call_target="tpu_custom_call" | custom-call | flops 21474836480 | bytes 1048576 | tf_op jit(solution)/shard_map/last0/pallas_call | solution.py:641
  39.5 0.1 collective-permute-start.9
  39.7 0.0 collective-permute-done.8.rest_8_
  39.7 2.8 %last1.1 = (bf16[48,2048]{1,0:T(8,128)(2,1)S(1)}, f32[8,2048]{1,0:T(8,128)S(1)}, f32[144,512]{1,0:T(8,128)S(1)}, bf16[1,96,512]{2,1,0:T(8,128)(2,1)S(1)}, f32[8,128]{1,0:T(8,128)S(1)}) custom-call(f32[16,128]{1,0:T(8,128)S(1)} %get-tuple-element.58.table, f32[8,128]{1,0:T(8,128)S(1)} %get-tuple-element.78.tok_in, f32[64,2048]{1,0:T(8,128)S(1)} %get-tuple-element.79.acc_ref, ...), custom_call_target="tpu_custom_call" | custom-call | flops 21474836480 | bytes 1048576 | tf_op jit(solution)/shard_map/last1/pallas_call | solution.py:641
  42.5 2.9 %collective-permute-start.10 = (bf16[96,512]{1,0:T(8,128)(2,1)S(1)}, bf16[96,512]{1,0:T(8,128)(2,1)S(1)}, u32[]{:S(2)}, u32[]{:S(2)}) collective-permute-start(bf16[96,512]{1,0:T(8,128)(2,1)S(1)} %bitcast.3), channel_id=1, source_target_pairs={{0,8},{1,9},{2,10},{3,11},{4,12},{5,13},{6,14},{7,15},{8,0},{9,1},... | collective-permute-start | bytes 294920 | tf_op jit(solution)/shard_map/ppermute | solution.py:555
  45.5 8.0 %backward0.1 = (f32[144,2048]{1,0:T(8,128)S(1)}, f32[8,128]{1,0:T(8,128)S(1)}) custom-call(f32[16,128]{1,0:T(8,128)S(1)} %get-tuple-element.58.table, f32[8,128]{1,0:T(8,128)S(1)} %get-tuple-element.82.tok_in, f32[8,2048]{1,0:T(8,128)S(1)} %get-tuple-element.83.ld_ref, bf16[8,144,256]{2,1,0:T(8,128)(2,1)S(1)} %all-to-all-done.refs_0_, ...), custom_call_target="tpu_custom_call" | custom-call | flops 80530636800 | bytes 1048576 | tf_op jit(solution)/shard_map/backward0/pallas_call | solution.py:665
  53.5 1.4 %finish0.1 = (bf16[8,240,256]{2,1,0:T(8,128)(2,1)}, f32[8,128]{1,0:T(8,128)S(1)}) custom-call(f32[16,128]{1,0:T(8,128)S(1)} %get-tuple-element.58.table, f32[8,128]{1,0:T(8,128)S(1)} %get-tuple-element.84.tok_in, f32[144,2048]{1,0:T(8,128)S(1)} %get-tuple-element.85.near_ref, bf16[48,2048]{1,0:T(8,128)(2,1)S(1)} %get-tuple-element.86.refs_0_, ...), custom_call_target="tpu_custom_call" | custom-call | bytes 1048576 | tf_op jit(solution)/shard_map/finish0/pallas_call | solution.py:682
  54.9 3.8 %all-to-all-start.1 = ((bf16[8,240,256]{2,1,0:T(8,128)(2,1)}), bf16[8,240,256]{2,1,0:T(8,128)(2,1)S(1)}, u32[]{:S(2)}, u32[]{:S(2)}) async-start(bf16[8,240,256]{2,1,0:T(8,128)(2,1)} %get-tuple-element.90), calls=%async_computation.1 | async-start | bytes 1966080 | tf_op jit(solution)/shard_map/all_to_all | solution.py:558
  58.7 8.3 %backward1.1 = (bf16[144,256]{1,0:T(8,128)(2,1)S(1)}, bf16[144,256]{1,0:T(8,128)(2,1)S(1)}, bf16[144,256]{1,0:T(8,128)(2,1)S(1)}, bf16[144,256]{1,0:T(8,128)(2,1...) custom-call(f32[16,128]{1,0:T(8,128)S(1)} %get-tuple-element.58.tabl, ...), custom_call_target="tpu_custom_call" | custom-call | flops 80530636800 | bytes 1048576 | tf_op jit(solution)/shard_map/backward1/pallas_call | solution.py:665
  67.0 2.4 %collective-permute-start.11 = (bf16[144,256]{1,0:T(8,128)(2,1)S(1)}, bf16[144,256]{1,0:T(8,128)(2,1)S(1)}, u32[]{:S(2)}, u32[]{:S(2)}) collective-permute-start(bf16[144,256]{1,0:T(8,128)(2,1)S(1)} %get-tuple-element.96), channel_id=1, source_target_pairs={{0,7},{1,6},{2,5},{3,4},{4,3},{5,2},{6,1},{7,0},{8,15},{9,14},{10,... | collective-permute-start | bytes 221192 | tf_op jit(solution)/shard_map/ppermute | solution.py:555
  69.4 0.3 collective-permute-start.12
  69.7 1.4 %collective-permute-start.13 = (bf16[144,256]{1,0:T(8,128)(2,1)S(1)}, bf16[144,256]{1,0:T(8,128)(2,1)S(1)}, u32[]{:S(2)}, u32[]{:S(2)}) collective-permute-start(bf16[144,256]{1,0:T(8,128)(2,1)S(1)} %get-tuple-element.98), channel_id=1, source_target_pairs={{0,5},{1,4},{2,7},{3,6},{4,1},{5,0},{6,3},{7,2},{8,13},{9,12},{10,... | collective-permute-start | bytes 221192 | tf_op jit(solution)/shard_map/ppermute | solution.py:555
  71.1 0.4 collective-permute-start.14
  71.5 1.4 %collective-permute-start.15 = (bf16[144,256]{1,0:T(8,128)(2,1)S(1)}, bf16[144,256]{1,0:T(8,128)(2,1)S(1)}, u32[]{:S(2)}, u32[]{:S(2)}) collective-permute-start(bf16[144,256]{1,0:T(8,128)(2,1)S(1)} %get-tuple-element.100), channel_id=1, source_target_pairs={{0,3},{1,2},{2,1},{3,0},{4,7},{5,6},{6,5},{7,4},{8,11},{9,10},{10,... | collective-permute-start | bytes 221192 | tf_op jit(solution)/shard_map/ppermute | solution.py:555
  72.9 1.3 %collective-permute-done.11.refs_0_ = bf16[144,256]{1,0:T(8,128)(2,1)S(1)} collective-permute-done((bf16[144,256]{1,0:T(8,128)(2,1)S(1)}, bf16[144,256]{1,0:T(8,128)(2,1)S(1)}, u32[]{:S(2)}, u32[]{:S(2)}) %collective-permute-start.11) | collective-permute-done | bytes 73760 | tf_op jit(solution)/shard_map/ppermute | solution.py:555
  74.2 0.6 collective-permute-start.16
  74.7 2.0 %collective-permute-done.12.refs_1_ = bf16[144,256]{1,0:T(8,128)(2,1)S(1)} collective-permute-done((bf16[144,256]{1,0:T(8,128)(2,1)S(1)}, bf16[144,256]{1,0:T(8,128)(2,1)S(1)}, u32[]{:S(2)}, u32[]{:S(2)}) %collective-permute-start.12) | collective-permute-done | bytes 73760 | tf_op jit(solution)/shard_map/ppermute | solution.py:555
  76.7 0.0 collective-permute-start.17
  76.7 0.0 all-to-all-done.1.refs_0_
  76.7 1.3 %unpack.2 = (bf16[256,768]{1,0:T(8,128)(2,1)}, bf16[256,768]{1,0:T(8,128)(2,1)}, bf16[256,768]{1,0:T(8,128)(2,1)}, bf16[256,768]{1,0:T(8,128)(2,1)}) custom-call(bf16[8,240,256]{2,1,0:T(8,128)(2,1)S(1)} %all-to-all-done.1.refs_0_), custom_call_target="tpu_custom_call" | custom-call | bytes 1048576 | tf_op jit(solution)/shard_map/unpack/pallas_call | solution.py:694
  77.9 0.0 collective-permute-done.13.refs_2_
  77.9 0.5 collective-permute-done.14.refs_3_
  78.5 0.9 %collective-permute-done.16.refs_5_ = bf16[144,256]{1,0:T(8,128)(2,1)S(1)} collective-permute-done((bf16[144,256]{1,0:T(8,128)(2,1)S(1)}, bf16[144,256]{1,0:T(8,128)(2,1)S(1)}, u32[]{:S(2)}, u32[]{:S(2)}) %collective-permute-start.16) | collective-permute-done | bytes 73760 | tf_op jit(solution)/shard_map/ppermute | solution.py:555
  79.4 1.1 %unpack.3 = (bf16[256,768]{1,0:T(8,128)(2,1)}, bf16[256,768]{1,0:T(8,128)(2,1)}, bf16[256,768]{1,0:T(8,128)(2,1)}) custom-call(bf16[144,256]{1,0:T(8,128)(2,1)S(1)} %collective-permute-done.11.refs_0_, bf16[144,256]{1,0:T(8,128)(2,1)S(1)} %collective-permute-done.12.refs_1_, ...), custom_call_target="tpu_custom_call", output_to_operand_aliasing={{0}: (8, {}), {1}: (9, {}), {2}: (10, {})} | custom-call | bytes 1048576 | tf_op jit(solution)/shard_map/unpack/pallas_call | solution.py:704
  (18 shorter events, 0.0 us)
Async XLA Ops:
  0.6 8.1 %copy-start.1 = (bf16[256,768]{1,0:T(8,128)(2,1)S(1)}, bf16[256,768]{1,0:T(8,128)(2,1)}, u32[]{:S(2)}) copy-start(bf16[256,768]{1,0:T(8,128)(2,1)} %refs_0_.3) | copy-start | bytes 1179652
  0.6 8.1 %copy-start.6 = (s32[8]{0:T(128)S(1)}, s32[8]{0:T(128)}, u32[]{:S(2)}) copy-start(s32[8]{0:T(128)} %refs_5_.1) | copy-start | bytes 100
  0.7 8.1 %copy-start.5 = (s32[3,16]{1,0:T(4,128)S(1)}, s32[3,16]{1,0:T(4,128)}, u32[]{:S(2)}) copy-start(s32[3,16]{1,0:T(4,128)} %refs_6_.1) | copy-start | bytes 580
  0.7 8.1 %copy-start = (bf16[256,768]{1,0:T(8,128)(2,1)S(1)}, bf16[256,768]{1,0:T(8,128)(2,1)}, u32[]{:S(2)}) copy-start(bf16[256,768]{1,0:T(8,128)(2,1)} %refs_4_.1) | copy-start | bytes 1179652
  3.4 5.4 %copy-start.2 = (bf16[256,768]{1,0:T(8,128)(2,1)S(1)}, bf16[256,768]{1,0:T(8,128)(2,1)}, u32[]{:S(2)}) copy-start(bf16[256,768]{1,0:T(8,128)(2,1)} %refs_1_.3) | copy-start | bytes 1179652
  3.4 5.4 %copy-start.3 = (bf16[256,768]{1,0:T(8,128)(2,1)S(1)}, bf16[256,768]{1,0:T(8,128)(2,1)}, u32[]{:S(2)}) copy-start(bf16[256,768]{1,0:T(8,128)(2,1)} %refs_2_.3) | copy-start | bytes 1179652
  3.4 5.4 %copy-start.4 = (f32[8,128]{1,0:T(8,128)S(1)}, f32[8,128]{1,0:T(8,128)}, u32[]{:S(2)}) copy-start(f32[8,128]{1,0:T(8,128)} %get-tuple-element.57.refs_7_) | copy-start | bytes 12292
  3.4 18.5 %all-to-all-start = ((bf16[8,144,256]{2,1,0:T(8,128)(2,1)}), bf16[8,144,256]{2,1,0:T(8,128)(2,1)S(1)}, u32[]{:S(2)}, u32[]{:S(2)}) async-start(bf16[8,144,256]{2,1,0:T(8,128)(2,1)} %get-tuple-element.60), calls=%async_computation | async-start | bytes 1179648 | tf_op jit(solution)/shard_map/all_to_all | solution.py:558
  11.1 4.1 %collective-permute-start = (bf16[240,256]{1,0:T(8,128)(2,1)S(1)}, bf16[240,256]{1,0:T(8,128)(2,1)S(1)}, u32[]{:S(2)}, u32[]{:S(2)}) collective-permute-start(bf16[240,256]{1,0:T(8,128)(2,1)S(1)} %get-tuple-element.63), channel_id=1, source_target_pairs={{0,1},{1,0},{2,3},{3,2},{4,5},{5,4},{6,7},{7,6},{8,9},{9,8},{10,11... | collective-permute-start | bytes 368648 | tf_op jit(solution)/shard_map/ppermute | solution.py:555
  11.7 9.8 %collective-permute-start.1 = (bf16[240,256]{1,0:T(8,128)(2,1)S(1)}, bf16[240,256]{1,0:T(8,128)(2,1)S(1)}, u32[]{:S(2)}, u32[]{:S(2)}) collective-permute-start(bf16[240,256]{1,0:T(8,128)(2,1)S(1)} %get-tuple-element.64), channel_id=1, source_target_pairs={{0,2},{1,3},{2,0},{3,1},{4,6},{5,7},{6,4},{7,5},{8,10},{9,11},{10,... | collective-permute-start | bytes 368648 | tf_op jit(solution)/shard_map/ppermute | solution.py:555
  13.3 12.8 %collective-permute-start.2 = (bf16[240,256]{1,0:T(8,128)(2,1)S(1)}, bf16[240,256]{1,0:T(8,128)(2,1)S(1)}, u32[]{:S(2)}, u32[]{:S(2)}) collective-permute-start(bf16[240,256]{1,0:T(8,128)(2,1)S(1)} %get-tuple-element.65), channel_id=1, source_target_pairs={{0,3},{1,2},{2,1},{3,0},{4,7},{5,6},{6,5},{7,4},{8,11},{9,10},{10,... | collective-permute-start | bytes 368648 | tf_op jit(solution)/shard_map/ppermute | solution.py:555
  13.3 15.5 %collective-permute-start.3 = (bf16[240,256]{1,0:T(8,128)(2,1)S(1)}, bf16[240,256]{1,0:T(8,128)(2,1)S(1)}, u32[]{:S(2)}, u32[]{:S(2)}) collective-permute-start(bf16[240,256]{1,0:T(8,128)(2,1)S(1)} %get-tuple-element.66), channel_id=1, source_target_pairs={{0,4},{1,5},{2,6},{3,7},{4,0},{5,1},{6,2},{7,3},{8,12},{9,13},{10,... | collective-permute-start | bytes 368648 | tf_op jit(solution)/shard_map/ppermute | solution.py:555
  15.0 13.8 %collective-permute-start.4 = (bf16[240,256]{1,0:T(8,128)(2,1)S(1)}, bf16[240,256]{1,0:T(8,128)(2,1)S(1)}, u32[]{:S(2)}, u32[]{:S(2)}) collective-permute-start(bf16[240,256]{1,0:T(8,128)(2,1)S(1)} %get-tuple-element.67), channel_id=1, source_target_pairs={{0,5},{1,4},{2,7},{3,6},{4,1},{5,0},{6,3},{7,2},{8,13},{9,12},{10,... | collective-permute-start | bytes 368648 | tf_op jit(solution)/shard_map/ppermute | solution.py:555
  15.1 13.7 %collective-permute-start.5 = (bf16[240,256]{1,0:T(8,128)(2,1)S(1)}, bf16[240,256]{1,0:T(8,128)(2,1)S(1)}, u32[]{:S(2)}, u32[]{:S(2)}) collective-permute-start(bf16[240,256]{1,0:T(8,128)(2,1)S(1)} %get-tuple-element.68), channel_id=1, source_target_pairs={{0,6},{1,7},{2,4},{3,5},{4,2},{5,3},{6,0},{7,1},{8,14},{9,15},{10,... | collective-permute-start | bytes 368648 | tf_op jit(solution)/shard_map/ppermute | solution.py:555
  21.4 7.9 %collective-permute-start.6 = (bf16[240,256]{1,0:T(8,128)(2,1)S(1)}, bf16[240,256]{1,0:T(8,128)(2,1)S(1)}, u32[]{:S(2)}, u32[]{:S(2)}) collective-permute-start(bf16[240,256]{1,0:T(8,128)(2,1)S(1)} %get-tuple-element.69), channel_id=1, source_target_pairs={{0,7},{1,6},{2,5},{3,4},{4,3},{5,2},{6,1},{7,0},{8,15},{9,14},{10,... | collective-permute-start | bytes 368648 | tf_op jit(solution)/shard_map/ppermute | solution.py:555
  26.2 10.7 %collective-permute-start.7 = (bf16[96,512]{1,0:T(8,128)(2,1)S(1)}, bf16[96,512]{1,0:T(8,128)(2,1)S(1)}, u32[]{:S(2)}, u32[]{:S(2)}) collective-permute-start(bf16[96,512]{1,0:T(8,128)(2,1)S(1)} %get-tuple-element.77.kv2), channel_id=1, source_target_pairs={{0,8},{1,9},{2,10},{3,11},{4,12},{5,13},{6,14},{7,15},{8,0},{9,1},... | collective-permute-start | bytes 294920 | tf_op jit(solution)/shard_map/ppermute | solution.py:555
  29.9 9.8 %collective-permute-start.8 = (bf16[96,512]{1,0:T(8,128)(2,1)S(1)}, bf16[96,512]{1,0:T(8,128)(2,1)S(1)}, u32[]{:S(2)}, u32[]{:S(2)}) collective-permute-start(bf16[96,512]{1,0:T(8,128)(2,1)S(1)} %get-tuple-element.81.kv2), channel_id=1, source_target_pairs={{0,8},{1,9},{2,10},{3,11},{4,12},{5,13},{6,14},{7,15},{8,0},{9,1},... | collective-permute-start | bytes 294920 | tf_op jit(solution)/shard_map/ppermute | solution.py:555
  39.5 13.9 %collective-permute-start.9 = (bf16[96,512]{1,0:T(8,128)(2,1)S(1)}, bf16[96,512]{1,0:T(8,128)(2,1)S(1)}, u32[]{:S(2)}, u32[]{:S(2)}) collective-permute-start(bf16[96,512]{1,0:T(8,128)(2,1)S(1)} %bitcast.2), channel_id=1, source_target_pairs={{0,8},{1,9},{2,10},{3,11},{4,12},{5,13},{6,14},{7,15},{8,0},{9,1},... | collective-permute-start | bytes 294920 | tf_op jit(solution)/shard_map/ppermute | solution.py:555
  42.5 16.1 %collective-permute-start.10 = (bf16[96,512]{1,0:T(8,128)(2,1)S(1)}, bf16[96,512]{1,0:T(8,128)(2,1)S(1)}, u32[]{:S(2)}, u32[]{:S(2)}) collective-permute-start(bf16[96,512]{1,0:T(8,128)(2,1)S(1)} %bitcast.3), channel_id=1, source_target_pairs={{0,8},{1,9},{2,10},{3,11},{4,12},{5,13},{6,14},{7,15},{8,0},{9,1},... | collective-permute-start | bytes 294920 | tf_op jit(solution)/shard_map/ppermute | solution.py:555
  54.9 21.8 %all-to-all-start.1 = ((bf16[8,240,256]{2,1,0:T(8,128)(2,1)}), bf16[8,240,256]{2,1,0:T(8,128)(2,1)S(1)}, u32[]{:S(2)}, u32[]{:S(2)}) async-start(bf16[8,240,256]{2,1,0:T(8,128)(2,1)} %get-tuple-element.90), calls=%async_computation.1 | async-start | bytes 1966080 | tf_op jit(solution)/shard_map/all_to_all | solution.py:558
  67.0 7.2 %collective-permute-start.11 = (bf16[144,256]{1,0:T(8,128)(2,1)S(1)}, bf16[144,256]{1,0:T(8,128)(2,1)S(1)}, u32[]{:S(2)}, u32[]{:S(2)}) collective-permute-start(bf16[144,256]{1,0:T(8,128)(2,1)S(1)} %get-tuple-element.96), channel_id=1, source_target_pairs={{0,7},{1,6},{2,5},{3,4},{4,3},{5,2},{6,1},{7,0},{8,15},{9,14},{10,... | collective-permute-start | bytes 221192 | tf_op jit(solution)/shard_map/ppermute | solution.py:555
  69.4 7.3 %collective-permute-start.12 = (bf16[144,256]{1,0:T(8,128)(2,1)S(1)}, bf16[144,256]{1,0:T(8,128)(2,1)S(1)}, u32[]{:S(2)}, u32[]{:S(2)}) collective-permute-start(bf16[144,256]{1,0:T(8,128)(2,1)S(1)} %get-tuple-element.97), channel_id=1, source_target_pairs={{0,6},{1,7},{2,4},{3,5},{4,2},{5,3},{6,0},{7,1},{8,14},{9,15},{10,... | collective-permute-start | bytes 221192 | tf_op jit(solution)/shard_map/ppermute | solution.py:555
  69.7 8.2 %collective-permute-start.13 = (bf16[144,256]{1,0:T(8,128)(2,1)S(1)}, bf16[144,256]{1,0:T(8,128)(2,1)S(1)}, u32[]{:S(2)}, u32[]{:S(2)}) collective-permute-start(bf16[144,256]{1,0:T(8,128)(2,1)S(1)} %get-tuple-element.98), channel_id=1, source_target_pairs={{0,5},{1,4},{2,7},{3,6},{4,1},{5,0},{6,3},{7,2},{8,13},{9,12},{10,... | collective-permute-start | bytes 221192 | tf_op jit(solution)/shard_map/ppermute | solution.py:555
  71.1 7.4 %collective-permute-start.14 = (bf16[144,256]{1,0:T(8,128)(2,1)S(1)}, bf16[144,256]{1,0:T(8,128)(2,1)S(1)}, u32[]{:S(2)}, u32[]{:S(2)}) collective-permute-start(bf16[144,256]{1,0:T(8,128)(2,1)S(1)} %get-tuple-element.99), channel_id=1, source_target_pairs={{0,4},{1,5},{2,6},{3,7},{4,0},{5,1},{6,2},{7,3},{8,12},{9,13},{10,... | collective-permute-start | bytes 221192 | tf_op jit(solution)/shard_map/ppermute | solution.py:555
  71.5 7.0 %collective-permute-start.15 = (bf16[144,256]{1,0:T(8,128)(2,1)S(1)}, bf16[144,256]{1,0:T(8,128)(2,1)S(1)}, u32[]{:S(2)}, u32[]{:S(2)}) collective-permute-start(bf16[144,256]{1,0:T(8,128)(2,1)S(1)} %get-tuple-element.100), channel_id=1, source_target_pairs={{0,3},{1,2},{2,1},{3,0},{4,7},{5,6},{6,5},{7,4},{8,11},{9,10},{10,... | collective-permute-start | bytes 221192 | tf_op jit(solution)/shard_map/ppermute | solution.py:555
  74.2 5.2 %collective-permute-start.16 = (bf16[144,256]{1,0:T(8,128)(2,1)S(1)}, bf16[144,256]{1,0:T(8,128)(2,1)S(1)}, u32[]{:S(2)}, u32[]{:S(2)}) collective-permute-start(bf16[144,256]{1,0:T(8,128)(2,1)S(1)} %get-tuple-element.101), channel_id=1, source_target_pairs={{0,2},{1,3},{2,0},{3,1},{4,6},{5,7},{6,4},{7,5},{8,10},{9,11},{10,... | collective-permute-start | bytes 221192 | tf_op jit(solution)/shard_map/ppermute | solution.py:555
  76.7 2.7 %collective-permute-start.17 = (bf16[144,256]{1,0:T(8,128)(2,1)S(1)}, bf16[144,256]{1,0:T(8,128)(2,1)S(1)}, u32[]{:S(2)}, u32[]{:S(2)}) collective-permute-start(bf16[144,256]{1,0:T(8,128)(2,1)S(1)} %get-tuple-element.102), channel_id=1, source_target_pairs={{0,1},{1,0},{2,3},{3,2},{4,5},{5,4},{6,7},{7,6},{8,9},{9,8},{10,11... | collective-permute-start | bytes 221192 | tf_op jit(solution)/shard_map/ppermute | solution.py:555

commit v6 on v5

--- a/solution.py
+++ b/solution.py
@@ -361,7 +361,7 @@
         raw[:, rows] = xt.astype(BF16)
         q, k, v = (xt[i * hd : (i + 1) * hd] for i in range(3))
         one_hot = segment_slides(plan, seg, table)
-        ka[rows, :] = key_features(plan, k, one_hot).T.astype(BF16)
+        ka[rows, :] = key_features(plan, k, one_hot).astype(BF16).T
         qat[:, rows] = query_features(plan, q, one_hot).astype(BF16)
         vat[:, rows] = value_features(plan, v).astype(BF16)
     for tile in range(plan.segs, len(plan.tiles)):
@@ -408,7 +408,7 @@
     key_f = key_features(plan, x[0:hd], one_hot)
     query_f = query_features(plan, q2[...].astype(F32), one_hot[:, 0 : plan.last])
     vat2 = value_features(plan, x[hd : 2 * hd]).astype(BF16)
-    res = forward_tile(plan, dot(key_f.T.astype(BF16), query_f.astype(BF16)), vat2)
+    res = forward_tile(plan, dot(key_f.astype(BF16).T, query_f.astype(BF16)), vat2)
     last_update(plan, starts, acc, slice(None), res, partial(merged, plan), no_level(plan))
     for seg in range(plan.segs):
         rows = slice(seg * SEG0, (seg + 1) * SEG0)
@@ -441,7 +441,7 @@
     grad_f = jnp.concatenate(
         [g, three_rows(-ld[1:2]), jnp.zeros((120 - hd, g.shape[1]), F32)], axis=0
     )
-    return query_f.T.astype(BF16), grad_f.T.astype(BF16)
+    return query_f.astype(BF16).T, grad_f.astype(BF16).T
 
 
 def backward_body(plan, chunk, places, blocks, ends, table, tok_in, ld_ref, *refs):

time: 80.8 us -> 80.5 us (level)
  no operation moved by 1% of the time
where the time goes in v6:
time: 80.5 us; the launch traced here: 80.2 us
  Pallas kernels  38.9 us (48%)
  starting transfers between devices  31 us (39%)
  waiting for transfers between devices  9.45 us (12%)
  between operations  0.88 us (1%)
    ppermute x18, starting transfers between devices, permuted(): return lax.ppermute(x, 'seq', [(i, target(i)) for i in range(device_count)])  21.8 us
    pallas_call x2, Pallas kernels, body(): kernel_call(partial(backward_body, plan, chunk, [x[1] for x in sources],...  15.7 us
    ppermute x18, waiting for transfers between devices, permuted(): return lax.ppermute(x, 'seq', [(i, target(i)) for i in range(device_count)])  9.44 us
    all_to_all x2, starting transfers between devices, swap(): return lax.all_to_all(x, 'seq', 0, 0, tiled=True, axis_index_groups=groups)  9.15 us
    pallas_call x2, Pallas kernels, body(): kernel_call(partial(last_body, plan, chunk, first, len(received[source]))...  5.45 us
    pallas_call x2, Pallas kernels, body(): kernel_call(partial(pack_body, plan, [c for c, _ in pieces], near + 1 if...  4.93 us
    pallas_call x1, Pallas kernels, body(): kernel_call(partial(make, len(near_x), 'both'), last_rows + [sums, TOKEN]...  4.39 us
    pallas_call x1, Pallas kernels, body(): kernel_call(partial(make, 0, 'sums'), [sums, TOKEN], [VMEM, ANY] + [VMEM]...  4.05 us
  transfers between devices with their start and end apart: 20, of which 7 were waited for; matrix products, arithmetic and copies ran while one was open for 0% of the time, Pallas kernels for 44%

profile of v6, /device:TPU:0, one launch (start us, length us, event | category | flops | bytes accessed | tf_op | source)
XLA Modules:
  0.0 80.2 jit_solution(5728341844877303724)
XLA Ops:
  0.7 2.7 %pack.2 = (bf16[8,144,256]{2,1,0:T(8,128)(2,1)}, f32[8,128]{1,0:T(8,128)}) custom-call(bf16[256,768]{1,0:T(8,128)(2,1)} %refs_0_.3, bf16[256,768]{1,0:T(8,128)(2,1)} %refs_1_.3, bf16[256,768]{1,0:T(8,128)(2,1)} %refs_2_.3), custom_call_target="tpu_custom_call" | custom-call | bytes 1048576 | tf_op jit(solution)/shard_map/pack/pallas_call | solution.py:576
  3.4 0.0 copy-start.2
  3.4 0.0 copy-start.3
  3.4 0.0 copy-start.4
  3.4 5.4 %all-to-all-start = ((bf16[8,144,256]{2,1,0:T(8,128)(2,1)}), bf16[8,144,256]{2,1,0:T(8,128)(2,1)S(1)}, u32[]{:S(2)}, u32[]{:S(2)}) async-start(bf16[8,144,256]{2,1,0:T(8,128)(2,1)} %get-tuple-element.60), calls=%async_computation | async-start | bytes 1179648 | tf_op jit(solution)/shard_map/all_to_all | solution.py:558
  8.8 2.3 %pack.3 = (bf16[240,256]{1,0:T(8,128)(2,1)S(1)}, bf16[240,256]{1,0:T(8,128)(2,1)S(1)}, bf16[240,256]{1,0:T(8,128)(2,1)S(1)}, bf16[240,256]{1,0:T(8,128)(2,1)S(1)...) custom-call(bf16[256,768]{1,0:T(8,128)(2,1)S(1)} %copy-done.1, ...), custom_call_target="tpu_custom_call" | custom-call | bytes 1048576 | tf_op jit(solution)/shard_map/pack/pallas_call | solution.py:576
  11.1 0.6 collective-permute-start
  11.7 1.7 %collective-permute-start.1 = (bf16[240,256]{1,0:T(8,128)(2,1)S(1)}, bf16[240,256]{1,0:T(8,128)(2,1)S(1)}, u32[]{:S(2)}, u32[]{:S(2)}) collective-permute-start(bf16[240,256]{1,0:T(8,128)(2,1)S(1)} %get-tuple-element.64), channel_id=1, source_target_pairs={{0,2},{1,3},{2,0},{3,1},{4,6},{5,7},{6,4},{7,5},{8,10},{9,11},{10,... | collective-permute-start | bytes 368648 | tf_op jit(solution)/shard_map/ppermute | solution.py:555
  13.3 0.0 collective-permute-start.2
  13.3 1.7 %collective-permute-start.3 = (bf16[240,256]{1,0:T(8,128)(2,1)S(1)}, bf16[240,256]{1,0:T(8,128)(2,1)S(1)}, u32[]{:S(2)}, u32[]{:S(2)}) collective-permute-start(bf16[240,256]{1,0:T(8,128)(2,1)S(1)} %get-tuple-element.66), channel_id=1, source_target_pairs={{0,4},{1,5},{2,6},{3,7},{4,0},{5,1},{6,2},{7,3},{8,12},{9,13},{10,... | collective-permute-start | bytes 368648 | tf_op jit(solution)/shard_map/ppermute | solution.py:555
  15.0 0.1 collective-permute-start.4
  15.1 0.0 collective-permute-done.refs_1_.rest_1_.refs_2_.refs_9_
  15.1 2.6 %collective-permute-start.5 = (bf16[240,256]{1,0:T(8,128)(2,1)S(1)}, bf16[240,256]{1,0:T(8,128)(2,1)S(1)}, u32[]{:S(2)}, u32[]{:S(2)}) collective-permute-start(bf16[240,256]{1,0:T(8,128)(2,1)S(1)} %get-tuple-element.68), channel_id=1, source_target_pairs={{0,6},{1,7},{2,4},{3,5},{4,2},{5,3},{6,0},{7,1},{8,14},{9,15},{10,... | collective-permute-start | bytes 368648 | tf_op jit(solution)/shard_map/ppermute | solution.py:555
  17.7 3.7 %collective-permute-done.1.refs_2_.rest_2_.refs_3_.refs_10_ = bf16[240,256]{1,0:T(8,128)(2,1)S(1)} collective-permute-done((bf16[240,256]{1,0:T(8,128)(2,1)S(1)}, bf16[240,256]{1,0:T(8,128)(2,1)S(1)}, u32[]{:S(2)}, u32[]{:S(2)}) %collective-permute-start.1) | collective-permute-done | bytes 122912 | tf_op jit(solution)/shard_map/ppermute | solution.py:555
  21.4 0.4 collective-permute-start.6
  21.8 0.0 all-to-all-done.refs_0_
  21.8 4.4 %forward0.1 = (bf16[48,512]{1,0:T(8,128)(2,1)S(1)}, bf16[96,512]{1,0:T(8,128)(2,1)S(1)}, f32[64,2048]{1,0:T(8,128)S(1)}, f32[8,128]{1,0:T(8,128)S(1)}) custom-call(f32[16,128]{1,0:T(8,128)S(1)} %get-tuple-element.58.table, f32[8,128]{1,0:T(8,128)S(1)} %get-tuple-element.59.tok_in, bf16[8,144,256]{2,1,0:T(8,128)(2,1)S(1)} %all-to-all-done.refs_0_), custom_call_target="tpu_custom_call" | custom-call | bytes 1048576 | tf_op jit(solution)/shard_map/forward0/pallas_call | solution.py:613
  26.3 2.6 %collective-permute-start.7 = (bf16[96,512]{1,0:T(8,128)(2,1)S(1)}, bf16[96,512]{1,0:T(8,128)(2,1)S(1)}, u32[]{:S(2)}, u32[]{:S(2)}) collective-permute-start(bf16[96,512]{1,0:T(8,128)(2,1)S(1)} %get-tuple-element.77.kv2), channel_id=1, source_target_pairs={{0,8},{1,9},{2,10},{3,11},{4,12},{5,13},{6,14},{7,15},{8,0},{9,1},... | collective-permute-start | bytes 294920 | tf_op jit(solution)/shard_map/ppermute | solution.py:555
  28.9 0.0 collective-permute-done.3.refs_4_.rest_4_.refs_5_.refs_12_
  28.9 0.0 collective-permute-done.4.refs_5_.rest_5_.refs_6_.refs_13_
  28.9 0.4 collective-permute-done.6.refs_7_.rest_7_.refs_8_.refs_15_
  29.3 0.6 rows1.1
  29.9 2.7 %collective-permute-start.8 = (bf16[96,512]{1,0:T(8,128)(2,1)S(1)}, bf16[96,512]{1,0:T(8,128)(2,1)S(1)}, u32[]{:S(2)}, u32[]{:S(2)}) collective-permute-start(bf16[96,512]{1,0:T(8,128)(2,1)S(1)} %get-tuple-element.81.kv2), channel_id=1, source_target_pairs={{0,8},{1,9},{2,10},{3,11},{4,12},{5,13},{6,14},{7,15},{8,0},{9,1},... | collective-permute-start | bytes 294920 | tf_op jit(solution)/shard_map/ppermute | solution.py:555
  32.5 4.1 %sums1.1 = (f32[64,2048]{1,0:T(8,128)S(1)}, f32[8,128]{1,0:T(8,128)S(1)}) custom-call(f32[16,128]{1,0:T(8,128)S(1)} %get-tuple-element.58.table, f32[8,128]{1,0:T(8,128)S(1)} %get-tuple-element.70.tok_in, bf16[3072,128]{1,0:T(8,128)(2,1)S(1)} %get-tuple-element.71.refs_0_, bf16[128,3072]{1,0:T(8,128)(2,1)S(1)} %get-tuple-element.72.refs_1_, ...), custom_call_target="tpu_custom_call" | custom-call | bytes 1048576 | tf_op jit(solution)/shard_map/sums1/pallas_call | solution.py:630
  36.6 0.4 collective-permute-done.7.rest_8_
  37.0 2.6 %last0.1 = (bf16[48,2048]{1,0:T(8,128)(2,1)S(1)}, f32[8,2048]{1,0:T(8,128)S(1)}, f32[144,512]{1,0:T(8,128)S(1)}, bf16[1,96,512]{2,1,0:T(8,128)(2,1)S(1)}, f32[8,128]{1,0:T(8,128)S(1)}) custom-call(f32[16,128]{1,0:T(8,128)S(1)} %get-tuple-element.58.table, f32[8,128]{1,0:T(8,128)S(1)} %get-tuple-element.74.tok_in, f32[64,2048]{1,0:T(8,128)S(1)} %get-tuple-element.75.acc_ref, ...), custom_call_target="tpu_custom_call" | custom-call | flops 21474836480 | bytes 1048576 | tf_op jit(solution)/shard_map/last0/pallas_call | solution.py:641
  39.6 0.1 collective-permute-start.9
  39.7 0.0 collective-permute-done.8.rest_8_
  39.7 2.8 %last1.1 = (bf16[48,2048]{1,0:T(8,128)(2,1)S(1)}, f32[8,2048]{1,0:T(8,128)S(1)}, f32[144,512]{1,0:T(8,128)S(1)}, bf16[1,96,512]{2,1,0:T(8,128)(2,1)S(1)}, f32[8,128]{1,0:T(8,128)S(1)}) custom-call(f32[16,128]{1,0:T(8,128)S(1)} %get-tuple-element.58.table, f32[8,128]{1,0:T(8,128)S(1)} %get-tuple-element.78.tok_in, f32[64,2048]{1,0:T(8,128)S(1)} %get-tuple-element.79.acc_ref, ...), custom_call_target="tpu_custom_call" | custom-call | flops 21474836480 | bytes 1048576 | tf_op jit(solution)/shard_map/last1/pallas_call | solution.py:641
  42.5 3.0 %collective-permute-start.10 = (bf16[96,512]{1,0:T(8,128)(2,1)S(1)}, bf16[96,512]{1,0:T(8,128)(2,1)S(1)}, u32[]{:S(2)}, u32[]{:S(2)}) collective-permute-start(bf16[96,512]{1,0:T(8,128)(2,1)S(1)} %bitcast.3), channel_id=1, source_target_pairs={{0,8},{1,9},{2,10},{3,11},{4,12},{5,13},{6,14},{7,15},{8,0},{9,1},... | collective-permute-start | bytes 294920 | tf_op jit(solution)/shard_map/ppermute | solution.py:555
  45.5 7.7 %backward0.1 = (f32[144,2048]{1,0:T(8,128)S(1)}, f32[8,128]{1,0:T(8,128)S(1)}) custom-call(f32[16,128]{1,0:T(8,128)S(1)} %get-tuple-element.58.table, f32[8,128]{1,0:T(8,128)S(1)} %get-tuple-element.82.tok_in, f32[8,2048]{1,0:T(8,128)S(1)} %get-tuple-element.83.ld_ref, bf16[8,144,256]{2,1,0:T(8,128)(2,1)S(1)} %all-to-all-done.refs_0_, ...), custom_call_target="tpu_custom_call" | custom-call | flops 80530636800 | bytes 1048576 | tf_op jit(solution)/shard_map/backward0/pallas_call | solution.py:665
  53.2 1.4 %finish0.1 = (bf16[8,240,256]{2,1,0:T(8,128)(2,1)}, f32[8,128]{1,0:T(8,128)S(1)}) custom-call(f32[16,128]{1,0:T(8,128)S(1)} %get-tuple-element.58.table, f32[8,128]{1,0:T(8,128)S(1)} %get-tuple-element.84.tok_in, f32[144,2048]{1,0:T(8,128)S(1)} %get-tuple-element.85.near_ref, bf16[48,2048]{1,0:T(8,128)(2,1)S(1)} %get-tuple-element.86.refs_0_, ...), custom_call_target="tpu_custom_call" | custom-call | bytes 1048576 | tf_op jit(solution)/shard_map/finish0/pallas_call | solution.py:682
  54.6 3.8 %all-to-all-start.1 = ((bf16[8,240,256]{2,1,0:T(8,128)(2,1)}), bf16[8,240,256]{2,1,0:T(8,128)(2,1)S(1)}, u32[]{:S(2)}, u32[]{:S(2)}) async-start(bf16[8,240,256]{2,1,0:T(8,128)(2,1)} %get-tuple-element.90), calls=%async_computation.1 | async-start | bytes 1966080 | tf_op jit(solution)/shard_map/all_to_all | solution.py:558
  58.4 8.0 %backward1.1 = (bf16[144,256]{1,0:T(8,128)(2,1)S(1)}, bf16[144,256]{1,0:T(8,128)(2,1)S(1)}, bf16[144,256]{1,0:T(8,128)(2,1)S(1)}, bf16[144,256]{1,0:T(8,128)(2,1...) custom-call(f32[16,128]{1,0:T(8,128)S(1)} %get-tuple-element.58.tabl, ...), custom_call_target="tpu_custom_call" | custom-call | flops 80530636800 | bytes 1048576 | tf_op jit(solution)/shard_map/backward1/pallas_call | solution.py:665
  66.4 2.4 %collective-permute-start.11 = (bf16[144,256]{1,0:T(8,128)(2,1)S(1)}, bf16[144,256]{1,0:T(8,128)(2,1)S(1)}, u32[]{:S(2)}, u32[]{:S(2)}) collective-permute-start(bf16[144,256]{1,0:T(8,128)(2,1)S(1)} %get-tuple-element.96), channel_id=1, source_target_pairs={{0,7},{1,6},{2,5},{3,4},{4,3},{5,2},{6,1},{7,0},{8,15},{9,14},{10,... | collective-permute-start | bytes 221192 | tf_op jit(solution)/shard_map/ppermute | solution.py:555
  68.8 0.3 collective-permute-start.12
  69.1 1.4 %collective-permute-start.13 = (bf16[144,256]{1,0:T(8,128)(2,1)S(1)}, bf16[144,256]{1,0:T(8,128)(2,1)S(1)}, u32[]{:S(2)}, u32[]{:S(2)}) collective-permute-start(bf16[144,256]{1,0:T(8,128)(2,1)S(1)} %get-tuple-element.98), channel_id=1, source_target_pairs={{0,5},{1,4},{2,7},{3,6},{4,1},{5,0},{6,3},{7,2},{8,13},{9,12},{10,... | collective-permute-start | bytes 221192 | tf_op jit(solution)/shard_map/ppermute | solution.py:555
  70.5 0.4 collective-permute-start.14
  70.9 1.4 %collective-permute-start.15 = (bf16[144,256]{1,0:T(8,128)(2,1)S(1)}, bf16[144,256]{1,0:T(8,128)(2,1)S(1)}, u32[]{:S(2)}, u32[]{:S(2)}) collective-permute-start(bf16[144,256]{1,0:T(8,128)(2,1)S(1)} %get-tuple-element.100), channel_id=1, source_target_pairs={{0,3},{1,2},{2,1},{3,0},{4,7},{5,6},{6,5},{7,4},{8,11},{9,10},{10,... | collective-permute-start | bytes 221192 | tf_op jit(solution)/shard_map/ppermute | solution.py:555
  72.3 1.6 %collective-permute-done.11.refs_0_ = bf16[144,256]{1,0:T(8,128)(2,1)S(1)} collective-permute-done((bf16[144,256]{1,0:T(8,128)(2,1)S(1)}, bf16[144,256]{1,0:T(8,128)(2,1)S(1)}, u32[]{:S(2)}, u32[]{:S(2)}) %collective-permute-start.11) | collective-permute-done | bytes 73760 | tf_op jit(solution)/shard_map/ppermute | solution.py:555
  73.9 0.6 collective-permute-start.16
  74.4 2.0 %collective-permute-done.12.refs_1_ = bf16[144,256]{1,0:T(8,128)(2,1)S(1)} collective-permute-done((bf16[144,256]{1,0:T(8,128)(2,1)S(1)}, bf16[144,256]{1,0:T(8,128)(2,1)S(1)}, u32[]{:S(2)}, u32[]{:S(2)}) %collective-permute-start.12) | collective-permute-done | bytes 73760 | tf_op jit(solution)/shard_map/ppermute | solution.py:555
  76.4 1.3 %unpack.2 = (bf16[256,768]{1,0:T(8,128)(2,1)}, bf16[256,768]{1,0:T(8,128)(2,1)}, bf16[256,768]{1,0:T(8,128)(2,1)}, bf16[256,768]{1,0:T(8,128)(2,1)}) custom-call(bf16[8,240,256]{2,1,0:T(8,128)(2,1)S(1)} %all-to-all-done.1.refs_0_), custom_call_target="tpu_custom_call" | custom-call | bytes 1048576 | tf_op jit(solution)/shard_map/unpack/pallas_call | solution.py:694
  77.7 0.0 collective-permute-done.13.refs_2_
  77.7 0.5 collective-permute-done.14.refs_3_
  78.2 0.0 collective-permute-done.15.refs_4_
  78.2 0.9 %collective-permute-done.16.refs_5_ = bf16[144,256]{1,0:T(8,128)(2,1)S(1)} collective-permute-done((bf16[144,256]{1,0:T(8,128)(2,1)S(1)}, bf16[144,256]{1,0:T(8,128)(2,1)S(1)}, u32[]{:S(2)}, u32[]{:S(2)}) %collective-permute-start.16) | collective-permute-done | bytes 73760 | tf_op jit(solution)/shard_map/ppermute | solution.py:555
  79.1 1.1 %unpack.3 = (bf16[256,768]{1,0:T(8,128)(2,1)}, bf16[256,768]{1,0:T(8,128)(2,1)}, bf16[256,768]{1,0:T(8,128)(2,1)}) custom-call(bf16[144,256]{1,0:T(8,128)(2,1)S(1)} %collective-permute-done.11.refs_0_, bf16[144,256]{1,0:T(8,128)(2,1)S(1)} %collective-permute-done.12.refs_1_, ...), custom_call_target="tpu_custom_call", output_to_operand_aliasing={{0}: (8, {}), {1}: (9, {}), {2}: (10, {})} | custom-call | bytes 1048576 | tf_op jit(solution)/shard_map/unpack/pallas_call | solution.py:704
  (18 shorter events, 0.0 us)
Async XLA Ops:
  0.6 8.1 %copy-start.1 = (bf16[256,768]{1,0:T(8,128)(2,1)S(1)}, bf16[256,768]{1,0:T(8,128)(2,1)}, u32[]{:S(2)}) copy-start(bf16[256,768]{1,0:T(8,128)(2,1)} %refs_0_.3) | copy-start | bytes 1179652
  0.6 8.1 %copy-start.6 = (s32[8]{0:T(128)S(1)}, s32[8]{0:T(128)}, u32[]{:S(2)}) copy-start(s32[8]{0:T(128)} %refs_5_.1) | copy-start | bytes 100
  0.7 8.1 %copy-start.5 = (s32[3,16]{1,0:T(4,128)S(1)}, s32[3,16]{1,0:T(4,128)}, u32[]{:S(2)}) copy-start(s32[3,16]{1,0:T(4,128)} %refs_6_.1) | copy-start | bytes 580
  0.7 8.1 %copy-start = (bf16[256,768]{1,0:T(8,128)(2,1)S(1)}, bf16[256,768]{1,0:T(8,128)(2,1)}, u32[]{:S(2)}) copy-start(bf16[256,768]{1,0:T(8,128)(2,1)} %refs_4_.1) | copy-start | bytes 1179652
  3.4 5.4 %copy-start.2 = (bf16[256,768]{1,0:T(8,128)(2,1)S(1)}, bf16[256,768]{1,0:T(8,128)(2,1)}, u32[]{:S(2)}) copy-start(bf16[256,768]{1,0:T(8,128)(2,1)} %refs_1_.3) | copy-start | bytes 1179652
  3.4 5.4 %copy-start.3 = (bf16[256,768]{1,0:T(8,128)(2,1)S(1)}, bf16[256,768]{1,0:T(8,128)(2,1)}, u32[]{:S(2)}) copy-start(bf16[256,768]{1,0:T(8,128)(2,1)} %refs_2_.3) | copy-start | bytes 1179652
  3.4 5.4 %copy-start.4 = (f32[8,128]{1,0:T(8,128)S(1)}, f32[8,128]{1,0:T(8,128)}, u32[]{:S(2)}) copy-start(f32[8,128]{1,0:T(8,128)} %get-tuple-element.57.refs_7_) | copy-start | bytes 12292
  3.4 18.5 %all-to-all-start = ((bf16[8,144,256]{2,1,0:T(8,128)(2,1)}), bf16[8,144,256]{2,1,0:T(8,128)(2,1)S(1)}, u32[]{:S(2)}, u32[]{:S(2)}) async-start(bf16[8,144,256]{2,1,0:T(8,128)(2,1)} %get-tuple-element.60), calls=%async_computation | async-start | bytes 1179648 | tf_op jit(solution)/shard_map/all_to_all | solution.py:558
  11.1 4.1 %collective-permute-start = (bf16[240,256]{1,0:T(8,128)(2,1)S(1)}, bf16[240,256]{1,0:T(8,128)(2,1)S(1)}, u32[]{:S(2)}, u32[]{:S(2)}) collective-permute-start(bf16[240,256]{1,0:T(8,128)(2,1)S(1)} %get-tuple-element.63), channel_id=1, source_target_pairs={{0,1},{1,0},{2,3},{3,2},{4,5},{5,4},{6,7},{7,6},{8,9},{9,8},{10,11... | collective-permute-start | bytes 368648 | tf_op jit(solution)/shard_map/ppermute | solution.py:555
  11.7 9.8 %collective-permute-start.1 = (bf16[240,256]{1,0:T(8,128)(2,1)S(1)}, bf16[240,256]{1,0:T(8,128)(2,1)S(1)}, u32[]{:S(2)}, u32[]{:S(2)}) collective-permute-start(bf16[240,256]{1,0:T(8,128)(2,1)S(1)} %get-tuple-element.64), channel_id=1, source_target_pairs={{0,2},{1,3},{2,0},{3,1},{4,6},{5,7},{6,4},{7,5},{8,10},{9,11},{10,... | collective-permute-start | bytes 368648 | tf_op jit(solution)/shard_map/ppermute | solution.py:555
  13.3 12.9 %collective-permute-start.2 = (bf16[240,256]{1,0:T(8,128)(2,1)S(1)}, bf16[240,256]{1,0:T(8,128)(2,1)S(1)}, u32[]{:S(2)}, u32[]{:S(2)}) collective-permute-start(bf16[240,256]{1,0:T(8,128)(2,1)S(1)} %get-tuple-element.65), channel_id=1, source_target_pairs={{0,3},{1,2},{2,1},{3,0},{4,7},{5,6},{6,5},{7,4},{8,11},{9,10},{10,... | collective-permute-start | bytes 368648 | tf_op jit(solution)/shard_map/ppermute | solution.py:555
  13.3 15.6 %collective-permute-start.3 = (bf16[240,256]{1,0:T(8,128)(2,1)S(1)}, bf16[240,256]{1,0:T(8,128)(2,1)S(1)}, u32[]{:S(2)}, u32[]{:S(2)}) collective-permute-start(bf16[240,256]{1,0:T(8,128)(2,1)S(1)} %get-tuple-element.66), channel_id=1, source_target_pairs={{0,4},{1,5},{2,6},{3,7},{4,0},{5,1},{6,2},{7,3},{8,12},{9,13},{10,... | collective-permute-start | bytes 368648 | tf_op jit(solution)/shard_map/ppermute | solution.py:555
  15.0 13.9 %collective-permute-start.4 = (bf16[240,256]{1,0:T(8,128)(2,1)S(1)}, bf16[240,256]{1,0:T(8,128)(2,1)S(1)}, u32[]{:S(2)}, u32[]{:S(2)}) collective-permute-start(bf16[240,256]{1,0:T(8,128)(2,1)S(1)} %get-tuple-element.67), channel_id=1, source_target_pairs={{0,5},{1,4},{2,7},{3,6},{4,1},{5,0},{6,3},{7,2},{8,13},{9,12},{10,... | collective-permute-start | bytes 368648 | tf_op jit(solution)/shard_map/ppermute | solution.py:555
  15.1 13.8 %collective-permute-start.5 = (bf16[240,256]{1,0:T(8,128)(2,1)S(1)}, bf16[240,256]{1,0:T(8,128)(2,1)S(1)}, u32[]{:S(2)}, u32[]{:S(2)}) collective-permute-start(bf16[240,256]{1,0:T(8,128)(2,1)S(1)} %get-tuple-element.68), channel_id=1, source_target_pairs={{0,6},{1,7},{2,4},{3,5},{4,2},{5,3},{6,0},{7,1},{8,14},{9,15},{10,... | collective-permute-start | bytes 368648 | tf_op jit(solution)/shard_map/ppermute | solution.py:555
  21.4 7.9 %collective-permute-start.6 = (bf16[240,256]{1,0:T(8,128)(2,1)S(1)}, bf16[240,256]{1,0:T(8,128)(2,1)S(1)}, u32[]{:S(2)}, u32[]{:S(2)}) collective-permute-start(bf16[240,256]{1,0:T(8,128)(2,1)S(1)} %get-tuple-element.69), channel_id=1, source_target_pairs={{0,7},{1,6},{2,5},{3,4},{4,3},{5,2},{6,1},{7,0},{8,15},{9,14},{10,... | collective-permute-start | bytes 368648 | tf_op jit(solution)/shard_map/ppermute | solution.py:555
  26.3 10.7 %collective-permute-start.7 = (bf16[96,512]{1,0:T(8,128)(2,1)S(1)}, bf16[96,512]{1,0:T(8,128)(2,1)S(1)}, u32[]{:S(2)}, u32[]{:S(2)}) collective-permute-start(bf16[96,512]{1,0:T(8,128)(2,1)S(1)} %get-tuple-element.77.kv2), channel_id=1, source_target_pairs={{0,8},{1,9},{2,10},{3,11},{4,12},{5,13},{6,14},{7,15},{8,0},{9,1},... | collective-permute-start | bytes 294920 | tf_op jit(solution)/shard_map/ppermute | solution.py:555
  29.9 9.8 %collective-permute-start.8 = (bf16[96,512]{1,0:T(8,128)(2,1)S(1)}, bf16[96,512]{1,0:T(8,128)(2,1)S(1)}, u32[]{:S(2)}, u32[]{:S(2)}) collective-permute-start(bf16[96,512]{1,0:T(8,128)(2,1)S(1)} %get-tuple-element.81.kv2), channel_id=1, source_target_pairs={{0,8},{1,9},{2,10},{3,11},{4,12},{5,13},{6,14},{7,15},{8,0},{9,1},... | collective-permute-start | bytes 294920 | tf_op jit(solution)/shard_map/ppermute | solution.py:555
  39.6 13.6 %collective-permute-start.9 = (bf16[96,512]{1,0:T(8,128)(2,1)S(1)}, bf16[96,512]{1,0:T(8,128)(2,1)S(1)}, u32[]{:S(2)}, u32[]{:S(2)}) collective-permute-start(bf16[96,512]{1,0:T(8,128)(2,1)S(1)} %bitcast.2), channel_id=1, source_target_pairs={{0,8},{1,9},{2,10},{3,11},{4,12},{5,13},{6,14},{7,15},{8,0},{9,1},... | collective-permute-start | bytes 294920 | tf_op jit(solution)/shard_map/ppermute | solution.py:555
  42.5 15.9 %collective-permute-start.10 = (bf16[96,512]{1,0:T(8,128)(2,1)S(1)}, bf16[96,512]{1,0:T(8,128)(2,1)S(1)}, u32[]{:S(2)}, u32[]{:S(2)}) collective-permute-start(bf16[96,512]{1,0:T(8,128)(2,1)S(1)} %bitcast.3), channel_id=1, source_target_pairs={{0,8},{1,9},{2,10},{3,11},{4,12},{5,13},{6,14},{7,15},{8,0},{9,1},... | collective-permute-start | bytes 294920 | tf_op jit(solution)/shard_map/ppermute | solution.py:555
  54.6 21.8 %all-to-all-start.1 = ((bf16[8,240,256]{2,1,0:T(8,128)(2,1)}), bf16[8,240,256]{2,1,0:T(8,128)(2,1)S(1)}, u32[]{:S(2)}, u32[]{:S(2)}) async-start(bf16[8,240,256]{2,1,0:T(8,128)(2,1)} %get-tuple-element.90), calls=%async_computation.1 | async-start | bytes 1966080 | tf_op jit(solution)/shard_map/all_to_all | solution.py:558
  66.4 7.5 %collective-permute-start.11 = (bf16[144,256]{1,0:T(8,128)(2,1)S(1)}, bf16[144,256]{1,0:T(8,128)(2,1)S(1)}, u32[]{:S(2)}, u32[]{:S(2)}) collective-permute-start(bf16[144,256]{1,0:T(8,128)(2,1)S(1)} %get-tuple-element.96), channel_id=1, source_target_pairs={{0,7},{1,6},{2,5},{3,4},{4,3},{5,2},{6,1},{7,0},{8,15},{9,14},{10,... | collective-permute-start | bytes 221192 | tf_op jit(solution)/shard_map/ppermute | solution.py:555
  68.8 7.6 %collective-permute-start.12 = (bf16[144,256]{1,0:T(8,128)(2,1)S(1)}, bf16[144,256]{1,0:T(8,128)(2,1)S(1)}, u32[]{:S(2)}, u32[]{:S(2)}) collective-permute-start(bf16[144,256]{1,0:T(8,128)(2,1)S(1)} %get-tuple-element.97), channel_id=1, source_target_pairs={{0,6},{1,7},{2,4},{3,5},{4,2},{5,3},{6,0},{7,1},{8,14},{9,15},{10,... | collective-permute-start | bytes 221192 | tf_op jit(solution)/shard_map/ppermute | solution.py:555
  69.1 8.5 %collective-permute-start.13 = (bf16[144,256]{1,0:T(8,128)(2,1)S(1)}, bf16[144,256]{1,0:T(8,128)(2,1)S(1)}, u32[]{:S(2)}, u32[]{:S(2)}) collective-permute-start(bf16[144,256]{1,0:T(8,128)(2,1)S(1)} %get-tuple-element.98), channel_id=1, source_target_pairs={{0,5},{1,4},{2,7},{3,6},{4,1},{5,0},{6,3},{7,2},{8,13},{9,12},{10,... | collective-permute-start | bytes 221192 | tf_op jit(solution)/shard_map/ppermute | solution.py:555
  70.5 7.7 %collective-permute-start.14 = (bf16[144,256]{1,0:T(8,128)(2,1)S(1)}, bf16[144,256]{1,0:T(8,128)(2,1)S(1)}, u32[]{:S(2)}, u32[]{:S(2)}) collective-permute-start(bf16[144,256]{1,0:T(8,128)(2,1)S(1)} %get-tuple-element.99), channel_id=1, source_target_pairs={{0,4},{1,5},{2,6},{3,7},{4,0},{5,1},{6,2},{7,3},{8,12},{9,13},{10,... | collective-permute-start | bytes 221192 | tf_op jit(solution)/shard_map/ppermute | solution.py:555
  70.9 7.3 %collective-permute-start.15 = (bf16[144,256]{1,0:T(8,128)(2,1)S(1)}, bf16[144,256]{1,0:T(8,128)(2,1)S(1)}, u32[]{:S(2)}, u32[]{:S(2)}) collective-permute-start(bf16[144,256]{1,0:T(8,128)(2,1)S(1)} %get-tuple-element.100), channel_id=1, source_target_pairs={{0,3},{1,2},{2,1},{3,0},{4,7},{5,6},{6,5},{7,4},{8,11},{9,10},{10,... | collective-permute-start | bytes 221192 | tf_op jit(solution)/shard_map/ppermute | solution.py:555
  73.9 5.2 %collective-permute-start.16 = (bf16[144,256]{1,0:T(8,128)(2,1)S(1)}, bf16[144,256]{1,0:T(8,128)(2,1)S(1)}, u32[]{:S(2)}, u32[]{:S(2)}) collective-permute-start(bf16[144,256]{1,0:T(8,128)(2,1)S(1)} %get-tuple-element.101), channel_id=1, source_target_pairs={{0,2},{1,3},{2,0},{3,1},{4,6},{5,7},{6,4},{7,5},{8,10},{9,11},{10,... | collective-permute-start | bytes 221192 | tf_op jit(solution)/shard_map/ppermute | solution.py:555
  76.4 2.7 %collective-permute-start.17 = (bf16[144,256]{1,0:T(8,128)(2,1)S(1)}, bf16[144,256]{1,0:T(8,128)(2,1)S(1)}, u32[]{:S(2)}, u32[]{:S(2)}) collective-permute-start(bf16[144,256]{1,0:T(8,128)(2,1)S(1)} %get-tuple-element.102), channel_id=1, source_target_pairs={{0,1},{1,0},{2,3},{3,2},{4,5},{5,4},{6,7},{7,6},{8,9},{9,8},{10,11... | collective-permute-start | bytes 221192 | tf_op jit(solution)/shard_map/ppermute | solution.py:555
